TPU v7x, 512 devices: a whole 4x8x8 slice. The times are simulated.
512 devices in a mesh: dp: 64 (over y, z_lo, x), head: 8 (over z_hi, core).
Axes of the slice: x: 4, y: 8, z: 8 (z_hi: 4, z_lo: 2; z = z_hi * 2 + z_lo), core: 2. Of those that a mesh axis runs over, the one named last changes fastest.
Arguments:
- queries: bfloat16 [8192, 16384], P('dp', 'head'), may hold values from -100 to 100
- tree_keys: bfloat16 [8192, 1024], P('dp', 'head'), may hold values from -4 to 4
- tree_values: bfloat16 [8192, 1024], P('dp', 'head'), may hold values from -4 to 4
- cache_keys: bfloat16 [512, 128, 1024], P('dp', None, 'head'), may hold values from -4 to 4
- cache_values: bfloat16 [512, 128, 1024], P('dp', None, 'head'), may hold values from -4 to 4
- parents: int32 [512, 16], P('dp'), may hold values from -1 to 14, as said below
- cache_lengths: int32 [512], P('dp'), may hold values from 16 to 128, as said below
- accepted_counts: int32 [512], P('dp'), may hold values from 4 to 16, as said below
- dest_map: int32 [8192, 1], P('dp'), may hold values from 0 to 63; in each aligned block of 128 rows (0 to 127, 128 to 255, ...) at most 3 rows name the same one
- low_hidden: bfloat16 [8192, 16384], P('dp', 'head'), may hold values from -320 to 320
- mid_hidden: bfloat16 [8192, 16384], P('dp', 'head'), may hold values from -320 to 320
- norm_gains: bfloat16 [3, 16384], P(None, 'head'), may hold values from 0.099609375 to 1.8984375
- merge_down: bfloat16 [16384, 384], P('head'), may hold values from -0.02734375 to 0.02734375
- merge_up: bfloat16 [128, 16384], P(None, 'head'), may hold values from -0.5 to 0.5
- out_grad: bfloat16 [12288, 16384], P('dp', 'head'), may hold values from -0.059814453 to 0.059814453
Outputs:
- gradient_merge_down: float32 [16384, 384], P('head')
- grad_up: float32 [128, 16384], P(None, 'head')
Inputs may be any that keep to these rules, and one draw needn't show every extreme that they name: parents[b, 0] = -1, and 0 <= parents[b, t] < t for t >= 1. `cache_lengths`: some branch has all 128 positions live. A branch accepts its first accepted_counts[b] tree tokens; some branch accepts all 16. `dest_map`: among the rows of one dp index, each trainer shard is named at most 3 times.
All inputs are finite; a program needn't handle non-finite values.
Results may differ from a plain program's by a relative error of at most 0.0055.
Values may be sent and summed in bfloat16 or wider, within the bound.
No kernel may reach another device: no remote copies, remote signals or barrier semaphores. Data moves between devices by JAX's collectives and lax.ppermute only.
A program may use at most 64 MiB of HBM per device.

v0:
```python
import jax
import jax.numpy as jnp
from jax import lax
from jax.sharding import PartitionSpec as P

MODEL_WIDTH = 16384
QHEADS = 128
KVHEADS = 8
HEAD_DIM = 128
TREE = 16


EPSILON = 1e-05
MASKED = -1e30


def ancestors(parents):
    positions = jnp.arange(TREE)
    reached = (parents[:, :, None] == positions[None, None, :]).astype(jnp.float32) + jnp.eye(
        TREE, dtype=jnp.float32
    )[None]
    for repeat_no in range(max(1, (TREE - 1).bit_length())):
        reached = jnp.minimum(
            jnp.einsum("nts,nsu->ntu", reached, reached, precision=lax.Precision.HIGHEST), 1.0
        )
    return reached > 0.5


def verify_attention(
    queries, tree_keys, tree_values, cache_keys, cache_values, parents, cache_lengths
):
    branches = parents.shape[0]
    groups = cache_keys.shape[2] // HEAD_DIM
    group_size = QHEADS // KVHEADS
    cache_len = cache_keys.shape[1]
    score_scale = HEAD_DIM ** (-0.5)
    query_heads = queries.reshape(branches, TREE, groups, group_size, HEAD_DIM)
    far_keys = cache_keys.reshape(branches, cache_len, groups, HEAD_DIM)
    far_values = cache_values.reshape(branches, cache_len, groups, HEAD_DIM)
    near_keys = tree_keys.reshape(branches, TREE, groups, HEAD_DIM)
    near_values = tree_values.reshape(branches, TREE, groups, HEAD_DIM)
    cache_scores = (
        jnp.einsum("btgjd,bpgd->bgjtp", query_heads, far_keys, preferred_element_type=jnp.float32)
        * score_scale
    )
    tree_scores = (
        jnp.einsum("btgjd,bsgd->bgjts", query_heads, near_keys, preferred_element_type=jnp.float32)
        * score_scale
    )
    visible = jnp.arange(cache_len)[None, :] < cache_lengths[:, None]
    cache_scores = jnp.where(visible[:, None, None, None, :], cache_scores, MASKED)
    tree_scores = jnp.where(ancestors(parents)[:, None, None, :, :], tree_scores, MASKED)
    row_max = jnp.maximum(jnp.max(cache_scores, axis=-1), jnp.max(tree_scores, axis=-1))
    cache_weights = jnp.exp(cache_scores - row_max[..., None])
    tree_weights = jnp.exp(tree_scores - row_max[..., None])
    denominator = jnp.sum(cache_weights, axis=-1) + jnp.sum(tree_weights, axis=-1)
    cache_probs = (cache_weights / denominator[..., None]).astype(jnp.bfloat16)
    tree_probs = (tree_weights / denominator[..., None]).astype(jnp.bfloat16)
    attended = jnp.einsum(
        "bgjtp,bpgd->btgjd", cache_probs, far_values, preferred_element_type=jnp.float32
    )
    attended = attended + jnp.einsum(
        "bgjts,bsgd->btgjd", tree_probs, near_values, preferred_element_type=jnp.float32
    )
    return attended.reshape(branches * TREE, groups * group_size * HEAD_DIM).astype(jnp.bfloat16)


def draft_grads(features, grad_in, norm_gains, merge_down, merge_up):
    rank_size = merge_up.shape[0]
    widened = features.astype(jnp.float32)
    squares = jnp.sum(widened * widened, axis=2)
    rescaled_rows = (widened * norm_gains.astype(jnp.float32)[None]).astype(jnp.bfloat16)
    partial_terms = jnp.stack(
        [
            jnp.dot(
                rescaled_rows[:, layer_index],
                merge_down[:, layer_index * rank_size : (layer_index + 1) * rank_size],
                preferred_element_type=jnp.float32,
            )
            for layer_index in range(3)
        ],
        axis=1,
    )
    back_part = lax.dot_general(
        grad_in, merge_up, (((1,), (1,)), ((), ())), preferred_element_type=jnp.float32
    )
    totals, back_rows = lax.psum((squares, back_part), "head")
    inverse = lax.rsqrt(totals / MODEL_WIDTH + EPSILON)
    mixed_rank = lax.psum(jnp.sum(inverse[:, :, None] * partial_terms, axis=1), "head")
    active = jax.nn.silu(mixed_rank).astype(jnp.bfloat16)
    sigmoid_z = jax.nn.sigmoid(mixed_rank)
    grad_mixed = back_rows * sigmoid_z * (1.0 + mixed_rank * (1.0 - sigmoid_z))
    gradient_rescaled = (inverse[:, :, None] * grad_mixed[:, None, :]).astype(jnp.bfloat16)
    gradient_merge_down = jnp.concatenate(
        [
            lax.dot_general(
                rescaled_rows[:, layer_index],
                gradient_rescaled[:, layer_index],
                (((0,), (0,)), ((), ())),
                preferred_element_type=jnp.float32,
            )
            for layer_index in range(3)
        ],
        axis=1,
    )
    grad_up = lax.dot_general(
        active, grad_in, (((0,), (0,)), ((), ())), preferred_element_type=jnp.float32
    )
    return (gradient_merge_down, grad_up)


def body(
    queries,
    tree_keys,
    tree_values,
    cache_keys,
    cache_values,
    parents,
    cache_lengths,
    accepted_counts,
    dest_map,
    low_hidden,
    mid_hidden,
    norm_gains,
    merge_down,
    merge_up,
    out_grad,
):
    row_count = queries.shape[0]
    width = low_hidden.shape[1]
    peer_count = lax.axis_size("dp")
    slot_count = out_grad.shape[0]
    per_peer = slot_count // peer_count
    accepted = jnp.arange(row_count) % TREE < jnp.repeat(
        accepted_counts, TREE, total_repeat_length=row_count
    )
    target = dest_map[:, 0]
    one_hot = (target[:, None] == jnp.arange(peer_count)[None, :]).astype(jnp.float32)
    earlier = (jnp.arange(row_count)[:, None] > jnp.arange(row_count)[None, :]).astype(jnp.float32)
    before = jnp.dot(earlier, one_hot, precision=lax.Precision.HIGHEST)
    slot_rank = jnp.sum(before * one_hot, axis=1).astype(jnp.int32)
    slot_index = target * per_peer + slot_rank
    placer = ((slot_index[None, :] == jnp.arange(slot_count)[:, None]) & accepted[None, :]).astype(
        jnp.bfloat16
    )

    def packed(array):
        return jnp.dot(placer, array, preferred_element_type=jnp.float32).astype(jnp.bfloat16)

    attended = verify_attention(
        queries, tree_keys, tree_values, cache_keys, cache_values, parents, cache_lengths
    )
    all_block = jnp.stack(
        [packed(low_hidden), packed(mid_hidden), packed(attended)], axis=1
    ).reshape(peer_count, per_peer, 3, width)
    features = lax.all_to_all(all_block, "dp", split_axis=0, concat_axis=0, tiled=True).reshape(
        slot_count, 3, width
    )
    gradient_merge_down, grad_up = draft_grads(features, out_grad, norm_gains, merge_down, merge_up)
    summed_down, summed_up = lax.psum((gradient_merge_down, grad_up), "dp")
    return (summed_down, summed_up)


def solution(mesh):
    placed = (
        P("dp", "head"),
        P("dp", "head"),
        P("dp", "head"),
        P("dp", None, "head"),
        P("dp", None, "head"),
        P("dp", None),
        P("dp"),
        P("dp"),
        P("dp", None),
        P("dp", "head"),
        P("dp", "head"),
        P(None, "head"),
        P("head", None),
        P(None, "head"),
        P("dp", "head"),
    )
    return jax.shard_map(
        body,
        mesh=mesh,
        in_specs=placed,
        out_specs=(P("head", None), P(None, "head")),
        check_vma=False,
    )
```

profile of v0, /device:TPU:2, one launch (start us, length us, event | category | flops | bytes accessed | tf_op | source)
XLA Modules:
  0.0 882.6 jit_solution(13178435317797646712)
XLA Ops:
  9.6 1.1 copy.41
  10.8 2.3 fusion.49
  15.8 1.4 fusion.22
  18.2 5.0 fusion.45
  24.1 1.2 convolution_convert_fusion.2
  25.3 2.4 stack.24
  27.8 1.5 copy.31
  29.5 1.4 fusion.6
  31.1 1.2 convolution_convert_fusion
  32.3 3.3 stack.26
  35.6 3.8 pad_maximum_fusion
  39.4 3.2 copy.33
  42.6 12.8 %all-to-all-start = ((bf16[64,3,3,2048]{3,1,2,0:T(4,128)(2,1)}), bf16[64,3,3,2048]{3,1,2,0:T(4,128)(2,1)}, u32[]{:S(2)}, u32[]{:S(2)}) async-start(bf16[64,3,3,2048]{3,1,2,0:T(4,128)(2,1)} %copy.33), calls=%async_computation | async-start | bytes 6291456 | tf_op jit(solution)/shard_map/all_to_all | solution.py:156
  56.7 71.0 %all-to-all-done = bf16[64,3,3,2048]{3,1,2,0:T(4,128)(2,1)} async-done(((bf16[64,3,3,2048]{3,1,2,0:T(4,128)(2,1)}), bf16[64,3,3,2048]{3,1,2,0:T(4,128)(2,1)}, u32[]{:S(2)}, u32[]{:S(2)}) %all-to-all-start) | async-done | bytes 2359328 | tf_op jit(solution)/shard_map/all_to_all | solution.py:156
  127.6 5.6 copy.34
  133.2 8.2 reshape.184
  141.4 3.0 multiply_convert_fusion
  145.6 3.6 multiply_reduce_fusion
  149.4 18.6 %psum.35 = f32[192,3]{0,1:T(4,128)S(1)} all-reduce(f32[192,3]{0,1:T(4,128)S(1)} %reduce_sum.51), channel_id=1, replica_groups=mesh['dp'=64,'head'=8] {'head'}, use_global_device_ids=true, to_apply=%region_6.7 | all-reduce | flops 576 | bytes 4608 | tf_op jit(solution)/shard_map/psum | solution.py:87
  168.8 75.0 %all-reduce.7.cloned.1.call-done = (f32[192,128]{1,0:T(8,128)}, f32[192,128]{1,0:T(8,128)}) async-done(((f32[192,128]{1,0:T(8,128)}, f32[192,128]{1,0:T(8,128)}), (f32[192,128]{1,0:T(8,128)}, f32[192,128]{1,0:T(8,128)})) %all-reduce.7.cloned.1.call-update) | async-done | bytes 196624 | tf_op jit(solution)/shard_map/psum | solution.py:89
  243.8 2.2 fusion.33
  248.2 2.0 pad_maximum_fusion.1
  250.3 620.9 %all-reduce.5.cloned.1.call-done = (f32[2048,384]{0,1:T(8,128)}, f32[128,2048]{1,0:T(8,128)}) async-done(((f32[2048,384]{0,1:T(8,128)}, f32[128,2048]{1,0:T(8,128)}), (f32[2048,384]{0,1:T(8,128)}, f32[128,2048]{1,0:T(8,128)})) %all-reduce.5.cloned.1.call-update) | async-done | bytes 4194320 | tf_op jit(solution)/shard_map/psum | solution.py:160
  871.2 3.6 copy.36
  (74 shorter events, 13.7 us)
Async XLA Ops:
  7.2 48.5 %copy-start = (bf16[192,2048]{1,0:T(8,128)(2,1)S(1)}, bf16[192,2048]{1,0:T(8,128)(2,1)}, u32[]{:S(2)}) copy-start(bf16[192,2048]{1,0:T(8,128)(2,1)} %param.31) | copy-start | bytes 2359300
  7.2 5.9 copy-start.5
  13.6 3.6 copy-start.17
  13.7 3.8 copy-start.7
  13.7 4.4 copy-start.9
  13.7 4.4 copy-start.10
  13.7 4.4 copy-start.11
  13.7 4.4 copy-start.12
  13.7 4.4 copy-start.13
  13.7 4.4 copy-start.14
  13.7 4.4 copy-start.15
  13.8 9.4 %copy-start.2 = (bf16[128,2048]{1,0:T(8,128)(2,1)S(1)}, bf16[128,2048]{1,0:T(8,128)(2,1)}, u32[]{:S(2)}) copy-start(bf16[128,2048]{1,0:T(8,128)(2,1)} %param.27) | copy-start | bytes 1572868
  14.8 9.3 %copy-start.3 = (bf16[128,2048]{1,0:T(8,128)(2,1)S(1)}, bf16[128,2048]{1,0:T(8,128)(2,1)}, u32[]{:S(2)}) copy-start(bf16[128,2048]{1,0:T(8,128)(2,1)} %param.26) | copy-start | bytes 1572868
  23.5 5.7 copy-start.6
  42.6 13.0 %copy-start.8 = (bf16[3,2048]{1,0:T(4,128)(2,1)S(1)}, bf16[3,2048]{1,0:T(4,128)(2,1)}, u32[]{:S(2)}) copy-start(bf16[3,2048]{1,0:T(4,128)(2,1)} %param.28) | copy-start | bytes 36868
  42.6 13.0 %copy-start.4 = (bf16[128,2048]{1,0:T(8,128)(2,1)S(1)}, bf16[128,2048]{1,0:T(8,128)(2,1)}, u32[]{:S(2)}) copy-start(bf16[128,2048]{1,0:T(8,128)(2,1)} %param.30) | copy-start | bytes 1572868
  42.6 85.0 %all-to-all-start = ((bf16[64,3,3,2048]{3,1,2,0:T(4,128)(2,1)}), bf16[64,3,3,2048]{3,1,2,0:T(4,128)(2,1)}, u32[]{:S(2)}, u32[]{:S(2)}) async-start(bf16[64,3,3,2048]{3,1,2,0:T(4,128)(2,1)} %copy.33), calls=%async_computation | async-start | bytes 6291456 | tf_op jit(solution)/shard_map/all_to_all | solution.py:156
  55.4 188.4 %all-reduce.7.cloned.1.call-start = ((), (), s32[]{:S(2)}) async-start(), calls=%async_computation.2 | async-start | bytes 393216 | tf_op jit(solution)/shard_map/psum | solution.py:89
  141.4 3.1 copy-start.16
  168.7 702.5 %all-reduce.5.cloned.1.call-start = ((), (), s32[]{:S(2)}) async-start(), calls=%async_computation.1 | async-start | bytes 8388608 | tf_op jit(solution)/shard_map/psum | solution.py:160
  871.2 3.6 copy-start.1
Sparse Core Ops, SparseCore 0:
  168.9 74.9 all-reduce.6
  250.4 620.7 all-reduce.4
where the time goes:
time: 884 us; the launch traced here: 883 us
  waiting for transfers between devices  767 us (87%)
  local copies, waits for them, and re-layouts  31.5 us (4%)
  other arithmetic  23.7 us (3%)
  blocking collectives  18.6 us (2%)
  matrix products  14.5 us (2%)
  between operations  14.5 us (2%)
  starting transfers between devices  13 us (1%)
    psum x1, waiting for transfers between devices, body(): summed_down, summed_up = lax.psum((gradient_merge_down, grad_up), 'dp')  621 us
    psum x1, waiting for transfers between devices, draft_grads(): lax.psum(jnp.sum(inverse[:, :, None] * partial_terms, axis=1), 'head')  75 us
    all_to_all x1, waiting for transfers between devices, body(): lax.all_to_all(all_block, 'dp', split_axis=0, concat_axis=0, tiled=True)  71 us
    psum x1, blocking collectives, draft_grads(): totals, back_rows = lax.psum((squares, back_part), 'head')  18.6 us
  transfers between devices with their start and end apart: 3, of which 3 were waited for; matrix products, arithmetic and copies ran while one was open for 0% of the time, Pallas kernels for 0%

commit v1 on v0

v1 whole, which is shorter than its diff:
```python
import functools

import jax
import jax.numpy as jnp
from jax import lax
from jax.experimental import pallas as pl
from jax.experimental.pallas import tpu as pltpu
from jax.sharding import Mesh, PartitionSpec as P

MODEL_WIDTH = 16384
HEAD_DIM = 128
TREE = 16
CACHE = 128
RANK = 128
MOST = 3
EPSILON = 1e-05
MASKED = -1e30
BF = jnp.bfloat16
F32 = jnp.float32
VMEM_LIMIT = 48 * 1024 * 1024


def params():
    return pltpu.CompilerParams(vmem_limit_bytes=VMEM_LIMIT)


def iota(shape, dim):
    return lax.broadcasted_iota(jnp.int32, shape, dim)


def dot(a, b):
    return jnp.dot(a, b, preferred_element_type=F32)


def dot_nt(a, b):
    return lax.dot_general(a, b, (((1,), (1,)), ((), ())), preferred_element_type=F32)


def dot_tn(a, b):
    return lax.dot_general(a, b, (((0,), (0,)), ((), ())), preferred_element_type=F32)


def feature_kernel(
    lengths,
    counts,
    parents,
    queries,
    tree_keys,
    tree_values,
    cache_keys,
    cache_values,
    low,
    mid,
    gains,
    merge_down,
    turned,
    partial,
    reach,
    rows,
    squares,
):
    branch = pl.program_id(0)
    branches = pl.num_programs(0)
    count, width = rows.shape[1], rows.shape[2]
    heads = width // HEAD_DIM

    @pl.when(branch == 0)
    def _():
        groups = parents.shape[0]
        owner = (iota((count, groups), 0) // TREE == iota((count, groups), 1)).astype(F32)
        spread = jnp.dot(owner, parents[...].astype(F32), preferred_element_type=F32)
        own = iota((count, TREE), 0) % TREE == iota((count, TREE), 1)
        parent = jnp.sum(jnp.where(own, spread, 0.0), axis=1, keepdims=True).astype(jnp.int32)
        row, column = iota((count, count), 0), iota((count, count), 1)
        linked = (column == row) | ((parent >= 0) & (column == row // TREE * TREE + parent))
        reached = jnp.where(linked, 1.0, 0.0)
        for _ in range((TREE - 1).bit_length()):
            step = reached.astype(BF)
            reached = jnp.minimum(dot(step, step), 1.0)
        reach[...] = reached

    start = pl.multiple_of(branch * TREE, TREE)
    here = pl.ds(start, TREE)
    query = queries[...]
    query = jnp.concatenate(
        [query[:, h * HEAD_DIM : (h + 1) * HEAD_DIM] for h in range(heads)], axis=0
    )
    keys = jnp.concatenate([cache_keys[0], tree_keys[...]], axis=0)
    values = jnp.concatenate([cache_values[0], tree_values[...]], axis=0)
    scores = dot_nt(query, keys) * (HEAD_DIM**-0.5)
    live = jnp.where(iota((TREE, CACHE), 1) < lengths[branch], 1.0, 0.0)
    seen = jnp.concatenate([live, reach[here, :]], axis=1) > 0.5
    scores = jnp.where(seen[None], scores.reshape(heads, TREE, CACHE + count), MASKED)
    weights = jnp.exp(scores - jnp.max(scores, axis=2, keepdims=True))
    probs = (weights / jnp.sum(weights, axis=2, keepdims=True)).astype(BF)
    attended = dot(probs.reshape(heads * TREE, CACHE + count), values).astype(BF)
    attended = jnp.concatenate(
        [attended[h * TREE : (h + 1) * TREE, :] for h in range(heads)], axis=1
    )
    kept = iota((TREE, 1), 0) < counts[branch]
    lane = iota((TREE, RANK), 1)
    totals = jnp.zeros((TREE, RANK), F32)
    for layer, feature in enumerate((low[...], mid[...], attended)):
        feature = jnp.where(kept, feature.astype(F32), 0.0)
        total = jnp.sum(feature * feature, axis=1, keepdims=True)
        rough = total.astype(BF).astype(F32)
        totals = totals + jnp.where(lane == layer, rough, 0.0)
        totals = totals + jnp.where(lane == 3 + layer, total - rough, 0.0)
        gain = gains[layer : layer + 1, :].astype(F32)
        rows[layer, here, :] = (feature * gain).astype(BF)
    squares[here, :] = totals.astype(BF)

    @pl.when(branch == branches - 1)
    def _():
        for layer in range(3):
            block = rows[layer]
            columns = slice(layer * RANK, (layer + 1) * RANK)
            partial[:, columns] = dot(block, merge_down[:, columns]).astype(BF)
            turned[layer] = block.T
        partial[:, 3 * RANK :] = squares[...]


def back_kernel(targets, received, merge_up, partial, sent, chosen):
    count, slots = chosen.shape
    peers = slots // MOST
    target = targets[...]
    named = (target == iota((count, peers), 1)).astype(F32)
    earlier = (iota((count, count), 0) > iota((count, count), 1)).astype(BF)
    before = dot(earlier, named.astype(BF))
    place = target * MOST + jnp.sum(before * named, axis=1, keepdims=True).astype(jnp.int32)
    pick = (place == iota((count, slots), 1)).astype(BF)
    back = dot_nt(received[...], merge_up[...]).astype(BF)
    chosen[...] = pick
    sent[:, : 3 * RANK] = partial[:, : 3 * RANK]
    sent[:, 3 * RANK : 4 * RANK] = dot(pick, back).astype(BF)
    sent[:, 4 * RANK :] = partial[:, 3 * RANK :]


def merge_kernel(parts, out):
    total = parts[0].astype(F32)
    for peer in range(1, parts.shape[0]):
        total = total + parts[peer].astype(F32)
    squares = total[:, 4 * RANK :]
    inverse = [
        lax.rsqrt(
            (squares[:, i : i + 1] + squares[:, 3 + i : 4 + i]) / MODEL_WIDTH + EPSILON
        )
        for i in range(3)
    ]
    mixed = inverse[0] * total[:, :RANK]
    for i in (1, 2):
        mixed = mixed + inverse[i] * total[:, i * RANK : (i + 1) * RANK]
    back = total[:, 3 * RANK : 4 * RANK]
    gate = 1.0 / (1.0 + jnp.exp(-mixed))
    grad = back * gate * (1.0 + mixed * (1.0 - gate))
    result = [(inverse[i] * grad).astype(BF) for i in range(3)] + [(mixed * gate).astype(BF)]
    out[...] = jnp.broadcast_to(jnp.concatenate(result, axis=1)[None], out.shape)


def grads_kernel(turned, received, merged, chosen, out, up):
    step = pl.program_id(0)
    width = received.shape[1]

    @pl.when(step == 0)
    def _():
        placed = dot_tn(merged[:, 3 * RANK :], chosen[...]).astype(BF)
        up[...] = dot(placed, received[...]).astype(BF)

    for layer in range(3):
        columns = slice(layer * RANK, (layer + 1) * RANK)
        out[0, :, columns] = dot(turned[layer], merged[:, columns]).astype(BF)
    rows = up.shape[0] // pl.num_programs(0)
    block = up[pl.ds(pl.multiple_of(step * rows, rows), rows), :]
    for j in range(width // RANK):
        out[0, j * rows : (j + 1) * rows, 3 * RANK :] = block[:, j * RANK : (j + 1) * RANK]


def sum_kernel(parts, out):
    total = parts[0].astype(F32)
    for peer in range(1, parts.shape[0]):
        total = total + parts[peer].astype(F32)
    out[...] = jnp.broadcast_to(total.astype(BF), out.shape)


def final_kernel(parts, down, up):
    rows = up.shape[0]
    down[...] = parts[0, :, : 3 * RANK].astype(F32)
    for j in range(up.shape[1] // RANK):
        up[:, j * RANK : (j + 1) * RANK] = parts[0, j * rows : (j + 1) * rows, 3 * RANK :].astype(
            F32
        )


def whole(shape):
    return pl.BlockSpec(shape, lambda *_: (0,) * len(shape))


def body(
    queries,
    tree_keys,
    tree_values,
    cache_keys,
    cache_values,
    parents,
    cache_lengths,
    accepted_counts,
    dest_map,
    low_hidden,
    mid_hidden,
    norm_gains,
    merge_down,
    merge_up,
    out_grad,
):
    count, width = low_hidden.shape
    branches = parents.shape[0]
    slots = out_grad.shape[0]
    ny, nzx, nh = lax.axis_size("y"), lax.axis_size("zx"), lax.axis_size("head")
    peers = ny * nzx
    smem = pl.BlockSpec(memory_space=pltpu.SMEM)
    row_block = pl.BlockSpec((TREE, width), lambda b: (b, 0))
    cache_block = pl.BlockSpec((1, CACHE, HEAD_DIM), lambda b: (b, 0, 0))

    received = lax.all_to_all(
        out_grad.reshape(peers, slots // peers, width), ("y", "zx"), 0, 0, tiled=True
    ).reshape(slots, width)
    turned, partial = pl.pallas_call(
        feature_kernel,
        grid=(branches,),
        in_specs=[
            smem,
            smem,
            whole((branches, TREE)),
            row_block,
            whole((count, HEAD_DIM)),
            whole((count, HEAD_DIM)),
            cache_block,
            cache_block,
            row_block,
            row_block,
            whole((3, width)),
            whole((width, 3 * RANK)),
        ],
        out_specs=[whole((3, width, count)), whole((count, 4 * RANK))],
        out_shape=[
            jax.ShapeDtypeStruct((3, width, count), BF),
            jax.ShapeDtypeStruct((count, 4 * RANK), BF),
        ],
        scratch_shapes=[
            pltpu.VMEM((count, count), F32),
            pltpu.VMEM((3, count, width), BF),
            pltpu.VMEM((count, RANK), BF),
        ],
        compiler_params=params(),
        cost_estimate=pl.CostEstimate(
            flops=400_000_000, bytes_accessed=8_000_000, transcendentals=600_000
        ),
        name="features",
    )(
        cache_lengths,
        accepted_counts,
        parents,
        queries,
        tree_keys,
        tree_values,
        cache_keys,
        cache_values,
        low_hidden,
        mid_hidden,
        norm_gains,
        merge_down,
    )
    sent, chosen = pl.pallas_call(
        back_kernel,
        out_shape=[
            jax.ShapeDtypeStruct((count, 5 * RANK), BF),
            jax.ShapeDtypeStruct((count, slots), BF),
        ],
        compiler_params=params(),
        name="back",
    )(dest_map, received, merge_up, partial)
    share = count // nh
    parts = lax.all_to_all(sent.reshape(nh, share, 5 * RANK), "head", 0, 0, tiled=True)
    merged = pl.pallas_call(
        merge_kernel,
        out_shape=jax.ShapeDtypeStruct((nh, share, 4 * RANK), BF),
        compiler_params=params(),
        name="merge",
    )(parts)
    merged = lax.all_to_all(merged, "head", 0, 0, tiled=True).reshape(count, 4 * RANK)
    block = width // nzx
    grads = pl.pallas_call(
        grads_kernel,
        grid=(nzx,),
        in_specs=[
            pl.BlockSpec((3, block, count), lambda i: (0, i, 0)),
            whole((slots, width)),
            whole((count, 4 * RANK)),
            whole((count, slots)),
        ],
        out_specs=pl.BlockSpec((1, block, 4 * RANK), lambda i: (i, 0, 0)),
        out_shape=jax.ShapeDtypeStruct((nzx, block, 4 * RANK), BF),
        scratch_shapes=[pltpu.VMEM((RANK, width), BF)],
        compiler_params=params(),
        name="grads",
    )(turned, received, merged, chosen)
    grads = lax.all_to_all(grads, "zx", 0, 0, tiled=True)
    piece = block // ny
    grads = pl.pallas_call(
        sum_kernel,
        grid=(ny,),
        in_specs=[pl.BlockSpec((nzx, piece, 4 * RANK), lambda i: (0, i, 0))],
        out_specs=pl.BlockSpec((1, piece, 4 * RANK), lambda i: (i, 0, 0)),
        out_shape=jax.ShapeDtypeStruct((ny, piece, 4 * RANK), BF),
        compiler_params=params(),
        name="sum_zx",
    )(grads)
    grads = lax.all_to_all(grads, "y", 0, 0, tiled=True)
    grads = pl.pallas_call(
        sum_kernel,
        out_shape=jax.ShapeDtypeStruct((ny, piece, 4 * RANK), BF),
        compiler_params=params(),
        name="sum_y",
    )(grads)
    grads = lax.all_to_all(grads, "y", 0, 0, tiled=True).reshape(block, 4 * RANK)
    grads = lax.all_to_all(
        jnp.broadcast_to(grads[None], (nzx, block, 4 * RANK)), "zx", 0, 0, tiled=True
    )
    return pl.pallas_call(
        final_kernel,
        grid=(nzx,),
        in_specs=[pl.BlockSpec((1, block, 4 * RANK), lambda i: (i, 0, 0))],
        out_specs=[
            pl.BlockSpec((block, 3 * RANK), lambda i: (i, 0)),
            pl.BlockSpec((RANK // nzx, width), lambda i: (i, 0)),
        ],
        out_shape=[
            jax.ShapeDtypeStruct((width, 3 * RANK), F32),
            jax.ShapeDtypeStruct((RANK, width), F32),
        ],
        compiler_params=params(),
        name="final",
    )(grads)


def solution(mesh):
    fine = Mesh(mesh.devices.reshape(8, 8, 8), ("y", "zx", "head"))
    dp = ("y", "zx")
    placed = (
        P(dp, "head"),
        P(dp, "head"),
        P(dp, "head"),
        P(dp, None, "head"),
        P(dp, None, "head"),
        P(dp, None),
        P(dp),
        P(dp),
        P(dp, None),
        P(dp, "head"),
        P(dp, "head"),
        P(None, "head"),
        P("head", None),
        P(None, "head"),
        P(dp, "head"),
    )
    return jax.shard_map(
        body,
        mesh=fine,
        in_specs=placed,
        out_specs=(P("head", None), P(None, "head")),
        check_vma=False,
    )
```

time: 884 us -> 169 us (0.19)
  waiting for transfers between devices: 767 us -> 13.9 us
  blocking collectives: 18.6 us -> 113 us
  other arithmetic: 23.7 us -> 0 us
  local copies, waits for them, and re-layouts: 31.5 us -> 13.7 us
  matrix products: 14.5 us -> 0 us
  Pallas kernels: 0 us -> 14 us
  between operations: 14.5 us -> 0.83 us
    psum x2 -> x0, waiting for transfers between devices: 696 us -> none  [the longest x1 621 us: body(): summed_down, summed_up = lax.psum((gradient_merge_down, grad_up), 'dp')]
    all_to_all x0 -> x6, blocking collectives: none -> 113 us  [the longest x1 29 us: body(): grads = lax.all_to_all(grads, 'zx', 0, 0, tiled=True)]
    all_to_all x1, waiting for transfers between devices: 71 us -> 13.9 us  [body(): lax.all_to_all(out_grad.reshape(peers, slots // peers, width), ('y', 'zx'...]
    psum x1 -> x0, blocking collectives: 18.6 us -> none  [draft_grads(): totals, back_rows = lax.psum((squares, back_part), 'head')]
    dot_general x20 -> x0, matrix products: 14.5 us -> none  [the longest x3 2.85 us: packed(): jnp.dot(placer, array, preferred_element_type=jnp.float32)]
    pallas_call x0 -> x7, Pallas kernels: none -> 14 us  [the longest x1 6.96 us: body(): pl.pallas_call(feature_kernel, grid=(branches,), in_specs=[smem, smem, wh...]
    convert_element_type x3 -> x0, local copies, waits for them, and re-layouts: 13.9 us -> none  [the longest x2 13.8 us: draft_grads(): widened = features.astype(jnp.float32)]
    another operation x5 -> x0, local copies, waits for them, and re-layouts: 10.9 us -> none  [the longest x4 9.42 us: body(): jnp.stack([packed(low_hidden), packed(mid_hidden), packed(attended)], axi...]
  transfers between devices with their start and end apart: 3 -> 1, of which waited for: 3 -> 1; matrix products, arithmetic and copies ran while one was open for 0% -> 0% of each run, Pallas kernels for 0% -> 4%
where the time goes in v1:
time: 169 us; the launch traced here: 168 us
  blocking collectives  113 us (67%)
  Pallas kernels  14 us (8%)
  waiting for transfers between devices  13.9 us (8%)
  local copies, waits for them, and re-layouts  13.7 us (8%)
  starting transfers between devices  12.6 us (7%)
    all_to_all x1, blocking collectives, body(): grads = lax.all_to_all(grads, 'zx', 0, 0, tiled=True)  29 us
    all_to_all x1, blocking collectives, body(): lax.all_to_all(jnp.broadcast_to(grads[None], (nzx, block, 4 * RANK)), 'zx...  25.9 us
    all_to_all x1, blocking collectives, body(): lax.all_to_all(sent.reshape(nh, share, 5 * RANK), 'head', 0, 0, tiled=True)  19.8 us
    all_to_all x1, waiting for transfers between devices, body(): lax.all_to_all(out_grad.reshape(peers, slots // peers, width), ('y', 'zx'...  13.9 us
    all_to_all x1, blocking collectives, body(): grads = lax.all_to_all(grads, 'y', 0, 0, tiled=True)  13.3 us
    all_to_all x1, blocking collectives, body(): lax.all_to_all(grads, 'y', 0, 0, tiled=True).reshape(block, 4 * RANK)  12.9 us
    all_to_all x1, starting transfers between devices, body(): lax.all_to_all(out_grad.reshape(peers, slots // peers, width), ('y', 'zx'...  12.6 us
    all_to_all x1, blocking collectives, body(): lax.all_to_all(merged, 'head', 0, 0, tiled=True).reshape(count, 4 * RANK)  12 us
  transfers between devices with their start and end apart: 1, of which 1 were waited for; matrix products, arithmetic and copies ran while one was open for 0% of the time, Pallas kernels for 4%

profile of v1, /device:TPU:2, one launch (start us, length us, event | category | flops | bytes accessed | tf_op | source)
XLA Modules:
  0.0 168.1 jit_solution(10367006488879376629)
XLA Ops:
  0.7 3.4 %reshape.17 = bf16[64,3,2048]{2,1,0:T(4,128)(2,1)} reshape(bf16[192,2048]{1,0:T(8,128)(2,1)} %param.29) | data formatting | bytes 1572864 | tf_op jit(solution)/shard_map/reshape | solution.py:225
  4.1 12.6 %all-to-all-start = ((bf16[64,3,2048]{2,1,0:T(4,128)(2,1)}), bf16[64,3,2048]{2,1,0:T(4,128)(2,1)}, u32[]{:S(2)}, u32[]{:S(2)}) async-start(bf16[64,3,2048]{2,1,0:T(4,128)(2,1)} %reshape.17), calls=%async_computation | async-start | bytes 2097152 | tf_op jit(solution)/shard_map/all_to_all | solution.py:224
  16.9 1.0 copy-done.1
  18.0 1.0 copy-done.2
  19.0 1.0 copy-done.3
  20.1 0.9 copy-done.6
  21.0 0.7 copy-done.12
  21.7 0.7 copy-done.13
  22.4 0.7 copy-done.14
  23.0 7.0 %features.1 = (bf16[3,2048,128]{2,1,0:T(8,128)(2,1)S(1)}, bf16[128,512]{1,0:T(8,128)(2,1)S(1)}) custom-call(s32[8]{0:T(128)S(1)} %copy-done.13, s32[8]{0:T(128)S(1)} %copy-done.14, s32[8,16]{1,0:T(8,128)S(1)} %copy-done.12, bf16[128,2048]{1,0:T(8,128)(2,1)S(1)} %copy-done.1, bf16[128,128]{1,0:T(8,128)(2,1)S(1)} %copy-done.9, ...), custom_call_target="tpu_custom_call" | custom-call | flops 400000000 | bytes 8000000 | tf_op jit(solution)/shard_map/features/pallas_call | solution.py:227
  30.0 0.6 copy-done.7
  30.6 13.9 %all-to-all-done = bf16[64,3,2048]{2,1,0:T(4,128)(2,1)} async-done(((bf16[64,3,2048]{2,1,0:T(4,128)(2,1)}), bf16[64,3,2048]{2,1,0:T(4,128)(2,1)}, u32[]{:S(2)}, u32[]{:S(2)}) %all-to-all-start) | async-done | bytes 786464 | tf_op jit(solution)/shard_map/all_to_all | solution.py:224
  44.6 2.4 %reshape.18.received = bf16[192,2048]{1,0:T(8,128)(2,1)S(1)} reshape(bf16[64,3,2048]{2,1,0:T(4,128)(2,1)} %all-to-all-done) | data formatting | bytes 1572864 | tf_op jit(solution)/shard_map/reshape | solution.py:226
  47.0 0.9 copy-done.8
  47.9 0.6 back.1
  48.5 19.8 %all_to_all.35.parts = bf16[8,16,640]{2,1,0:T(8,128)(2,1)S(1)} all-to-all(bf16[8,16,640]{2,1,0:T(8,128)(2,1)S(1)} %bitcast.4), channel_id=1, replica_groups=mesh['y'=8,'zx'=8,'head'=8] {'head'}, dimensions={0} | all-to-all | bytes 327680 | tf_op jit(solution)/shard_map/all_to_all | solution.py:283
  68.5 12.0 %all_to_all.36 = bf16[8,16,512]{2,1,0:T(8,128)(2,1)S(1)} all-to-all(bf16[8,16,512]{2,1,0:T(8,128)(2,1)S(1)} %merge.1), channel_id=1, replica_groups=mesh['y'=8,'zx'=8,'head'=8] {'head'}, dimensions={0} | all-to-all | bytes 262144 | tf_op jit(solution)/shard_map/all_to_all | solution.py:290
  80.5 2.3 %grads.1 = bf16[8,256,512]{2,1,0:T(8,128)(2,1)S(1)} custom-call(bf16[3,2048,128]{2,1,0:T(8,128)(2,1)S(1)} %get-tuple-element.6.turned, bf16[192,2048]{1,0:T(8,128)(2,1)S(1)} %reshape.18.received, bf16[128,512]{1,0:T(8,128)(2,1)S(1)} %bitcast.3, bf16[128,192]{1,0:T(8,128)(2,1)S(1)} %get-tuple-element.9.chosen), custom_call_target="tpu_custom_call" | custom-call | tf_op jit(solution)/shard_map/grads/pallas_call | solution.py:292
  82.8 29.0 %all_to_all.37.parts = bf16[8,256,512]{2,1,0:T(8,128)(2,1)S(1)} all-to-all(bf16[8,256,512]{2,1,0:T(8,128)(2,1)S(1)} %grads.1), channel_id=1, replica_groups=mesh['y'=8,'zx'=8,'head'=8] {'zx'}, dimensions={0} | all-to-all | bytes 4194304 | tf_op jit(solution)/shard_map/all_to_all | solution.py:307
  111.8 0.6 sum_zx.1
  112.4 13.3 %all_to_all.38.parts = bf16[8,32,512]{2,1,0:T(8,128)(2,1)S(1)} all-to-all(bf16[8,32,512]{2,1,0:T(8,128)(2,1)S(1)} %sum_zx.1), channel_id=1, replica_groups=mesh['y'=8,'zx'=8,'head'=8] {'y'}, dimensions={0} | all-to-all | bytes 524288 | tf_op jit(solution)/shard_map/all_to_all | solution.py:318
  125.7 12.9 %all_to_all.39 = bf16[8,32,512]{2,1,0:T(8,128)(2,1)S(1)} all-to-all(bf16[8,32,512]{2,1,0:T(8,128)(2,1)S(1)} %sum_y.1), channel_id=1, replica_groups=mesh['y'=8,'zx'=8,'head'=8] {'y'}, dimensions={0} | all-to-all | bytes 524288 | tf_op jit(solution)/shard_map/all_to_all | solution.py:325
  138.8 25.9 %all_to_all.40.parts = bf16[8,256,512]{2,1,0:T(8,128)(2,1)S(1)} all-to-all(bf16[8,256,512]{2,1,0:T(8,128)(2,1)S(1)} %broadcast_in_dim.8), channel_id=1, replica_groups=mesh['y'=8,'zx'=8,'head'=8] {'zx'}, dimensions={0} | all-to-all | bytes 4194304 | tf_op jit(solution)/shard_map/all_to_all | solution.py:326
  164.7 3.4 %final.1 = (f32[2048,384]{1,0:T(8,128)}, f32[128,2048]{1,0:T(8,128)}) custom-call(bf16[8,256,512]{2,1,0:T(8,128)(2,1)S(1)} %all_to_all.40.parts), custom_call_target="tpu_custom_call" | custom-call | tf_op jit(solution)/shard_map/final/pallas_call | solution.py:329
  (27 shorter events, 0.6 us)
Async XLA Ops:
  0.6 16.1 %copy-start.15 = (s32[128,1]{0,1:T(1,128)S(1)}, s32[128,1]{0,1:T(1,128)}, u32[]{:S(2)}) copy-start(s32[128,1]{0,1:T(1,128)} %param.23) | copy-start | bytes 1540
  0.6 16.2 %copy-start = (bf16[2048,384]{1,0:T(8,128)(2,1)S(1)}, bf16[2048,384]{1,0:T(8,128)(2,1)}, u32[]{:S(2)}) copy-start(bf16[2048,384]{1,0:T(8,128)(2,1)} %merge_down.1) | copy-start | bytes 4718596
  0.7 16.2 %copy-start.11 = (bf16[3,2048]{1,0:T(4,128)(2,1)S(1)}, bf16[3,2048]{1,0:T(4,128)(2,1)}, u32[]{:S(2)}) copy-start(bf16[3,2048]{1,0:T(4,128)(2,1)} %gains.1) | copy-start | bytes 36868
  0.7 16.2 %copy-start.5 = (bf16[8,128,128]{2,1,0:T(8,128)(2,1)S(1)}, bf16[8,128,128]{2,1,0:T(8,128)(2,1)}, u32[]{:S(2)}) copy-start(bf16[8,128,128]{2,1,0:T(8,128)(2,1)} %cache_keys.1) | copy-start | bytes 786436
  0.7 16.2 %copy-start.10 = (bf16[128,128]{1,0:T(8,128)(2,1)S(1)}, bf16[128,128]{1,0:T(8,128)(2,1)}, u32[]{:S(2)}) copy-start(bf16[128,128]{1,0:T(8,128)(2,1)} %tree_values.1) | copy-start | bytes 98308
  0.7 16.2 %copy-start.9 = (bf16[128,128]{1,0:T(8,128)(2,1)S(1)}, bf16[128,128]{1,0:T(8,128)(2,1)}, u32[]{:S(2)}) copy-start(bf16[128,128]{1,0:T(8,128)(2,1)} %tree_keys.1) | copy-start | bytes 98308
  4.1 40.5 %all-to-all-start = ((bf16[64,3,2048]{2,1,0:T(4,128)(2,1)}), bf16[64,3,2048]{2,1,0:T(4,128)(2,1)}, u32[]{:S(2)}, u32[]{:S(2)}) async-start(bf16[64,3,2048]{2,1,0:T(4,128)(2,1)} %reshape.17), calls=%async_computation | async-start | bytes 2097152 | tf_op jit(solution)/shard_map/all_to_all | solution.py:224
  16.9 1.0 copy-start.1
  18.0 1.0 copy-start.2
  19.0 1.0 copy-start.3
  20.1 0.9 copy-start.6
  21.0 0.7 copy-start.12
  21.7 0.7 copy-start.13
  22.3 0.7 copy-start.14
  30.0 0.7 copy-start.7
  30.6 16.4 %copy-start.4 = (bf16[128,2048]{1,0:T(8,128)(2,1)S(1)}, bf16[128,2048]{1,0:T(8,128)(2,1)}, u32[]{:S(2)}) copy-start(bf16[128,2048]{1,0:T(8,128)(2,1)} %merge_up.1) | copy-start | bytes 1572868
  47.0 0.9 copy-start.8

commit v2 on v1

v2 whole, which is shorter than its diff:
```python
import jax
import jax.numpy as jnp
from jax import lax
from jax.experimental import pallas as pl
from jax.experimental.pallas import tpu as pltpu
from jax.sharding import Mesh, PartitionSpec as P

MODEL_WIDTH = 16384
HEAD_DIM = 128
TREE = 16
CACHE = 128
RANK = 128
MOST = 3
NX = 4
EPSILON = 1e-05
MASKED = -1e30
BF = jnp.bfloat16
F32 = jnp.float32
VMEM_LIMIT = 48 * 1024 * 1024


def params():
    return pltpu.CompilerParams(vmem_limit_bytes=VMEM_LIMIT)


def iota(shape, dim):
    return lax.broadcasted_iota(jnp.int32, shape, dim)


def dot(a, b):
    return jnp.dot(a, b, preferred_element_type=F32)


def dot_nt(a, b):
    return lax.dot_general(a, b, (((1,), (1,)), ((), ())), preferred_element_type=F32)


def dot_tn(a, b):
    return lax.dot_general(a, b, (((0,), (0,)), ((), ())), preferred_element_type=F32)


def feature_kernel(
    place,
    lengths,
    counts,
    parents,
    queries,
    tree_keys,
    tree_values,
    cache_keys,
    cache_values,
    low,
    mid,
    gains,
    merge_down,
    own,
    first,
    second,
    third,
    partial,
    reach,
    rows,
    squares,
):
    branch = pl.program_id(0)
    branches = pl.num_programs(0)
    count, width = rows.shape[1], rows.shape[2]
    heads = width // HEAD_DIM

    @pl.when(branch == 0)
    def _():
        groups = parents.shape[0]
        owner = (iota((count, groups), 0) // TREE == iota((count, groups), 1)).astype(F32)
        spread = jnp.dot(owner, parents[...].astype(F32), preferred_element_type=F32)
        same = iota((count, TREE), 0) % TREE == iota((count, TREE), 1)
        parent = jnp.sum(jnp.where(same, spread, 0.0), axis=1, keepdims=True).astype(jnp.int32)
        row, column = iota((count, count), 0), iota((count, count), 1)
        linked = (column == row) | ((parent >= 0) & (column == row // TREE * TREE + parent))
        reached = jnp.where(linked, 1.0, 0.0)
        for _ in range((TREE - 1).bit_length()):
            step = reached.astype(BF)
            reached = jnp.minimum(dot(step, step), 1.0)
        reach[...] = reached

    start = pl.multiple_of(branch * TREE, TREE)
    here = pl.ds(start, TREE)
    query = queries[...]
    query = jnp.concatenate(
        [query[:, h * HEAD_DIM : (h + 1) * HEAD_DIM] for h in range(heads)], axis=0
    )
    keys = jnp.concatenate([cache_keys[0], tree_keys[...]], axis=0)
    values = jnp.concatenate([cache_values[0], tree_values[...]], axis=0)
    scores = dot_nt(query, keys) * (HEAD_DIM**-0.5)
    live = jnp.where(iota((TREE, CACHE), 1) < lengths[branch], 1.0, 0.0)
    seen = jnp.concatenate([live, reach[here, :]], axis=1) > 0.5
    scores = jnp.where(seen[None], scores.reshape(heads, TREE, CACHE + count), MASKED)
    weights = jnp.exp(scores - jnp.max(scores, axis=2, keepdims=True))
    probs = (weights / jnp.sum(weights, axis=2, keepdims=True)).astype(BF)
    attended = dot(probs.reshape(heads * TREE, CACHE + count), values).astype(BF)
    attended = jnp.concatenate(
        [attended[h * TREE : (h + 1) * TREE, :] for h in range(heads)], axis=1
    )
    kept = iota((TREE, 1), 0) < counts[branch]
    lane = iota((TREE, RANK), 1)
    totals = jnp.zeros((TREE, RANK), F32)
    for layer, feature in enumerate((low[...], mid[...], attended)):
        feature = jnp.where(kept, feature.astype(F32), 0.0)
        total = jnp.sum(feature * feature, axis=1, keepdims=True)
        totals = totals + jnp.where(lane == layer, total, 0.0)
        gain = gains[layer : layer + 1, :].astype(F32)
        rows[layer, here, :] = (feature * gain).astype(BF)
    squares[here, :] = totals

    @pl.when(branch == branches - 1)
    def _():
        block = own.shape[1]
        for layer in range(3):
            columns = slice(layer * RANK, (layer + 1) * RANK)
            partial[:, columns] = dot(rows[layer], merge_down[:, columns])
            for k, out in enumerate((own, first, second, third)):
                chunk = (place[0] + k) % (width // block)
                chunk = pl.ds(pl.multiple_of(chunk * block, block), block)
                out[layer] = rows[layer, :, chunk].T
        partial[:, 3 * RANK :] = squares[...]


def pack_kernel(grads, merge_up, out, rows):
    peers, height = out.shape[0], out.shape[1]
    slots = grads.shape[0] // (peers // NX)
    blocks = grads.shape[1] // NX // RANK
    wide = grads[...].astype(F32)
    products = dot_nt(grads[...], merge_up[...])
    rows[:, blocks * slots :, :] = jnp.zeros((peers, height - blocks * slots, RANK), F32)
    for x in range(NX):
        for b in range(blocks):
            column = (x * blocks + b) * RANK
            for g in range(peers // NX):
                rows[g * NX + x, b * slots : (b + 1) * slots, :] = wide[
                    g * slots : (g + 1) * slots, column : column + RANK
                ]
    for d in range(peers):
        rows[d, blocks * slots : blocks * slots + MOST, :] = products[d * MOST : (d + 1) * MOST, :]
    out[...] = rows[...].astype(BF)


def unpack_kernel(received, out, rows):
    peers = received.shape[0]
    slots = out.shape[0] // peers
    for j in range(peers):
        wide = received[j].astype(F32)
        for b in range(out.shape[1] // RANK):
            rows[j * slots : (j + 1) * slots, b * RANK : (b + 1) * RANK] = wide[
                b * slots : (b + 1) * slots, :
            ]
    out[...] = rows[...].astype(BF)


def pick_kernel(place, targets, received, partial, keep, give, info, rows, notes):
    count = rows.shape[0]
    half = keep.shape[0]
    peers = received.shape[0]
    tail = received[:, received.shape[1] - 8 :, :].astype(F32).reshape(peers * 8, RANK).astype(BF)
    target = targets[...]
    named = (target == iota((count, peers), 1)).astype(F32)
    earlier = (iota((count, count), 0) > iota((count, count), 1)).astype(BF)
    before = dot(earlier, named.astype(BF))
    rank = jnp.sum(before * named, axis=1, keepdims=True)
    chosen = target * 8 + rank.astype(jnp.int32) == iota((count, peers * 8), 1)
    rows[:, : 3 * RANK] = partial[:, : 3 * RANK]
    rows[:, 3 * RANK : 4 * RANK] = dot(chosen.astype(BF), tail)
    rows[:, 4 * RANK :] = partial[:, 3 * RANK :]
    lane = iota((count, RANK), 1)
    notes[...] = jnp.where(lane == 6, target.astype(F32), jnp.where(lane == 7, rank, 0.0))
    mine = pl.ds(pl.multiple_of(place[1] * half, half), half)
    keep[...] = rows[mine, :]
    info[...] = notes[mine, :]
    give[...] = rows[pl.ds(pl.multiple_of((1 - place[1]) * half, half), half), :]


def pair_kernel(keep, got, out):
    total = keep[...] + got[...]
    squares = total[:, 4 * RANK :]
    rough = squares.astype(BF).astype(F32)
    lane = iota(squares.shape, 1)
    for i in range(3):
        rest = squares[:, i : i + 1] - rough[:, i : i + 1]
        rough = jnp.where(lane == 3 + i, rest, rough)
    out[:, : 4 * RANK] = total[:, : 4 * RANK].astype(BF)
    out[:, 4 * RANK :] = rough.astype(BF)


def merge_kernel(parts, info, out):
    total = parts[0].astype(F32)
    for peer in range(1, parts.shape[0]):
        total = total + parts[peer].astype(F32)
    squares = total[:, 4 * RANK :]
    inverse = [
        lax.rsqrt((squares[:, i : i + 1] + squares[:, 3 + i : 4 + i]) / MODEL_WIDTH + EPSILON)
        for i in range(3)
    ]
    mixed = inverse[0] * total[:, :RANK]
    for i in (1, 2):
        mixed = mixed + inverse[i] * total[:, i * RANK : (i + 1) * RANK]
    back = total[:, 3 * RANK : 4 * RANK]
    gate = 1.0 / (1.0 + jnp.exp(-mixed))
    out[:, :RANK] = (back * gate * (1.0 + mixed * (1.0 - gate))).astype(BF)
    out[:, RANK : 2 * RANK] = (mixed * gate).astype(BF)
    notes = info[...]
    lane = iota(notes.shape, 1)
    for i in range(3):
        rough = inverse[i].astype(BF).astype(F32)
        notes = jnp.where(lane == i, rough, notes)
        notes = jnp.where(lane == 3 + i, inverse[i] - rough, notes)
    out[:, 2 * RANK :] = notes.astype(BF)


def grads_kernel(place, own, first, second, third, slots, merged, out):
    blocks = slots.shape[1] // RANK
    peer_slots = NX * MOST
    down = [None] * 3
    placed = None
    for k, turned in enumerate((own, first, second, third)):
        source = (place[0] + NX - k) % NX
        rows = jnp.concatenate([merged[2 * source], merged[2 * source + 1]], axis=0)
        notes = rows[:, 2 * RANK :].astype(F32)
        grad = rows[:, :RANK].astype(F32)
        for i in range(3):
            inverse = notes[:, i : i + 1] + notes[:, 3 + i : 4 + i]
            term = dot(turned[i], (inverse * grad).astype(BF))
            down[i] = term if down[i] is None else down[i] + term
        slot = notes[:, 6:7].astype(jnp.int32) * peer_slots + notes[:, 7:8].astype(jnp.int32)
        slot = slot + source * MOST
        chosen = (slot == iota((rows.shape[0], slots.shape[0]), 1)).astype(BF)
        term = dot_tn(rows[:, RANK : 2 * RANK], chosen)
        placed = term if placed is None else placed + term
    for i in range(3):
        out[:, i * RANK : (i + 1) * RANK] = down[i].astype(BF)
    up = dot(placed.astype(BF), slots[...]).astype(BF)
    for b in range(blocks):
        out[b * RANK : (b + 1) * RANK, 3 * RANK :] = up[:, b * RANK : (b + 1) * RANK]


def sum_kernel(parts, out):
    total = parts[0].astype(F32)
    for peer in range(1, parts.shape[0]):
        total = total + parts[peer].astype(F32)
    out[...] = jnp.broadcast_to(total.astype(BF)[None], out.shape)


def final_kernel(parts, down, up):
    down[...] = parts[0, :, : 3 * RANK].astype(F32)
    for b in range(up.shape[1] // RANK):
        columns = slice(b * RANK, (b + 1) * RANK)
        up[:, columns] = parts[0, columns, 3 * RANK :].astype(F32)


def whole(shape):
    return pl.BlockSpec(shape, lambda *_: (0,) * len(shape))


def shape(dims, kind=BF):
    return jax.ShapeDtypeStruct(dims, kind)


def call(kernel, name, out_shape, *args, scratch=(), flops=1_000_000):
    smem = pl.BlockSpec(memory_space=pltpu.SMEM)
    vmem = pl.BlockSpec(memory_space=pltpu.VMEM)
    return pl.pallas_call(
        kernel,
        in_specs=[smem if a.ndim == 1 else vmem for a in args],
        out_shape=out_shape,
        scratch_shapes=[pltpu.VMEM(*s) for s in scratch],
        compiler_params=params(),
        cost_estimate=pl.CostEstimate(flops=flops, bytes_accessed=2_000_000, transcendentals=0),
        name=name,
    )(*args)


def spread(array, n, axes):
    return lax.all_to_all(jnp.broadcast_to(array[None], (n, *array.shape)), axes, 0, 0, tiled=True)


def body(
    queries,
    tree_keys,
    tree_values,
    cache_keys,
    cache_values,
    parents,
    cache_lengths,
    accepted_counts,
    dest_map,
    low_hidden,
    mid_hidden,
    norm_gains,
    merge_down,
    merge_up,
    out_grad,
):
    count, width = low_hidden.shape
    branches = parents.shape[0]
    ny, nzl, nc = lax.axis_size("y"), lax.axis_size("zl"), lax.axis_size("c")
    nzh = lax.axis_size("zh")
    peers = ny * nzl * NX
    block = width // NX
    place = jnp.stack([lax.axis_index("x"), lax.axis_index("c")]).astype(jnp.int32)
    smem = pl.BlockSpec(memory_space=pltpu.SMEM)
    row_block = pl.BlockSpec((TREE, width), lambda b: (b, 0))
    cache_block = pl.BlockSpec((1, CACHE, HEAD_DIM), lambda b: (b, 0, 0))

    height = block // RANK * NX * MOST + 8
    packed = call(
        pack_kernel,
        "pack",
        shape((peers, height, RANK)),
        out_grad,
        merge_up,
        scratch=[((peers, height, RANK), F32)],
    )
    received = lax.all_to_all(packed, ("y", "zl", "x"), 0, 0, tiled=True)
    *turned, partial = pl.pallas_call(
        feature_kernel,
        grid=(branches,),
        in_specs=[
            smem,
            smem,
            smem,
            whole((branches, TREE)),
            row_block,
            whole((count, HEAD_DIM)),
            whole((count, HEAD_DIM)),
            cache_block,
            cache_block,
            row_block,
            row_block,
            whole((3, width)),
            whole((width, 3 * RANK)),
        ],
        out_specs=[whole((3, block, count))] * NX + [whole((count, 4 * RANK))],
        out_shape=[shape((3, block, count))] * NX + [shape((count, 4 * RANK), F32)],
        scratch_shapes=[
            pltpu.VMEM((count, count), F32),
            pltpu.VMEM((3, count, width), BF),
            pltpu.VMEM((count, RANK), F32),
        ],
        compiler_params=params(),
        cost_estimate=pl.CostEstimate(
            flops=400_000_000, bytes_accessed=8_000_000, transcendentals=600_000
        ),
        name="features",
    )(
        place,
        cache_lengths,
        accepted_counts,
        parents,
        queries,
        tree_keys,
        tree_values,
        cache_keys,
        cache_values,
        low_hidden,
        mid_hidden,
        norm_gains,
        merge_down,
    )
    for k in range(1, NX):
        turned[k] = lax.ppermute(turned[k], "x", [(i, (i + k) % NX) for i in range(NX)])
    half = count // nc
    keep, give, info = call(
        pick_kernel,
        "pick",
        [shape((half, 5 * RANK), F32), shape((half, 5 * RANK), F32), shape((half, RANK), F32)],
        place,
        dest_map,
        received,
        partial,
        scratch=[((count, 5 * RANK), F32), ((count, RANK), F32)],
    )
    got = lax.ppermute(give, "c", [(i, 1 - i) for i in range(nc)])
    paired = call(pair_kernel, "pair", shape((half, 5 * RANK)), keep, got)
    parts = spread(paired, nzh, "zh")
    merged = call(merge_kernel, "merge", shape((half, 3 * RANK)), parts, info)
    merged = spread(merged, NX * nc, ("x", "c"))
    slots = call(
        unpack_kernel,
        "unpack",
        shape((peers * NX * MOST, block)),
        received,
        scratch=[((peers * NX * MOST, block), F32)],
    )
    grads = call(
        grads_kernel, "grads", shape((block, 4 * RANK)), place, *turned, slots, merged
    )
    piece = block // (nzl * ny)
    grads = lax.all_to_all(
        grads.reshape(nzl * ny, piece, 4 * RANK), ("zl", "y"), 0, 0, tiled=True
    )
    grads = call(sum_kernel, "total", shape((ny, piece, 4 * RANK)), grads)
    grads = lax.all_to_all(grads, "y", 0, 0, tiled=True).reshape(ny * piece, 4 * RANK)
    grads = spread(grads, nzl * NX, ("zl", "x"))
    rows = ny * piece
    return pl.pallas_call(
        final_kernel,
        grid=(nzl * NX,),
        in_specs=[pl.BlockSpec((1, rows, 4 * RANK), lambda i: (i % nzl * NX + i // nzl, 0, 0))],
        out_specs=[
            pl.BlockSpec((rows, 3 * RANK), lambda i: (i, 0)),
            pl.BlockSpec((RANK, rows), lambda i: (0, i)),
        ],
        out_shape=[shape((width, 3 * RANK), F32), shape((RANK, width), F32)],
        compiler_params=params(),
        name="final",
    )(grads)


def solution(mesh):
    fine = Mesh(mesh.devices.reshape(8, 2, NX, 4, 2), ("y", "zl", "x", "zh", "c"))
    dp, head = ("y", "zl", "x"), ("zh", "c")
    placed = (
        P(dp, head),
        P(dp, head),
        P(dp, head),
        P(dp, None, head),
        P(dp, None, head),
        P(dp, None),
        P(dp),
        P(dp),
        P(dp, None),
        P(dp, head),
        P(dp, head),
        P(None, head),
        P(head, None),
        P(None, head),
        P(dp, head),
    )
    return jax.shard_map(
        body,
        mesh=fine,
        in_specs=placed,
        out_specs=(P(head, None), P(None, head)),
        check_vma=False,
    )
```

time: 169 us -> 158 us (0.935)
  the two profiles are of different devices: /device:TPU:2 before, /device:TPU:8 now
where the time goes in v2:
time: 158 us; the launch traced here: 156 us
  blocking collectives  63.2 us (40%)
  starting transfers between devices  38.2 us (24%)
  waiting for transfers between devices  21.1 us (13%)
  Pallas kernels  17 us (11%)
  local copies, waits for them, and re-layouts  16.2 us (10%)
    all_to_all x1, blocking collectives, spread(): lax.all_to_all(jnp.broadcast_to(array[None], (n, *array.shape)), axes, 0,...  29.8 us
    all_to_all x1, blocking collectives, body(): lax.all_to_all(grads.reshape(nzl * ny, piece, 4 * RANK), ('zl', 'y'), 0,...  19.8 us
    unnamed x45, local copies, waits for them, and re-layouts  14.5 us
    all_to_all x1, blocking collectives, body(): lax.all_to_all(grads, 'y', 0, 0, tiled=True).reshape(ny * piece, 4 * RANK)  13.6 us
    all_to_all x2, starting transfers between devices, spread(): lax.all_to_all(jnp.broadcast_to(array[None], (n, *array.shape)), axes, 0,...  13.2 us
    all_to_all x1, starting transfers between devices, body(): received = lax.all_to_all(packed, ('y', 'zl', 'x'), 0, 0, tiled=True)  12.4 us
    ppermute x3, starting transfers between devices, body(): lax.ppermute(turned[k], 'x', [(i, (i + k) % NX) for i in range(NX)])  10.7 us
    ppermute x3, waiting for transfers between devices, body(): lax.ppermute(turned[k], 'x', [(i, (i + k) % NX) for i in range(NX)])  9.17 us
  transfers between devices with their start and end apart: 7, of which 6 were waited for; matrix products, arithmetic and copies ran while one was open for 1% of the time, Pallas kernels for 5%

profile of v2, /device:TPU:8, one launch (start us, length us, event | category | flops | bytes accessed | tf_op | source)
XLA Modules:
  0.0 156.5 jit_solution(15223968103037856676)
XLA Ops:
  0.7 1.2 copy-done.1
  1.9 1.0 copy-done.2
  2.9 1.4 pack.1
  4.4 12.4 %all-to-all-start = ((bf16[64,56,128]{2,1,0:T(8,128)(2,1)}), bf16[64,56,128]{2,1,0:T(8,128)(2,1)S(1)}, u32[]{:S(2)}, u32[]{:S(2)}) async-start(bf16[64,56,128]{2,1,0:T(8,128)(2,1)} %pack.1), calls=%async_computation | async-start | bytes 1835008 | tf_op jit(solution)/shard_map/all_to_all | solution.py:320
  16.7 1.4 copy.17.targets
  24.7 7.9 %features.1 = (bf16[3,512,128]{2,1,0:T(8,128)(2,1)S(1)}, bf16[3,512,128]{2,1,0:T(8,128)(2,1)}, bf16[3,512,128]{2,1,0:T(8,128)(2,1)}, bf16[3,512,128]{2,1,0:T(8,128)(2,1)}, f32[128,512]{1,0:T(8,128)S(1)}) custom-call(s32[2]{0:T(128)S(1)} %pad_add_fusion.place, s32[8]{0:T(128)S(1)} %copy-done.20, s32[8]{0:T(128)S(1)} %copy-done.21, s32[8,16]{1,0:T(8,128)S(1)} %copy-done.19, ...), custom_call_target="tpu_custom_call" | custom-call | flops 400000000 | bytes 8000000 | tf_op jit(solution)/shard_map/features/pallas_call | solution.py:321
  34.6 7.0 %all-to-all-done.received = bf16[64,56,128]{2,1,0:T(8,128)(2,1)S(1)} async-done(((bf16[64,56,128]{2,1,0:T(8,128)(2,1)}), bf16[64,56,128]{2,1,0:T(8,128)(2,1)S(1)}, u32[]{:S(2)}, u32[]{:S(2)}) %all-to-all-start) | async-done | bytes 917536 | tf_op jit(solution)/shard_map/all_to_all | solution.py:320
  44.0 1.1 pick.1
  45.1 1.9 %collective-permute-start.3 = (f32[64,640]{1,0:T(8,128)S(1)}, f32[64,640]{1,0:T(8,128)S(1)}, u32[]{:S(2)}, u32[]{:S(2)}) collective-permute-start(f32[64,640]{1,0:T(8,128)S(1)} %get-tuple-element.16), channel_id=1, source_target_pairs={{0,1},{1,0},{2,3},{3,2},{4,5},{5,4},{6,7},{7,6},{8,9},{9,8},{10,11... | collective-permute-start | bytes 491528 | tf_op jit(solution)/shard_map/ppermute | solution.py:379
  47.0 1.4 collective-permute-done.3.got
  49.3 9.5 %all-to-all-start.1 = ((bf16[4,64,640]{2,1,0:T(8,128)(2,1)}), bf16[4,64,640]{2,1,0:T(8,128)(2,1)S(1)}, u32[]{:S(2)}, u32[]{:S(2)}) async-start(bf16[4,64,640]{2,1,0:T(8,128)(2,1)} %broadcast_in_dim.8), calls=%async_computation.1 | async-start | bytes 655360 | tf_op jit(solution)/shard_map/all_to_all | solution.py:280
  58.9 3.2 %collective-permute-start = (bf16[3,512,128]{2,1,0:T(8,128)(2,1)}, bf16[3,512,128]{2,1,0:T(8,128)(2,1)S(1)}, u32[]{:S(2)}, u32[]{:S(2)}) collective-permute-start(bf16[3,512,128]{2,1,0:T(8,128)(2,1)} %get-tuple-element.11), channel_id=1, source_target_pairs={{0,8},{8,16},{16,24},{24,0},{1,9},{9,17},{17,25},{25,1},{2,10},{10... | collective-permute-start | bytes 1179656 | tf_op jit(solution)/shard_map/ppermute | solution.py:367
  62.1 4.4 %collective-permute-start.1 = (bf16[3,512,128]{2,1,0:T(8,128)(2,1)}, bf16[3,512,128]{2,1,0:T(8,128)(2,1)S(1)}, u32[]{:S(2)}, u32[]{:S(2)}) collective-permute-start(bf16[3,512,128]{2,1,0:T(8,128)(2,1)} %get-tuple-element.12), channel_id=1, source_target_pairs={{0,16},{8,24},{16,0},{24,8},{1,17},{9,25},{17,1},{25,9},{2,18},{10... | collective-permute-start | bytes 1179656 | tf_op jit(solution)/shard_map/ppermute | solution.py:367
  66.6 3.1 %collective-permute-start.2 = (bf16[3,512,128]{2,1,0:T(8,128)(2,1)}, bf16[3,512,128]{2,1,0:T(8,128)(2,1)}, u32[]{:S(2)}, u32[]{:S(2)}) collective-permute-start(bf16[3,512,128]{2,1,0:T(8,128)(2,1)} %get-tuple-element.13), channel_id=1, source_target_pairs={{0,24},{8,0},{16,8},{24,16},{1,25},{9,1},{17,9},{25,17},{2,26},{10... | collective-permute-start | bytes 1179656 | tf_op jit(solution)/shard_map/ppermute | solution.py:367
  69.6 1.9 %all-to-all-done.1.parts = bf16[4,64,640]{2,1,0:T(8,128)(2,1)S(1)} async-done(((bf16[4,64,640]{2,1,0:T(8,128)(2,1)}), bf16[4,64,640]{2,1,0:T(8,128)(2,1)S(1)}, u32[]{:S(2)}, u32[]{:S(2)}) %all-to-all-start.1) | async-done | bytes 327712 | tf_op jit(solution)/shard_map/all_to_all | solution.py:280
  72.6 3.6 %all-to-all-start.2 = ((bf16[8,64,384]{2,1,0:T(8,128)(2,1)}), bf16[8,64,384]{2,1,0:T(8,128)(2,1)S(1)}, u32[]{:S(2)}, u32[]{:S(2)}) async-start(bf16[8,64,384]{2,1,0:T(8,128)(2,1)} %broadcast_in_dim.9), calls=%async_computation.2 | async-start | bytes 786432 | tf_op jit(solution)/shard_map/all_to_all | solution.py:280
  76.4 6.8 %collective-permute-done.1.second = bf16[3,512,128]{2,1,0:T(8,128)(2,1)S(1)} collective-permute-done((bf16[3,512,128]{2,1,0:T(8,128)(2,1)}, bf16[3,512,128]{2,1,0:T(8,128)(2,1)S(1)}, u32[]{:S(2)}, u32[]{:S(2)}) %collective-permute-start.1) | collective-permute-done | bytes 393248 | tf_op jit(solution)/shard_map/ppermute | solution.py:367
  83.2 2.3 %collective-permute-done.2.third = bf16[3,512,128]{2,1,0:T(8,128)(2,1)} collective-permute-done((bf16[3,512,128]{2,1,0:T(8,128)(2,1)}, bf16[3,512,128]{2,1,0:T(8,128)(2,1)}, u32[]{:S(2)}, u32[]{:S(2)}) %collective-permute-start.2) | collective-permute-done | bytes 393248 | tf_op jit(solution)/shard_map/ppermute | solution.py:367
  85.6 1.6 %all-to-all-done.2.merged = bf16[8,64,384]{2,1,0:T(8,128)(2,1)S(1)} async-done(((bf16[8,64,384]{2,1,0:T(8,128)(2,1)}), bf16[8,64,384]{2,1,0:T(8,128)(2,1)S(1)}, u32[]{:S(2)}, u32[]{:S(2)}) %all-to-all-start.2) | async-done | bytes 393248 | tf_op jit(solution)/shard_map/all_to_all | solution.py:280
  87.2 2.4 %grads.3 = bf16[512,512]{1,0:T(8,128)(2,1)S(1)} custom-call(s32[2]{0:T(128)S(1)} %copy-done.18, bf16[3,512,128]{2,1,0:T(8,128)(2,1)S(1)} %copy-done.7, bf16[3,512,128]{2,1,0:T(8,128)(2,1)S(1)} %collective-permute-done.first, bf16[3,512,128]{2,1,0:T(8,128)(2,1)S(1)} %collective-permute-done.1.second, bf16[3,512,128]{2,1,0:T(8,128)(2,1)} %collective-permute-done.2.third, ...), custom_call_target="tpu_custom_call" | custom-call | flops 1000000 | bytes 2000000 | tf_op jit(solution)/shard_map/grads/pallas_call | solution.py:268
  89.6 19.8 %all_to_all.30.parts = bf16[16,32,512]{2,1,0:T(8,128)(2,1)S(1)} all-to-all(bf16[16,32,512]{2,1,0:T(8,128)(2,1)S(1)} %bitcast.4), channel_id=1, replica_groups=mesh['y'=8,'zl'=2,'x'=4,'zh'=4,'c'=2] {'zl','y'}, dimensions={0} | all-to-all | bytes 1048576 | tf_op jit(solution)/shard_map/all_to_all | solution.py:395
  109.5 13.6 %all_to_all.31 = bf16[8,32,512]{2,1,0:T(8,128)(2,1)S(1)} all-to-all(bf16[8,32,512]{2,1,0:T(8,128)(2,1)S(1)} %total.1), channel_id=1, replica_groups=mesh['y'=8,'zl'=2,'x'=4,'zh'=4,'c'=2] {'y'}, dimensions={0} | all-to-all | bytes 524288 | tf_op jit(solution)/shard_map/all_to_all | solution.py:399
  123.3 29.8 %all_to_all.32.parts = bf16[8,256,512]{2,1,0:T(8,128)(2,1)S(1)} all-to-all(bf16[8,256,512]{2,1,0:T(8,128)(2,1)S(1)} %broadcast_in_dim.22), channel_id=1, replica_groups=mesh['y'=8,'zl'=2,'x'=4,'zh'=4,'c'=2] {'zl','x'}, dimensions={0} | all-to-all | bytes 4194304 | tf_op jit(solution)/shard_map/all_to_all | solution.py:280
  153.1 3.4 %final.1 = (f32[2048,384]{1,0:T(8,128)}, f32[128,2048]{1,0:T(8,128)}) custom-call(bf16[8,256,512]{2,1,0:T(8,128)(2,1)S(1)} %all_to_all.32.parts), custom_call_target="tpu_custom_call" | custom-call | tf_op jit(solution)/shard_map/final/pallas_call | solution.py:402
  (51 shorter events, 13.3 us)
Async XLA Ops:
  0.6 17.6 %copy-start = (bf16[2048,384]{1,0:T(8,128)(2,1)S(1)}, bf16[2048,384]{1,0:T(8,128)(2,1)}, u32[]{:S(2)}) copy-start(bf16[2048,384]{1,0:T(8,128)(2,1)} %merge_down.1) | copy-start | bytes 4718596
  0.6 1.3 copy-start.1
  1.9 1.0 copy-start.2
  2.9 15.3 %copy-start.3 = (bf16[128,2048]{1,0:T(8,128)(2,1)S(1)}, bf16[128,2048]{1,0:T(8,128)(2,1)}, u32[]{:S(2)}) copy-start(bf16[128,2048]{1,0:T(8,128)(2,1)} %queries.1) | copy-start | bytes 1572868
  2.9 15.3 %copy-start.4 = (bf16[128,2048]{1,0:T(8,128)(2,1)S(1)}, bf16[128,2048]{1,0:T(8,128)(2,1)}, u32[]{:S(2)}) copy-start(bf16[128,2048]{1,0:T(8,128)(2,1)} %low.1) | copy-start | bytes 1572868
  2.9 15.3 %copy-start.15 = (bf16[3,2048]{1,0:T(4,128)(2,1)S(1)}, bf16[3,2048]{1,0:T(4,128)(2,1)}, u32[]{:S(2)}) copy-start(bf16[3,2048]{1,0:T(4,128)(2,1)} %gains.1) | copy-start | bytes 36868
  4.4 37.2 %all-to-all-start = ((bf16[64,56,128]{2,1,0:T(8,128)(2,1)}), bf16[64,56,128]{2,1,0:T(8,128)(2,1)S(1)}, u32[]{:S(2)}, u32[]{:S(2)}) async-start(bf16[64,56,128]{2,1,0:T(8,128)(2,1)} %pack.1), calls=%async_computation | async-start | bytes 1835008 | tf_op jit(solution)/shard_map/all_to_all | solution.py:320
  18.2 1.0 copy-start.5
  19.3 0.9 copy-start.8
  20.2 0.9 copy-start.9
  21.2 0.8 copy-start.13
  21.9 0.8 copy-start.14
  32.6 0.8 copy-start.6
  33.4 0.7 copy-start.11
  41.6 0.8 copy-start.10
  42.4 0.9 copy-start.12
  45.1 3.3 %collective-permute-start.3 = (f32[64,640]{1,0:T(8,128)S(1)}, f32[64,640]{1,0:T(8,128)S(1)}, u32[]{:S(2)}, u32[]{:S(2)}) collective-permute-start(f32[64,640]{1,0:T(8,128)S(1)} %get-tuple-element.16), channel_id=1, source_target_pairs={{0,1},{1,0},{2,3},{3,2},{4,5},{5,4},{6,7},{7,6},{8,9},{9,8},{10,11... | collective-permute-start | bytes 491528 | tf_op jit(solution)/shard_map/ppermute | solution.py:379
  49.3 37.9 %copy-start.7 = (bf16[3,512,128]{2,1,0:T(8,128)(2,1)S(1)}, bf16[3,512,128]{2,1,0:T(8,128)(2,1)}, u32[]{:S(2)}) copy-start(bf16[3,512,128]{2,1,0:T(8,128)(2,1)} %copy-done.6) | copy-start | bytes 1179652
  49.3 37.9 %copy-start.18 = (s32[2]{0:T(128)S(1)}, s32[2]{0:T(128)}, u32[]{:S(2)}) copy-start(s32[2]{0:T(128)} %copy-done.16) | copy-start | bytes 28
  49.3 22.2 %all-to-all-start.1 = ((bf16[4,64,640]{2,1,0:T(8,128)(2,1)}), bf16[4,64,640]{2,1,0:T(8,128)(2,1)S(1)}, u32[]{:S(2)}, u32[]{:S(2)}) async-start(bf16[4,64,640]{2,1,0:T(8,128)(2,1)} %broadcast_in_dim.8), calls=%async_computation.1 | async-start | bytes 655360 | tf_op jit(solution)/shard_map/all_to_all | solution.py:280
  58.9 17.5 %collective-permute-start = (bf16[3,512,128]{2,1,0:T(8,128)(2,1)}, bf16[3,512,128]{2,1,0:T(8,128)(2,1)S(1)}, u32[]{:S(2)}, u32[]{:S(2)}) collective-permute-start(bf16[3,512,128]{2,1,0:T(8,128)(2,1)} %get-tuple-element.11), channel_id=1, source_target_pairs={{0,8},{8,16},{16,24},{24,0},{1,9},{9,17},{17,25},{25,1},{2,10},{10... | collective-permute-start | bytes 1179656 | tf_op jit(solution)/shard_map/ppermute | solution.py:367
  62.1 21.1 %collective-permute-start.1 = (bf16[3,512,128]{2,1,0:T(8,128)(2,1)}, bf16[3,512,128]{2,1,0:T(8,128)(2,1)S(1)}, u32[]{:S(2)}, u32[]{:S(2)}) collective-permute-start(bf16[3,512,128]{2,1,0:T(8,128)(2,1)} %get-tuple-element.12), channel_id=1, source_target_pairs={{0,16},{8,24},{16,0},{24,8},{1,17},{9,25},{17,1},{25,9},{2,18},{10... | collective-permute-start | bytes 1179656 | tf_op jit(solution)/shard_map/ppermute | solution.py:367
  66.6 19.0 %collective-permute-start.2 = (bf16[3,512,128]{2,1,0:T(8,128)(2,1)}, bf16[3,512,128]{2,1,0:T(8,128)(2,1)}, u32[]{:S(2)}, u32[]{:S(2)}) collective-permute-start(bf16[3,512,128]{2,1,0:T(8,128)(2,1)} %get-tuple-element.13), channel_id=1, source_target_pairs={{0,24},{8,0},{16,8},{24,16},{1,25},{9,1},{17,9},{25,17},{2,26},{10... | collective-permute-start | bytes 1179656 | tf_op jit(solution)/shard_map/ppermute | solution.py:367
  72.6 14.6 %all-to-all-start.2 = ((bf16[8,64,384]{2,1,0:T(8,128)(2,1)}), bf16[8,64,384]{2,1,0:T(8,128)(2,1)S(1)}, u32[]{:S(2)}, u32[]{:S(2)}) async-start(bf16[8,64,384]{2,1,0:T(8,128)(2,1)} %broadcast_in_dim.9), calls=%async_computation.2 | async-start | bytes 786432 | tf_op jit(solution)/shard_map/all_to_all | solution.py:280
  (5 other events, 3.1 us)

commit v3 on v2

--- a/solution.py
+++ b/solution.py
@@ -12,15 +12,16 @@
 RANK = 128
 MOST = 3
 NX = 4
+PEERS = 64
 EPSILON = 1e-05
 MASKED = -1e30
 BF = jnp.bfloat16
 F32 = jnp.float32
-VMEM_LIMIT = 48 * 1024 * 1024
-
-
-def params():
-    return pltpu.CompilerParams(vmem_limit_bytes=VMEM_LIMIT)
+MIB = 1024 * 1024
+
+
+def params(limit=32):
+    return pltpu.CompilerParams(vmem_limit_bytes=limit * MIB)
 
 
 def iota(shape, dim):
@@ -43,6 +44,7 @@
     place,
     lengths,
     counts,
+    targets,
     parents,
     queries,
     tree_keys,
@@ -121,7 +123,15 @@
                 chunk = (place[0] + k) % (width // block)
                 chunk = pl.ds(pl.multiple_of(chunk * block, block), block)
                 out[layer] = rows[layer, :, chunk].T
-        partial[:, 3 * RANK :] = squares[...]
+        target = targets[...]
+        named = (target == iota((count, PEERS), 1)).astype(F32)
+        earlier = (iota((count, count), 0) > iota((count, count), 1)).astype(BF)
+        rank = jnp.sum(dot(earlier, named.astype(BF)) * named, axis=1, keepdims=True)
+        notes = squares[...]
+        lane = iota((count, RANK), 1)
+        for i, note in ((6, target.astype(F32)), (7, rank), (8, place[1].astype(F32))):
+            notes = jnp.where(lane == i, note, notes)
+        partial[:, 3 * RANK :] = notes
 
 
 def pack_kernel(grads, merge_up, out, rows):
@@ -155,29 +165,24 @@
     out[...] = rows[...].astype(BF)
 
 
-def pick_kernel(place, targets, received, partial, keep, give, info, rows, notes):
-    count = rows.shape[0]
+def pick_kernel(received, partial, keep, give, info):
+    count = partial.shape[0]
     half = keep.shape[0]
     peers = received.shape[0]
     tail = received[:, received.shape[1] - 8 :, :].astype(F32).reshape(peers * 8, RANK).astype(BF)
-    target = targets[...]
-    named = (target == iota((count, peers), 1)).astype(F32)
-    earlier = (iota((count, count), 0) > iota((count, count), 1)).astype(BF)
-    before = dot(earlier, named.astype(BF))
-    rank = jnp.sum(before * named, axis=1, keepdims=True)
-    chosen = target * 8 + rank.astype(jnp.int32) == iota((count, peers * 8), 1)
-    rows[:, : 3 * RANK] = partial[:, : 3 * RANK]
-    rows[:, 3 * RANK : 4 * RANK] = dot(chosen.astype(BF), tail)
-    rows[:, 4 * RANK :] = partial[:, 3 * RANK :]
-    lane = iota((count, RANK), 1)
-    notes[...] = jnp.where(lane == 6, target.astype(F32), jnp.where(lane == 7, rank, 0.0))
-    mine = pl.ds(pl.multiple_of(place[1] * half, half), half)
-    keep[...] = rows[mine, :]
-    info[...] = notes[mine, :]
-    give[...] = rows[pl.ds(pl.multiple_of((1 - place[1]) * half, half), half), :]
-
-
-def pair_kernel(keep, got, out):
+    notes = partial[:, 3 * RANK :]
+    place = (notes[:, 6:7] * 8.0 + notes[:, 7:8]).astype(jnp.int32)
+    chosen = place == iota((count, peers * 8), 1)
+    back = dot(chosen.astype(BF), tail)
+    upper = notes[:half, 8:9] > 0.5
+    for source, start in ((partial[:, : 3 * RANK], 0), (back, 3 * RANK), (notes, 4 * RANK)):
+        columns = slice(start, start + source.shape[1])
+        keep[:, columns] = jnp.where(upper, source[half:], source[:half])
+        give[:, columns] = jnp.where(upper, source[:half], source[half:])
+    info[...] = jnp.where(upper, notes[half:], notes[:half])
+
+
+def pair_kernel(keep, got, first, second, third, out):
     total = keep[...] + got[...]
     squares = total[:, 4 * RANK :]
     rough = squares.astype(BF).astype(F32)
@@ -185,8 +190,10 @@
     for i in range(3):
         rest = squares[:, i : i + 1] - rough[:, i : i + 1]
         rough = jnp.where(lane == 3 + i, rest, rough)
-    out[:, : 4 * RANK] = total[:, : 4 * RANK].astype(BF)
-    out[:, 4 * RANK :] = rough.astype(BF)
+    rough = jnp.where(lane < 6, rough, 0.0)
+    for peer in range(out.shape[0]):
+        out[peer, :, : 4 * RANK] = total[:, : 4 * RANK].astype(BF)
+        out[peer, :, 4 * RANK :] = rough.astype(BF)
 
 
 def merge_kernel(parts, info, out):
@@ -203,15 +210,19 @@
         mixed = mixed + inverse[i] * total[:, i * RANK : (i + 1) * RANK]
     back = total[:, 3 * RANK : 4 * RANK]
     gate = 1.0 / (1.0 + jnp.exp(-mixed))
-    out[:, :RANK] = (back * gate * (1.0 + mixed * (1.0 - gate))).astype(BF)
-    out[:, RANK : 2 * RANK] = (mixed * gate).astype(BF)
+    grad = (back * gate * (1.0 + mixed * (1.0 - gate))).astype(BF)
+    active = (mixed * gate).astype(BF)
     notes = info[...]
     lane = iota(notes.shape, 1)
     for i in range(3):
         rough = inverse[i].astype(BF).astype(F32)
         notes = jnp.where(lane == i, rough, notes)
         notes = jnp.where(lane == 3 + i, inverse[i] - rough, notes)
-    out[:, 2 * RANK :] = notes.astype(BF)
+    notes = notes.astype(BF)
+    for peer in range(out.shape[0]):
+        out[peer, :, :RANK] = grad
+        out[peer, :, RANK : 2 * RANK] = active
+        out[peer, :, 2 * RANK :] = notes
 
 
 def grads_kernel(place, own, first, second, third, slots, merged, out):
@@ -262,22 +273,25 @@
     return jax.ShapeDtypeStruct(dims, kind)
 
 
-def call(kernel, name, out_shape, *args, scratch=(), flops=1_000_000):
+def call(kernel, name, out_shape, *args, unread=(), scratch=(), grid=(), limit=32):
     smem = pl.BlockSpec(memory_space=pltpu.SMEM)
-    vmem = pl.BlockSpec(memory_space=pltpu.VMEM)
+    specs = [smem if a.ndim == 1 else whole(a.shape) for a in args]
+    specs = specs + [pl.BlockSpec(memory_space=pl.ANY) for _ in unread]
+    outs = out_shape if isinstance(out_shape, list) else [out_shape]
+    outs = [whole(o.shape) for o in outs]
     return pl.pallas_call(
         kernel,
-        in_specs=[smem if a.ndim == 1 else vmem for a in args],
+        grid=grid,
+        in_specs=specs,
+        out_specs=outs if isinstance(out_shape, list) else outs[0],
         out_shape=out_shape,
         scratch_shapes=[pltpu.VMEM(*s) for s in scratch],
-        compiler_params=params(),
-        cost_estimate=pl.CostEstimate(flops=flops, bytes_accessed=2_000_000, transcendentals=0),
+        compiler_params=params(limit),
+        cost_estimate=pl.CostEstimate(
+            flops=1_000_000, bytes_accessed=2_000_000, transcendentals=0
+        ),
         name=name,
-    )(*args)
-
-
-def spread(array, n, axes):
-    return lax.all_to_all(jnp.broadcast_to(array[None], (n, *array.shape)), axes, 0, 0, tiled=True)
+    )(*args, *unread)
 
 
 def body(
@@ -299,9 +313,9 @@
 ):
     count, width = low_hidden.shape
     branches = parents.shape[0]
-    ny, nzl, nc = lax.axis_size("y"), lax.axis_size("zl"), lax.axis_size("c")
-    nzh = lax.axis_size("zh")
-    peers = ny * nzl * NX
+    nyh, nyl, nzl = lax.axis_size("yh"), lax.axis_size("yl"), lax.axis_size("zl")
+    nzh, nc = lax.axis_size("zh"), lax.axis_size("c")
+    peers = nyh * nyl * nzl * NX
     block = width // NX
     place = jnp.stack([lax.axis_index("x"), lax.axis_index("c")]).astype(jnp.int32)
     smem = pl.BlockSpec(memory_space=pltpu.SMEM)
@@ -316,8 +330,10 @@
         out_grad,
         merge_up,
         scratch=[((peers, height, RANK), F32)],
-    )
-    received = lax.all_to_all(packed, ("y", "zl", "x"), 0, 0, tiled=True)
+        grid=(1,),
+        limit=60,
+    )
+    received = lax.all_to_all(packed, ("yh", "yl", "zl", "x"), 0, 0, tiled=True)
     *turned, partial = pl.pallas_call(
         feature_kernel,
         grid=(branches,),
@@ -325,6 +341,7 @@
             smem,
             smem,
             smem,
+            whole((count, 1)),
             whole((branches, TREE)),
             row_block,
             whole((count, HEAD_DIM)),
@@ -343,7 +360,7 @@
             pltpu.VMEM((3, count, width), BF),
             pltpu.VMEM((count, RANK), F32),
         ],
-        compiler_params=params(),
+        compiler_params=params(60),
         cost_estimate=pl.CostEstimate(
             flops=400_000_000, bytes_accessed=8_000_000, transcendentals=600_000
         ),
@@ -352,6 +369,7 @@
         place,
         cache_lengths,
         accepted_counts,
+        dest_map,
         parents,
         queries,
         tree_keys,
@@ -370,17 +388,16 @@
         pick_kernel,
         "pick",
         [shape((half, 5 * RANK), F32), shape((half, 5 * RANK), F32), shape((half, RANK), F32)],
-        place,
-        dest_map,
         received,
         partial,
-        scratch=[((count, 5 * RANK), F32), ((count, RANK), F32)],
     )
     got = lax.ppermute(give, "c", [(i, 1 - i) for i in range(nc)])
-    paired = call(pair_kernel, "pair", shape((half, 5 * RANK)), keep, got)
-    parts = spread(paired, nzh, "zh")
-    merged = call(merge_kernel, "merge", shape((half, 3 * RANK)), parts, info)
-    merged = spread(merged, NX * nc, ("x", "c"))
+    parts = call(
+        pair_kernel, "pair", shape((nzh, half, 5 * RANK)), keep, got, unread=turned[1:]
+    )
+    parts = lax.all_to_all(parts, "zh", 0, 0, tiled=True)
+    merged = call(merge_kernel, "merge", shape((NX * nc, half, 3 * RANK)), parts, info)
+    merged = lax.all_to_all(merged, ("x", "c"), 0, 0, tiled=True)
     slots = call(
         unpack_kernel,
         "unpack",
@@ -391,18 +408,20 @@
     grads = call(
         grads_kernel, "grads", shape((block, 4 * RANK)), place, *turned, slots, merged
     )
-    piece = block // (nzl * ny)
+    piece = block // (nzl * nyl * nyh)
     grads = lax.all_to_all(
-        grads.reshape(nzl * ny, piece, 4 * RANK), ("zl", "y"), 0, 0, tiled=True
-    )
-    grads = call(sum_kernel, "total", shape((ny, piece, 4 * RANK)), grads)
-    grads = lax.all_to_all(grads, "y", 0, 0, tiled=True).reshape(ny * piece, 4 * RANK)
-    grads = spread(grads, nzl * NX, ("zl", "x"))
-    rows = ny * piece
+        grads.reshape(nzl * nyl * nyh, piece, 4 * RANK), ("zl", "yl", "yh"), 0, 0, tiled=True
+    )
+    grads = call(sum_kernel, "total", shape((nyh, piece, 4 * RANK)), grads)
+    rows = nyh * piece
+    grads = lax.all_to_all(grads, "yh", 0, 0, tiled=True).reshape(rows, 4 * RANK)
+    near = nzl * nyl
+    grads = jnp.broadcast_to(grads[None], (near * NX, rows, 4 * RANK))
+    grads = lax.all_to_all(grads, ("zl", "yl", "x"), 0, 0, tiled=True)
     return pl.pallas_call(
         final_kernel,
-        grid=(nzl * NX,),
-        in_specs=[pl.BlockSpec((1, rows, 4 * RANK), lambda i: (i % nzl * NX + i // nzl, 0, 0))],
+        grid=(near * NX,),
+        in_specs=[pl.BlockSpec((1, rows, 4 * RANK), lambda i: (i % near * NX + i // near, 0, 0))],
         out_specs=[
             pl.BlockSpec((rows, 3 * RANK), lambda i: (i, 0)),
             pl.BlockSpec((RANK, rows), lambda i: (0, i)),
@@ -414,8 +433,8 @@
 
 
 def solution(mesh):
-    fine = Mesh(mesh.devices.reshape(8, 2, NX, 4, 2), ("y", "zl", "x", "zh", "c"))
-    dp, head = ("y", "zl", "x"), ("zh", "c")
+    fine = Mesh(mesh.devices.reshape(4, 2, 2, NX, 4, 2), ("yh", "yl", "zl", "x", "zh", "c"))
+    dp, head = ("yh", "yl", "zl", "x"), ("zh", "c")
     placed = (
         P(dp, head),
         P(dp, head),

time: 158 us -> 162 us (1.025)
  the two profiles are of different devices: /device:TPU:8 before, /device:TPU:2 now
where the time goes in v3:
time: 162 us; the launch traced here: 161 us
  blocking collectives  85.7 us (53%)
  starting transfers between devices  28.3 us (17%)
  Pallas kernels  22.6 us (14%)
  waiting for transfers between devices  20.5 us (13%)
  local copies, waits for them, and re-layouts  2.88 us (2%)
    all_to_all x1, blocking collectives, body(): grads = lax.all_to_all(grads, ('zl', 'yl', 'x'), 0, 0, tiled=True)  29.9 us
    all_to_all x1, blocking collectives, body(): parts = lax.all_to_all(parts, 'zh', 0, 0, tiled=True)  22.4 us
    all_to_all x1, blocking collectives, body(): lax.all_to_all(grads.reshape(nzl * nyl * nyh, piece, 4 * RANK), ('zl', 'y...  21.6 us
    all_to_all x1, starting transfers between devices, body(): received = lax.all_to_all(packed, ('yh', 'yl', 'zl', 'x'), 0, 0, tiled=True)  12.5 us
    all_to_all x1, blocking collectives, body(): lax.all_to_all(grads, 'yh', 0, 0, tiled=True).reshape(rows, 4 * RANK)  11.8 us
    pallas_call x1, Pallas kernels, body(): pl.pallas_call(feature_kernel, grid=(branches,), in_specs=[smem, smem, sm...  10.5 us
    ppermute x3, waiting for transfers between devices, body(): lax.ppermute(turned[k], 'x', [(i, (i + k) % NX) for i in range(NX)])  10.4 us
    ppermute x3, starting transfers between devices, body(): lax.ppermute(turned[k], 'x', [(i, (i + k) % NX) for i in range(NX)])  10.4 us
  transfers between devices with their start and end apart: 6, of which 4 were waited for; matrix products, arithmetic and copies ran while one was open for 1% of the time, Pallas kernels for 7%

profile of v3, /device:TPU:2, one launch (start us, length us, event | category | flops | bytes accessed | tf_op | source)
XLA Modules:
  0.0 161.4 jit_solution(11379414118489078929)
XLA Ops:
  0.6 2.7 %pack.1 = bf16[64,56,128]{2,1,0:T(8,128)(2,1)} custom-call(bf16[192,2048]{1,0:T(8,128)(2,1)} %grads.2, bf16[128,2048]{1,0:T(8,128)(2,1)} %merge_up.1), custom_call_target="tpu_custom_call" | custom-call | flops 1000000 | bytes 2000000 | tf_op jit(solution)/shard_map/pack/pallas_call | solution.py:282
  3.3 12.5 %all-to-all-start = ((bf16[64,56,128]{2,1,0:T(8,128)(2,1)}), bf16[64,56,128]{2,1,0:T(8,128)(2,1)S(1)}, u32[]{:S(2)}, u32[]{:S(2)}) async-start(bf16[64,56,128]{2,1,0:T(8,128)(2,1)} %pack.1), calls=%async_computation | async-start | bytes 1835008 | tf_op jit(solution)/shard_map/all_to_all | solution.py:336
  15.8 0.7 copy.17.targets
  16.6 0.6 pad_add_fusion.place
  17.2 10.5 %features.1 = (bf16[3,512,128]{2,1,0:T(8,128)(2,1)}, bf16[3,512,128]{2,1,0:T(8,128)(2,1)}, bf16[3,512,128]{2,1,0:T(8,128)(2,1)}, bf16[3,512,128]{2,1,0:T(8,128)(2,1)}, f32[128,512]{1,0:T(8,128)}) custom-call(s32[2]{0:T(128)} %pad_add_fusion.place, s32[8]{0:T(128)} %lengths.1, s32[8]{0:T(128)} %counts.1, s32[128,1]{1,0:T(8,128)} %copy.17.targets, ...), custom_call_target="tpu_custom_call" | custom-call | flops 400000000 | bytes 8000000 | tf_op jit(solution)/shard_map/features/pallas_call | solution.py:337
  27.7 3.4 %collective-permute-start = (bf16[3,512,128]{2,1,0:T(8,128)(2,1)}, bf16[3,512,128]{2,1,0:T(8,128)(2,1)S(1)}, u32[]{:S(2)}, u32[]{:S(2)}) collective-permute-start(bf16[3,512,128]{2,1,0:T(8,128)(2,1)} %get-tuple-element.11), channel_id=1, source_target_pairs={{0,8},{8,16},{16,24},{24,0},{1,9},{9,17},{17,25},{25,1},{2,10},{10... | collective-permute-start | bytes 1179656 | tf_op jit(solution)/shard_map/ppermute | solution.py:385
  31.0 3.0 %collective-permute-start.1 = (bf16[3,512,128]{2,1,0:T(8,128)(2,1)}, bf16[3,512,128]{2,1,0:T(8,128)(2,1)S(1)}, u32[]{:S(2)}, u32[]{:S(2)}) collective-permute-start(bf16[3,512,128]{2,1,0:T(8,128)(2,1)} %get-tuple-element.12), channel_id=1, source_target_pairs={{0,16},{8,24},{16,0},{24,8},{1,17},{9,25},{17,1},{25,9},{2,18},{10... | collective-permute-start | bytes 1179656 | tf_op jit(solution)/shard_map/ppermute | solution.py:385
  34.0 4.1 %collective-permute-start.2 = (bf16[3,512,128]{2,1,0:T(8,128)(2,1)}, bf16[3,512,128]{2,1,0:T(8,128)(2,1)S(1)}, u32[]{:S(2)}, u32[]{:S(2)}) collective-permute-start(bf16[3,512,128]{2,1,0:T(8,128)(2,1)} %get-tuple-element.13), channel_id=1, source_target_pairs={{0,24},{8,0},{16,8},{24,16},{1,25},{9,1},{17,9},{25,17},{2,26},{10... | collective-permute-start | bytes 1179656 | tf_op jit(solution)/shard_map/ppermute | solution.py:385
  38.1 2.8 %all-to-all-done.received = bf16[64,56,128]{2,1,0:T(8,128)(2,1)S(1)} async-done(((bf16[64,56,128]{2,1,0:T(8,128)(2,1)}), bf16[64,56,128]{2,1,0:T(8,128)(2,1)S(1)}, u32[]{:S(2)}, u32[]{:S(2)}) %all-to-all-start) | async-done | bytes 917536 | tf_op jit(solution)/shard_map/all_to_all | solution.py:336
  40.9 0.9 copy-done.1
  41.9 0.3 pick.1
  42.2 1.9 %collective-permute-start.3 = (f32[64,640]{1,0:T(8,128)S(1)}, f32[64,640]{1,0:T(8,128)S(1)}, u32[]{:S(2)}, u32[]{:S(2)}) collective-permute-start(f32[64,640]{1,0:T(8,128)S(1)} %get-tuple-element.16), channel_id=1, source_target_pairs={{0,1},{1,0},{2,3},{3,2},{4,5},{5,4},{6,7},{7,6},{8,9},{9,8},{10,11... | collective-permute-start | bytes 491528 | tf_op jit(solution)/shard_map/ppermute | solution.py:394
  44.1 3.3 %collective-permute-done.1.second = bf16[3,512,128]{2,1,0:T(8,128)(2,1)S(1)} collective-permute-done((bf16[3,512,128]{2,1,0:T(8,128)(2,1)}, bf16[3,512,128]{2,1,0:T(8,128)(2,1)S(1)}, u32[]{:S(2)}, u32[]{:S(2)}) %collective-permute-start.1) | collective-permute-done | bytes 393248 | tf_op jit(solution)/shard_map/ppermute | solution.py:385
  47.4 7.2 %collective-permute-done.2.third = bf16[3,512,128]{2,1,0:T(8,128)(2,1)S(1)} collective-permute-done((bf16[3,512,128]{2,1,0:T(8,128)(2,1)}, bf16[3,512,128]{2,1,0:T(8,128)(2,1)S(1)}, u32[]{:S(2)}, u32[]{:S(2)}) %collective-permute-start.2) | collective-permute-done | bytes 393248 | tf_op jit(solution)/shard_map/ppermute | solution.py:385
  54.8 22.4 %all_to_all.30.parts = bf16[4,64,640]{2,1,0:T(8,128)(2,1)S(1)} all-to-all(bf16[4,64,640]{2,1,0:T(8,128)(2,1)S(1)} %pair.1), channel_id=1, replica_groups=mesh['yh'=4,'yl'=2,'zl'=2,'x'=4,'zh'=4,'c'=2] {'zh'}, dimensions={0} | all-to-all | bytes 655360 | tf_op jit(solution)/shard_map/all_to_all | solution.py:398
  77.2 1.0 merge.1
  78.2 3.5 %all-to-all-start.2 = ((bf16[8,64,384]{2,1,0:T(8,128)(2,1)}), bf16[8,64,384]{2,1,0:T(8,128)(2,1)S(1)}, u32[]{:S(2)}, u32[]{:S(2)}) async-start(bf16[8,64,384]{2,1,0:T(8,128)(2,1)} %merge.1), calls=%async_computation.2 | async-start | bytes 786432 | tf_op jit(solution)/shard_map/all_to_all | solution.py:400
  81.9 7.3 %all-to-all-done.2.merged = bf16[8,64,384]{2,1,0:T(8,128)(2,1)S(1)} async-done(((bf16[8,64,384]{2,1,0:T(8,128)(2,1)}), bf16[8,64,384]{2,1,0:T(8,128)(2,1)S(1)}, u32[]{:S(2)}, u32[]{:S(2)}) %all-to-all-start.2) | async-done | bytes 393248 | tf_op jit(solution)/shard_map/all_to_all | solution.py:400
  89.2 1.0 copy-done
  90.2 1.9 %grads.3 = bf16[512,512]{1,0:T(8,128)(2,1)S(1)} custom-call(s32[2]{0:T(128)S(1)} %copy-done.2, bf16[3,512,128]{2,1,0:T(8,128)(2,1)S(1)} %copy-done, bf16[3,512,128]{2,1,0:T(8,128)(2,1)S(1)} %collective-permute-done.first, bf16[3,512,128]{2,1,0:T(8,128)(2,1)S(1)} %collective-permute-done.1.second, bf16[3,512,128]{2,1,0:T(8,128)(2,1)S(1)} %collective-permute-done.2.third, ...), custom_call_target="tpu_custom_call" | custom-call | flops 1000000 | bytes 2000000 | tf_op jit(solution)/shard_map/grads/pallas_call | solution.py:282
  92.1 21.6 %all_to_all.31.parts = bf16[16,32,512]{2,1,0:T(8,128)(2,1)S(1)} all-to-all(bf16[16,32,512]{2,1,0:T(8,128)(2,1)S(1)} %bitcast.4), channel_id=1, replica_groups=mesh['yh'=4,'yl'=2,'zl'=2,'x'=4,'zh'=4,'c'=2] {'zl','yl','yh'}, dimensions={0} | all-to-all | bytes 1048576 | tf_op jit(solution)/shard_map/all_to_all | solution.py:412
  113.8 11.8 %all_to_all.32 = bf16[4,32,512]{2,1,0:T(8,128)(2,1)S(1)} all-to-all(bf16[4,32,512]{2,1,0:T(8,128)(2,1)S(1)} %total.1), channel_id=1, replica_groups=mesh['yh'=4,'yl'=2,'zl'=2,'x'=4,'zh'=4,'c'=2] {'yh'}, dimensions={0} | all-to-all | bytes 262144 | tf_op jit(solution)/shard_map/all_to_all | solution.py:417
  125.8 29.9 %all_to_all.33.parts = bf16[16,128,512]{2,1,0:T(8,128)(2,1)S(1)} all-to-all(bf16[16,128,512]{2,1,0:T(8,128)(2,1)S(1)} %broadcast_in_dim.8), channel_id=1, replica_groups=mesh['yh'=4,'yl'=2,'zl'=2,'x'=4,'zh'=4,'c'=2] {'zl','yl','x'}, dimensions={0} | all-to-all | bytes 4194304 | tf_op jit(solution)/shard_map/all_to_all | solution.py:420
  155.7 5.7 %final.1 = (f32[2048,384]{1,0:T(8,128)}, f32[128,2048]{1,0:T(8,128)}) custom-call(bf16[16,128,512]{2,1,0:T(8,128)(2,1)S(1)} %all_to_all.33.parts), custom_call_target="tpu_custom_call" | custom-call | tf_op jit(solution)/shard_map/final/pallas_call | solution.py:421
  (12 shorter events, 0.7 us)
Async XLA Ops:
  0.6 15.2 %copy-start.3 = (s32[128,1]{0,1:T(1,128)S(1)}, s32[128,1]{0,1:T(1,128)}, u32[]{:S(2)}) copy-start(s32[128,1]{0,1:T(1,128)} %param.23) | copy-start | bytes 1540
  3.3 37.6 %all-to-all-start = ((bf16[64,56,128]{2,1,0:T(8,128)(2,1)}), bf16[64,56,128]{2,1,0:T(8,128)(2,1)S(1)}, u32[]{:S(2)}, u32[]{:S(2)}) async-start(bf16[64,56,128]{2,1,0:T(8,128)(2,1)} %pack.1), calls=%async_computation | async-start | bytes 1835008 | tf_op jit(solution)/shard_map/all_to_all | solution.py:336
  27.7 16.4 %collective-permute-start = (bf16[3,512,128]{2,1,0:T(8,128)(2,1)}, bf16[3,512,128]{2,1,0:T(8,128)(2,1)S(1)}, u32[]{:S(2)}, u32[]{:S(2)}) collective-permute-start(bf16[3,512,128]{2,1,0:T(8,128)(2,1)} %get-tuple-element.11), channel_id=1, source_target_pairs={{0,8},{8,16},{16,24},{24,0},{1,9},{9,17},{17,25},{25,1},{2,10},{10... | collective-permute-start | bytes 1179656 | tf_op jit(solution)/shard_map/ppermute | solution.py:385
  31.0 16.3 %collective-permute-start.1 = (bf16[3,512,128]{2,1,0:T(8,128)(2,1)}, bf16[3,512,128]{2,1,0:T(8,128)(2,1)S(1)}, u32[]{:S(2)}, u32[]{:S(2)}) collective-permute-start(bf16[3,512,128]{2,1,0:T(8,128)(2,1)} %get-tuple-element.12), channel_id=1, source_target_pairs={{0,16},{8,24},{16,0},{24,8},{1,17},{9,25},{17,1},{25,9},{2,18},{10... | collective-permute-start | bytes 1179656 | tf_op jit(solution)/shard_map/ppermute | solution.py:385
  34.0 20.5 %collective-permute-start.2 = (bf16[3,512,128]{2,1,0:T(8,128)(2,1)}, bf16[3,512,128]{2,1,0:T(8,128)(2,1)S(1)}, u32[]{:S(2)}, u32[]{:S(2)}) collective-permute-start(bf16[3,512,128]{2,1,0:T(8,128)(2,1)} %get-tuple-element.13), channel_id=1, source_target_pairs={{0,24},{8,0},{16,8},{24,16},{1,25},{9,1},{17,9},{25,17},{2,26},{10... | collective-permute-start | bytes 1179656 | tf_op jit(solution)/shard_map/ppermute | solution.py:385
  40.9 1.0 copy-start.1
  42.2 12.4 %collective-permute-start.3 = (f32[64,640]{1,0:T(8,128)S(1)}, f32[64,640]{1,0:T(8,128)S(1)}, u32[]{:S(2)}, u32[]{:S(2)}) collective-permute-start(f32[64,640]{1,0:T(8,128)S(1)} %get-tuple-element.16), channel_id=1, source_target_pairs={{0,1},{1,0},{2,3},{3,2},{4,5},{5,4},{6,7},{7,6},{8,9},{9,8},{10,11... | collective-permute-start | bytes 491528 | tf_op jit(solution)/shard_map/ppermute | solution.py:394
  54.8 34.4 %copy-start.2 = (s32[2]{0:T(128)S(1)}, s32[2]{0:T(128)}, u32[]{:S(2)}) copy-start(s32[2]{0:T(128)} %pad_add_fusion.place) | copy-start | bytes 28
  78.2 11.0 %all-to-all-start.2 = ((bf16[8,64,384]{2,1,0:T(8,128)(2,1)}), bf16[8,64,384]{2,1,0:T(8,128)(2,1)S(1)}, u32[]{:S(2)}, u32[]{:S(2)}) async-start(bf16[8,64,384]{2,1,0:T(8,128)(2,1)} %merge.1), calls=%async_computation.2 | async-start | bytes 786432 | tf_op jit(solution)/shard_map/all_to_all | solution.py:400
  89.2 1.0 copy-start

commit v4 on v3

--- a/solution.py
+++ b/solution.py
@@ -63,13 +63,14 @@
     reach,
     rows,
     squares,
+    turned,
+    sent,
 ):
-    branch = pl.program_id(0)
-    branches = pl.num_programs(0)
+    together = cache_keys.shape[0]
     count, width = rows.shape[1], rows.shape[2]
     heads = width // HEAD_DIM
 
-    @pl.when(branch == 0)
+    @pl.when(pl.program_id(0) == 0)
     def _():
         groups = parents.shape[0]
         owner = (iota((count, groups), 0) // TREE == iota((count, groups), 1)).astype(F32)
@@ -84,45 +85,52 @@
             reached = jnp.minimum(dot(step, step), 1.0)
         reach[...] = reached
 
-    start = pl.multiple_of(branch * TREE, TREE)
-    here = pl.ds(start, TREE)
-    query = queries[...]
-    query = jnp.concatenate(
-        [query[:, h * HEAD_DIM : (h + 1) * HEAD_DIM] for h in range(heads)], axis=0
-    )
-    keys = jnp.concatenate([cache_keys[0], tree_keys[...]], axis=0)
-    values = jnp.concatenate([cache_values[0], tree_values[...]], axis=0)
-    scores = dot_nt(query, keys) * (HEAD_DIM**-0.5)
-    live = jnp.where(iota((TREE, CACHE), 1) < lengths[branch], 1.0, 0.0)
-    seen = jnp.concatenate([live, reach[here, :]], axis=1) > 0.5
-    scores = jnp.where(seen[None], scores.reshape(heads, TREE, CACHE + count), MASKED)
-    weights = jnp.exp(scores - jnp.max(scores, axis=2, keepdims=True))
-    probs = (weights / jnp.sum(weights, axis=2, keepdims=True)).astype(BF)
-    attended = dot(probs.reshape(heads * TREE, CACHE + count), values).astype(BF)
-    attended = jnp.concatenate(
-        [attended[h * TREE : (h + 1) * TREE, :] for h in range(heads)], axis=1
-    )
-    kept = iota((TREE, 1), 0) < counts[branch]
-    lane = iota((TREE, RANK), 1)
-    totals = jnp.zeros((TREE, RANK), F32)
-    for layer, feature in enumerate((low[...], mid[...], attended)):
-        feature = jnp.where(kept, feature.astype(F32), 0.0)
-        total = jnp.sum(feature * feature, axis=1, keepdims=True)
-        totals = totals + jnp.where(lane == layer, total, 0.0)
-        gain = gains[layer : layer + 1, :].astype(F32)
-        rows[layer, here, :] = (feature * gain).astype(BF)
-    squares[here, :] = totals
-
-    @pl.when(branch == branches - 1)
+    for j in range(together):
+        branch = pl.program_id(0) * together + j
+        start = pl.multiple_of(branch * TREE, TREE)
+        mine = slice(j * TREE, (j + 1) * TREE)
+        here = pl.ds(start, TREE)
+        query = queries[mine, :]
+        query = jnp.concatenate(
+            [query[:, h * HEAD_DIM : (h + 1) * HEAD_DIM] for h in range(heads)], axis=0
+        )
+        keys = jnp.concatenate([cache_keys[j], tree_keys[...]], axis=0)
+        values = jnp.concatenate([cache_values[j], tree_values[...]], axis=0)
+        scores = dot_nt(query, keys) * (HEAD_DIM**-0.5)
+        live = jnp.where(iota((TREE, CACHE), 1) < lengths[branch], 1.0, 0.0)
+        seen = jnp.concatenate([live, reach[here, :]], axis=1) > 0.5
+        scores = jnp.where(seen[None], scores.reshape(heads, TREE, CACHE + count), MASKED)
+        weights = jnp.exp(scores - jnp.max(scores, axis=2, keepdims=True))
+        probs = (weights / jnp.sum(weights, axis=2, keepdims=True)).astype(BF)
+        attended = dot(probs.reshape(heads * TREE, CACHE + count), values).astype(BF)
+        attended = jnp.concatenate(
+            [attended[h * TREE : (h + 1) * TREE, :] for h in range(heads)], axis=1
+        )
+        kept = iota((TREE, 1), 0) < counts[branch]
+        lane = iota((TREE, RANK), 1)
+        totals = jnp.zeros((TREE, RANK), F32)
+        for layer, feature in enumerate((low[mine, :], mid[mine, :], attended)):
+            feature = jnp.where(kept, feature.astype(F32), 0.0)
+            total = jnp.sum(feature * feature, axis=1, keepdims=True)
+            totals = totals + jnp.where(lane == layer, total, 0.0)
+            gain = gains[layer : layer + 1, :].astype(F32)
+            rows[layer, here, :] = (feature * gain).astype(BF)
+        squares[here, :] = totals
+
+    @pl.when(pl.program_id(0) == pl.num_programs(0) - 1)
     def _():
         block = own.shape[1]
+        copies = []
+        for k, out in enumerate((own, first, second, third)):
+            chunk = (place[0] + k) % (width // block)
+            chunk = pl.ds(pl.multiple_of(chunk * block, block), block)
+            for layer in range(3):
+                turned[k, layer] = rows[layer, :, chunk].T
+            copies.append(pltpu.make_async_copy(turned.at[k], out, sent.at[k]))
+            copies[k].start()
         for layer in range(3):
             columns = slice(layer * RANK, (layer + 1) * RANK)
             partial[:, columns] = dot(rows[layer], merge_down[:, columns])
-            for k, out in enumerate((own, first, second, third)):
-                chunk = (place[0] + k) % (width // block)
-                chunk = pl.ds(pl.multiple_of(chunk * block, block), block)
-                out[layer] = rows[layer, :, chunk].T
         target = targets[...]
         named = (target == iota((count, PEERS), 1)).astype(F32)
         earlier = (iota((count, count), 0) > iota((count, count), 1)).astype(BF)
@@ -132,15 +140,23 @@
         for i, note in ((6, target.astype(F32)), (7, rank), (8, place[1].astype(F32))):
             notes = jnp.where(lane == i, note, notes)
         partial[:, 3 * RANK :] = notes
-
-
-def pack_kernel(grads, merge_up, out, rows):
-    peers, height = out.shape[0], out.shape[1]
+        for copy in copies:
+            copy.wait()
+
+
+def products_kernel(grads, merge_up, out, rows):
+    products = dot_nt(grads[...], merge_up[...])
+    rows[...] = jnp.zeros_like(rows)
+    for d in range(out.shape[0]):
+        rows[d, :MOST, :] = products[d * MOST : (d + 1) * MOST, :]
+    out[...] = rows[...].astype(BF)
+
+
+def pack_kernel(grads, after, out, rows):
+    peers = out.shape[0]
     slots = grads.shape[0] // (peers // NX)
     blocks = grads.shape[1] // NX // RANK
     wide = grads[...].astype(F32)
-    products = dot_nt(grads[...], merge_up[...])
-    rows[:, blocks * slots :, :] = jnp.zeros((peers, height - blocks * slots, RANK), F32)
     for x in range(NX):
         for b in range(blocks):
             column = (x * blocks + b) * RANK
@@ -148,8 +164,6 @@
                 rows[g * NX + x, b * slots : (b + 1) * slots, :] = wide[
                     g * slots : (g + 1) * slots, column : column + RANK
                 ]
-    for d in range(peers):
-        rows[d, blocks * slots : blocks * slots + MOST, :] = products[d * MOST : (d + 1) * MOST, :]
     out[...] = rows[...].astype(BF)
 
 
@@ -169,7 +183,7 @@
     count = partial.shape[0]
     half = keep.shape[0]
     peers = received.shape[0]
-    tail = received[:, received.shape[1] - 8 :, :].astype(F32).reshape(peers * 8, RANK).astype(BF)
+    tail = received[...].astype(F32).reshape(peers * 8, RANK).astype(BF)
     notes = partial[:, 3 * RANK :]
     place = (notes[:, 6:7] * 8.0 + notes[:, 7:8]).astype(jnp.int32)
     chosen = place == iota((count, peers * 8), 1)
@@ -182,7 +196,7 @@
     info[...] = jnp.where(upper, notes[half:], notes[:half])
 
 
-def pair_kernel(keep, got, first, second, third, out):
+def pair_kernel(keep, got, first, out):
     total = keep[...] + got[...]
     squares = total[:, 4 * RANK :]
     rough = squares.astype(BF).astype(F32)
@@ -191,15 +205,14 @@
         rest = squares[:, i : i + 1] - rough[:, i : i + 1]
         rough = jnp.where(lane == 3 + i, rest, rough)
     rough = jnp.where(lane < 6, rough, 0.0)
-    for peer in range(out.shape[0]):
-        out[peer, :, : 4 * RANK] = total[:, : 4 * RANK].astype(BF)
-        out[peer, :, 4 * RANK :] = rough.astype(BF)
-
-
-def merge_kernel(parts, info, out):
-    total = parts[0].astype(F32)
-    for peer in range(1, parts.shape[0]):
-        total = total + parts[peer].astype(F32)
+    out[:, : 4 * RANK] = total[:, : 4 * RANK].astype(BF)
+    out[:, 4 * RANK :] = rough.astype(BF)
+
+
+def merge_kernel(own, near, far, last, info, second, third, out):
+    total = own[...].astype(F32)
+    for part in (near, far, last):
+        total = total + part[...].astype(F32)
     squares = total[:, 4 * RANK :]
     inverse = [
         lax.rsqrt((squares[:, i : i + 1] + squares[:, 3 + i : 4 + i]) / MODEL_WIDTH + EPSILON)
@@ -259,10 +272,10 @@
 
 
 def final_kernel(parts, down, up):
-    down[...] = parts[0, :, : 3 * RANK].astype(F32)
     for b in range(up.shape[1] // RANK):
-        columns = slice(b * RANK, (b + 1) * RANK)
-        up[:, columns] = parts[0, columns, 3 * RANK :].astype(F32)
+        rows = slice(b * RANK, (b + 1) * RANK)
+        down[rows, :] = parts[0, b, 0, :, : 3 * RANK].astype(F32)
+        up[:, rows] = parts[0, b, 0, :, 3 * RANK :].astype(F32)
 
 
 def whole(shape):
@@ -319,24 +332,26 @@
     block = width // NX
     place = jnp.stack([lax.axis_index("x"), lax.axis_index("c")]).astype(jnp.int32)
     smem = pl.BlockSpec(memory_space=pltpu.SMEM)
-    row_block = pl.BlockSpec((TREE, width), lambda b: (b, 0))
-    cache_block = pl.BlockSpec((1, CACHE, HEAD_DIM), lambda b: (b, 0, 0))
-
-    height = block // RANK * NX * MOST + 8
-    packed = call(
-        pack_kernel,
-        "pack",
-        shape((peers, height, RANK)),
+    together = 2
+    row_block = pl.BlockSpec((together * TREE, width), lambda b: (b, 0))
+    cache_block = pl.BlockSpec((together, CACHE, HEAD_DIM), lambda b: (b, 0, 0))
+
+    height = block // RANK * NX * MOST
+    everyone = ("yh", "yl", "zl", "x")
+    products = call(
+        products_kernel,
+        "products",
+        shape((peers, 8, RANK)),
         out_grad,
         merge_up,
-        scratch=[((peers, height, RANK), F32)],
+        scratch=[((peers, 8, RANK), F32)],
         grid=(1,),
         limit=60,
     )
-    received = lax.all_to_all(packed, ("yh", "yl", "zl", "x"), 0, 0, tiled=True)
+    products = lax.all_to_all(products, everyone, 0, 0, tiled=True)
     *turned, partial = pl.pallas_call(
         feature_kernel,
-        grid=(branches,),
+        grid=(branches // together,),
         in_specs=[
             smem,
             smem,
@@ -353,12 +368,14 @@
             whole((3, width)),
             whole((width, 3 * RANK)),
         ],
-        out_specs=[whole((3, block, count))] * NX + [whole((count, 4 * RANK))],
+        out_specs=[pl.BlockSpec(memory_space=pltpu.HBM)] * NX + [whole((count, 4 * RANK))],
         out_shape=[shape((3, block, count))] * NX + [shape((count, 4 * RANK), F32)],
         scratch_shapes=[
             pltpu.VMEM((count, count), F32),
             pltpu.VMEM((3, count, width), BF),
             pltpu.VMEM((count, RANK), F32),
+            pltpu.VMEM((NX, 3, block, count), BF),
+            pltpu.SemaphoreType.DMA((NX,)),
         ],
         compiler_params=params(60),
         cost_estimate=pl.CostEstimate(
@@ -381,6 +398,17 @@
         norm_gains,
         merge_down,
     )
+    packed = call(
+        pack_kernel,
+        "pack",
+        shape((peers, height, RANK)),
+        out_grad,
+        unread=[partial],
+        scratch=[((peers, height, RANK), F32)],
+        grid=(1,),
+        limit=24,
+    )
+    received = lax.all_to_all(packed, everyone, 0, 0, tiled=True)
     for k in range(1, NX):
         turned[k] = lax.ppermute(turned[k], "x", [(i, (i + k) % NX) for i in range(NX)])
     half = count // nc
@@ -388,15 +416,23 @@
         pick_kernel,
         "pick",
         [shape((half, 5 * RANK), F32), shape((half, 5 * RANK), F32), shape((half, RANK), F32)],
-        received,
+        products,
         partial,
     )
     got = lax.ppermute(give, "c", [(i, 1 - i) for i in range(nc)])
-    parts = call(
-        pair_kernel, "pair", shape((nzh, half, 5 * RANK)), keep, got, unread=turned[1:]
-    )
-    parts = lax.all_to_all(parts, "zh", 0, 0, tiled=True)
-    merged = call(merge_kernel, "merge", shape((NX * nc, half, 3 * RANK)), parts, info)
+    own = call(pair_kernel, "pair", shape((half, 5 * RANK)), keep, got, unread=turned[1:2])
+    parts = [
+        lax.ppermute(own, "zh", [(i, (i + k) % nzh) for i in range(nzh)]) for k in range(1, nzh)
+    ]
+    merged = call(
+        merge_kernel,
+        "merge",
+        shape((NX * nc, half, 3 * RANK)),
+        own,
+        *parts,
+        info,
+        unread=turned[2:],
+    )
     merged = lax.all_to_all(merged, ("x", "c"), 0, 0, tiled=True)
     slots = call(
         unpack_kernel,
@@ -418,13 +454,19 @@
     near = nzl * nyl
     grads = jnp.broadcast_to(grads[None], (near * NX, rows, 4 * RANK))
     grads = lax.all_to_all(grads, ("zl", "yl", "x"), 0, 0, tiled=True)
+    grads = grads.reshape(nzl, nyl, NX, rows, 4 * RANK)
+    step = nyl * rows
     return pl.pallas_call(
         final_kernel,
-        grid=(near * NX,),
-        in_specs=[pl.BlockSpec((1, rows, 4 * RANK), lambda i: (i % near * NX + i // near, 0, 0))],
+        grid=(nzl * NX,),
+        in_specs=[
+            pl.BlockSpec(
+                (1, nyl, 1, rows, 4 * RANK), lambda i: (i % nzl, 0, i // nzl, 0, 0)
+            )
+        ],
         out_specs=[
-            pl.BlockSpec((rows, 3 * RANK), lambda i: (i, 0)),
-            pl.BlockSpec((RANK, rows), lambda i: (0, i)),
+            pl.BlockSpec((step, 3 * RANK), lambda i: (i, 0)),
+            pl.BlockSpec((RANK, step), lambda i: (0, i)),
         ],
         out_shape=[shape((width, 3 * RANK), F32), shape((RANK, width), F32)],
         compiler_params=params(),

time: 162 us -> 171 us (1.056)
  starting transfers between devices: 28.3 us -> 64.9 us
  blocking collectives: 85.7 us -> 62.8 us
  Pallas kernels: 22.6 us -> 19.6 us
    all_to_all x1 -> x0, blocking collectives: 22.4 us -> none  [body(): parts = lax.all_to_all(parts, 'zh', 0, 0, tiled=True)]
    ppermute x0 -> x3, starting transfers between devices: none -> 16.9 us  [body(): lax.ppermute(own, 'zh', [(i, (i + k) % nzh) for i in range(nzh)])]
    all_to_all x1 -> x2, starting transfers between devices: 12.5 us -> 23.8 us  [the longest x1 12.6 us: body(): products = lax.all_to_all(products, everyone, 0, 0, tiled=True)]
    all_to_all x1, starting transfers between devices: 3.47 us -> 11.9 us  [body(): merged = lax.all_to_all(merged, ('x', 'c'), 0, 0, tiled=True)]
    ppermute x0 -> x3, waiting for transfers between devices: none -> 4.75 us  [body(): lax.ppermute(own, 'zh', [(i, (i + k) % nzh) for i in range(nzh)])]
    pallas_call x2, Pallas kernels: 16.2 us -> 12.5 us  [the longest x1 8.91 us: body(): pl.pallas_call(feature_kernel, grid=(branches // together,), in_specs=[sm...]
    ppermute x3, waiting for transfers between devices: 10.4 us -> 7 us  [body(): lax.ppermute(turned[k], 'x', [(i, (i + k) % NX) for i in range(NX)])]
    all_to_all x1 -> x2, waiting for transfers between devices: 2.82 us -> 0.01 us  [the longest x1 0.01 us: body(): products = lax.all_to_all(products, everyone, 0, 0, tiled=True)]
  transfers between devices with their start and end apart: 6 -> 10, of which waited for: 4 -> 4; matrix products, arithmetic and copies ran while one was open for 1% -> 1% of each run, Pallas kernels for 7% -> 7%
where the time goes in v4:
time: 171 us; the launch traced here: 170 us
  starting transfers between devices  64.9 us (38%)
  blocking collectives  62.8 us (37%)
  Pallas kernels  19.6 us (11%)
  waiting for transfers between devices  19 us (11%)
  local copies, waits for them, and re-layouts  2.56 us (1%)
    all_to_all x1, blocking collectives, body(): grads = lax.all_to_all(grads, ('zl', 'yl', 'x'), 0, 0, tiled=True)  29.9 us
    all_to_all x1, blocking collectives, body(): lax.all_to_all(grads.reshape(nzl * nyl * nyh, piece, 4 * RANK), ('zl', 'y...  21.2 us
    ppermute x3, starting transfers between devices, body(): lax.ppermute(own, 'zh', [(i, (i + k) % nzh) for i in range(nzh)])  16.9 us
    all_to_all x1, starting transfers between devices, body(): products = lax.all_to_all(products, everyone, 0, 0, tiled=True)  12.6 us
    all_to_all x1, starting transfers between devices, body(): merged = lax.all_to_all(merged, ('x', 'c'), 0, 0, tiled=True)  11.9 us
    all_to_all x1, blocking collectives, body(): lax.all_to_all(grads, 'yh', 0, 0, tiled=True).reshape(rows, 4 * RANK)  11.8 us
    all_to_all x1, starting transfers between devices, body(): received = lax.all_to_all(packed, everyone, 0, 0, tiled=True)  11.2 us
    ppermute x3, starting transfers between devices, body(): lax.ppermute(turned[k], 'x', [(i, (i + k) % NX) for i in range(NX)])  10.4 us
  transfers between devices with their start and end apart: 10, of which 4 were waited for; matrix products, arithmetic and copies ran while one was open for 1% of the time, Pallas kernels for 7%

profile of v4, /device:TPU:2, one launch (start us, length us, event | category | flops | bytes accessed | tf_op | source)
XLA Modules:
  0.0 170.4 jit_solution(14764861744946890742)
XLA Ops:
  0.6 2.3 %products.1 = bf16[64,8,128]{2,1,0:T(8,128)(2,1)} custom-call(bf16[192,2048]{1,0:T(8,128)(2,1)} %grads.4, bf16[128,2048]{1,0:T(8,128)(2,1)} %merge_up.1), custom_call_target="tpu_custom_call" | custom-call | flops 1000000 | bytes 2000000 | tf_op jit(solution)/shard_map/products/pallas_call | solution.py:295
  2.9 12.6 %all-to-all-start.1 = ((bf16[64,8,128]{2,1,0:T(8,128)(2,1)}), bf16[64,8,128]{2,1,0:T(8,128)(2,1)S(1)}, u32[]{:S(2)}, u32[]{:S(2)}) async-start(bf16[64,8,128]{2,1,0:T(8,128)(2,1)} %products.1), calls=%async_computation.1 | async-start | bytes 262144 | tf_op jit(solution)/shard_map/all_to_all | solution.py:351
  15.6 1.4 copy.17.targets
  17.6 8.9 %features.1 = (bf16[3,512,128]{2,1,0:T(8,128)(2,1)}, bf16[3,512,128]{2,1,0:T(8,128)(2,1)}, bf16[3,512,128]{2,1,0:T(8,128)(2,1)}, bf16[3,512,128]{2,1,0:T(8,128)(2,1)}, f32[128,512]{1,0:T(8,128)}) custom-call(s32[2]{0:T(128)} %pad_add_fusion.place, s32[8]{0:T(128)} %lengths.1, s32[8]{0:T(128)} %counts.1, s32[128,1]{1,0:T(8,128)} %copy.17.targets, ...), custom_call_target="tpu_custom_call" | custom-call | flops 400000000 | bytes 8000000 | tf_op jit(solution)/shard_map/features/pallas_call | solution.py:352
  26.5 0.9 copy-done.1
  27.5 1.1 pack.1
  28.5 11.2 %all-to-all-start = ((bf16[64,48,128]{2,1,0:T(8,128)(2,1)}), bf16[64,48,128]{2,1,0:T(8,128)(2,1)S(1)}, u32[]{:S(2)}, u32[]{:S(2)}) async-start(bf16[64,48,128]{2,1,0:T(8,128)(2,1)} %pack.1), calls=%async_computation | async-start | bytes 1572864 | tf_op jit(solution)/shard_map/all_to_all | solution.py:411
  39.8 3.4 %collective-permute-start = (bf16[3,512,128]{2,1,0:T(8,128)(2,1)S(1)}, bf16[3,512,128]{2,1,0:T(8,128)(2,1)S(1)}, u32[]{:S(2)}, u32[]{:S(2)}) collective-permute-start(bf16[3,512,128]{2,1,0:T(8,128)(2,1)S(1)} %copy-done.7), channel_id=1, source_target_pairs={{0,8},{8,16},{16,24},{24,0},{1,9},{9,17},{17,25},{25,1},{2,10},{10... | collective-permute-start | bytes 1179656 | tf_op jit(solution)/shard_map/ppermute | solution.py:413
  43.2 3.0 %collective-permute-start.1 = (bf16[3,512,128]{2,1,0:T(8,128)(2,1)S(1)}, bf16[3,512,128]{2,1,0:T(8,128)(2,1)S(1)}, u32[]{:S(2)}, u32[]{:S(2)}) collective-permute-start(bf16[3,512,128]{2,1,0:T(8,128)(2,1)S(1)} %copy-done.6), channel_id=1, source_target_pairs={{0,16},{8,24},{16,0},{24,8},{1,17},{9,25},{17,1},{25,9},{2,18},{10... | collective-permute-start | bytes 1179656 | tf_op jit(solution)/shard_map/ppermute | solution.py:413
  46.1 4.1 %collective-permute-start.2 = (bf16[3,512,128]{2,1,0:T(8,128)(2,1)S(1)}, bf16[3,512,128]{2,1,0:T(8,128)(2,1)S(1)}, u32[]{:S(2)}, u32[]{:S(2)}) collective-permute-start(bf16[3,512,128]{2,1,0:T(8,128)(2,1)S(1)} %copy-done.5), channel_id=1, source_target_pairs={{0,24},{8,0},{16,8},{24,16},{1,25},{9,1},{17,9},{25,17},{2,26},{10... | collective-permute-start | bytes 1179656 | tf_op jit(solution)/shard_map/ppermute | solution.py:413
  50.6 1.9 %collective-permute-start.3 = (f32[64,640]{1,0:T(8,128)S(1)}, f32[64,640]{1,0:T(8,128)S(1)}, u32[]{:S(2)}, u32[]{:S(2)}) collective-permute-start(f32[64,640]{1,0:T(8,128)S(1)} %get-tuple-element.16), channel_id=1, source_target_pairs={{0,1},{1,0},{2,3},{3,2},{4,5},{5,4},{6,7},{7,6},{8,9},{9,8},{10,11... | collective-permute-start | bytes 491528 | tf_op jit(solution)/shard_map/ppermute | solution.py:422
  52.5 7.0 %collective-permute-done.first = bf16[3,512,128]{2,1,0:T(8,128)(2,1)S(1)} collective-permute-done((bf16[3,512,128]{2,1,0:T(8,128)(2,1)S(1)}, bf16[3,512,128]{2,1,0:T(8,128)(2,1)S(1)}, u32[]{:S(2)}, u32[]{:S(2)}) %collective-permute-start) | collective-permute-done | bytes 393248 | tf_op jit(solution)/shard_map/ppermute | solution.py:413
  59.7 10.2 %collective-permute-start.6 = (bf16[64,640]{1,0:T(8,128)(2,1)S(1)}, bf16[64,640]{1,0:T(8,128)(2,1)S(1)}, u32[]{:S(2)}, u32[]{:S(2)}) collective-permute-start(bf16[64,640]{1,0:T(8,128)(2,1)S(1)} %pair.1.own), channel_id=1, source_target_pairs={{0,6},{2,0},{4,2},{6,4},{1,7},{3,1},{5,3},{7,5},{8,14},{10,8},{12,... | collective-permute-start | bytes 245768 | tf_op jit(solution)/shard_map/ppermute | solution.py:425
  69.9 1.9 %collective-permute-start.5 = (bf16[64,640]{1,0:T(8,128)(2,1)S(1)}, bf16[64,640]{1,0:T(8,128)(2,1)S(1)}, u32[]{:S(2)}, u32[]{:S(2)}) collective-permute-start(bf16[64,640]{1,0:T(8,128)(2,1)S(1)} %pair.1.own), channel_id=1, source_target_pairs={{0,4},{2,6},{4,0},{6,2},{1,5},{3,7},{5,1},{7,3},{8,12},{10,14},{12... | collective-permute-start | bytes 245768 | tf_op jit(solution)/shard_map/ppermute | solution.py:425
  71.8 4.8 %collective-permute-start.4 = (bf16[64,640]{1,0:T(8,128)(2,1)S(1)}, bf16[64,640]{1,0:T(8,128)(2,1)S(1)}, u32[]{:S(2)}, u32[]{:S(2)}) collective-permute-start(bf16[64,640]{1,0:T(8,128)(2,1)S(1)} %pair.1.own), channel_id=1, source_target_pairs={{0,2},{2,4},{4,6},{6,0},{1,3},{3,5},{5,7},{7,1},{8,10},{10,12},{12... | collective-permute-start | bytes 245768 | tf_op jit(solution)/shard_map/ppermute | solution.py:425
  76.7 4.3 %collective-permute-done.5.far = bf16[64,640]{1,0:T(8,128)(2,1)S(1)} collective-permute-done((bf16[64,640]{1,0:T(8,128)(2,1)S(1)}, bf16[64,640]{1,0:T(8,128)(2,1)S(1)}, u32[]{:S(2)}, u32[]{:S(2)}) %collective-permute-start.5) | collective-permute-done | bytes 81952 | tf_op jit(solution)/shard_map/ppermute | solution.py:425
  81.4 1.0 merge.1
  82.4 11.9 %all-to-all-start.2 = ((bf16[8,64,384]{2,1,0:T(8,128)(2,1)}), bf16[8,64,384]{2,1,0:T(8,128)(2,1)S(1)}, u32[]{:S(2)}, u32[]{:S(2)}) async-start(bf16[8,64,384]{2,1,0:T(8,128)(2,1)} %merge.1), calls=%async_computation.2 | async-start | bytes 786432 | tf_op jit(solution)/shard_map/all_to_all | solution.py:436
  94.5 7.3 %all-to-all-done.2.merged = bf16[8,64,384]{2,1,0:T(8,128)(2,1)S(1)} async-done(((bf16[8,64,384]{2,1,0:T(8,128)(2,1)}), bf16[8,64,384]{2,1,0:T(8,128)(2,1)S(1)}, u32[]{:S(2)}, u32[]{:S(2)}) %all-to-all-start.2) | async-done | bytes 393248 | tf_op jit(solution)/shard_map/all_to_all | solution.py:436
  101.8 1.9 %grads.5 = bf16[512,512]{1,0:T(8,128)(2,1)S(1)} custom-call(s32[2]{0:T(128)S(1)} %copy-done.4, bf16[3,512,128]{2,1,0:T(8,128)(2,1)S(1)} %copy-done.3, bf16[3,512,128]{2,1,0:T(8,128)(2,1)S(1)} %collective-permute-done.first, bf16[3,512,128]{2,1,0:T(8,128)(2,1)S(1)} %collective-permute-done.1.second, bf16[3,512,128]{2,1,0:T(8,128)(2,1)S(1)} %collective-permute-done.2.third, ...), custom_call_target="tpu_custom_call" | custom-call | flops 1000000 | bytes 2000000 | tf_op jit(solution)/shard_map/grads/pallas_call | solution.py:295
  103.7 21.2 %all_to_all.30.parts = bf16[16,32,512]{2,1,0:T(8,128)(2,1)S(1)} all-to-all(bf16[16,32,512]{2,1,0:T(8,128)(2,1)S(1)} %bitcast.6), channel_id=1, replica_groups=mesh['yh'=4,'yl'=2,'zl'=2,'x'=4,'zh'=4,'c'=2] {'zl','yl','yh'}, dimensions={0} | all-to-all | bytes 1048576 | tf_op jit(solution)/shard_map/all_to_all | solution.py:448
  125.0 11.8 %all_to_all.31 = bf16[4,32,512]{2,1,0:T(8,128)(2,1)S(1)} all-to-all(bf16[4,32,512]{2,1,0:T(8,128)(2,1)S(1)} %total.1), channel_id=1, replica_groups=mesh['yh'=4,'yl'=2,'zl'=2,'x'=4,'zh'=4,'c'=2] {'yh'}, dimensions={0} | all-to-all | bytes 262144 | tf_op jit(solution)/shard_map/all_to_all | solution.py:453
  137.0 29.9 %all_to_all.32 = bf16[16,128,512]{2,1,0:T(8,128)(2,1)S(1)} all-to-all(bf16[16,128,512]{2,1,0:T(8,128)(2,1)S(1)} %broadcast_in_dim.8), channel_id=1, replica_groups=mesh['yh'=4,'yl'=2,'zl'=2,'x'=4,'zh'=4,'c'=2] {'zl','yl','x'}, dimensions={0} | all-to-all | bytes 4194304 | tf_op jit(solution)/shard_map/all_to_all | solution.py:456
  166.8 3.6 %final.1 = (f32[2048,384]{1,0:T(8,128)}, f32[128,2048]{1,0:T(8,128)}) custom-call(bf16[2,2,4,128,512]{4,3,2,1,0:T(8,128)(2,1)S(1)} %bitcast.5), custom_call_target="tpu_custom_call" | custom-call | tf_op jit(solution)/shard_map/final/pallas_call | solution.py:459
  (28 shorter events, 2.2 us)
Async XLA Ops:
  2.9 23.6 %copy-start = (bf16[192,2048]{1,0:T(8,128)(2,1)S(1)}, bf16[192,2048]{1,0:T(8,128)(2,1)}, u32[]{:S(2)}) copy-start(bf16[192,2048]{1,0:T(8,128)(2,1)} %grads.4) | copy-start | bytes 2359300
  2.9 25.6 %all-to-all-start.1 = ((bf16[64,8,128]{2,1,0:T(8,128)(2,1)}), bf16[64,8,128]{2,1,0:T(8,128)(2,1)S(1)}, u32[]{:S(2)}, u32[]{:S(2)}) async-start(bf16[64,8,128]{2,1,0:T(8,128)(2,1)} %products.1), calls=%async_computation.1 | async-start | bytes 262144 | tf_op jit(solution)/shard_map/all_to_all | solution.py:351
  26.5 1.0 copy-start.1
  27.5 12.3 %copy-start.7 = (bf16[3,512,128]{2,1,0:T(8,128)(2,1)S(1)}, bf16[3,512,128]{2,1,0:T(8,128)(2,1)}, u32[]{:S(2)}) copy-start(bf16[3,512,128]{2,1,0:T(8,128)(2,1)} %get-tuple-element.11) | copy-start | bytes 1179652
  27.5 15.7 %copy-start.6 = (bf16[3,512,128]{2,1,0:T(8,128)(2,1)S(1)}, bf16[3,512,128]{2,1,0:T(8,128)(2,1)}, u32[]{:S(2)}) copy-start(bf16[3,512,128]{2,1,0:T(8,128)(2,1)} %get-tuple-element.12) | copy-start | bytes 1179652
  27.5 18.7 %copy-start.5 = (bf16[3,512,128]{2,1,0:T(8,128)(2,1)S(1)}, bf16[3,512,128]{2,1,0:T(8,128)(2,1)}, u32[]{:S(2)}) copy-start(bf16[3,512,128]{2,1,0:T(8,128)(2,1)} %get-tuple-element.13) | copy-start | bytes 1179652
  27.5 22.8 %copy-start.2 = (f32[128,512]{1,0:T(8,128)S(1)}, f32[128,512]{1,0:T(8,128)}, u32[]{:S(2)}) copy-start(f32[128,512]{1,0:T(8,128)} %get-tuple-element.14.after.partial) | copy-start | bytes 786436
  28.5 53.9 %all-to-all-start = ((bf16[64,48,128]{2,1,0:T(8,128)(2,1)}), bf16[64,48,128]{2,1,0:T(8,128)(2,1)S(1)}, u32[]{:S(2)}, u32[]{:S(2)}) async-start(bf16[64,48,128]{2,1,0:T(8,128)(2,1)} %pack.1), calls=%async_computation | async-start | bytes 1572864 | tf_op jit(solution)/shard_map/all_to_all | solution.py:411
  39.8 19.7 %collective-permute-start = (bf16[3,512,128]{2,1,0:T(8,128)(2,1)S(1)}, bf16[3,512,128]{2,1,0:T(8,128)(2,1)S(1)}, u32[]{:S(2)}, u32[]{:S(2)}) collective-permute-start(bf16[3,512,128]{2,1,0:T(8,128)(2,1)S(1)} %copy-done.7), channel_id=1, source_target_pairs={{0,8},{8,16},{16,24},{24,0},{1,9},{9,17},{17,25},{25,1},{2,10},{10... | collective-permute-start | bytes 1179656 | tf_op jit(solution)/shard_map/ppermute | solution.py:413
  43.2 33.5 %collective-permute-start.1 = (bf16[3,512,128]{2,1,0:T(8,128)(2,1)S(1)}, bf16[3,512,128]{2,1,0:T(8,128)(2,1)S(1)}, u32[]{:S(2)}, u32[]{:S(2)}) collective-permute-start(bf16[3,512,128]{2,1,0:T(8,128)(2,1)S(1)} %copy-done.6), channel_id=1, source_target_pairs={{0,16},{8,24},{16,0},{24,8},{1,17},{9,25},{17,1},{25,9},{2,18},{10... | collective-permute-start | bytes 1179656 | tf_op jit(solution)/shard_map/ppermute | solution.py:413
  46.1 30.5 %collective-permute-start.2 = (bf16[3,512,128]{2,1,0:T(8,128)(2,1)S(1)}, bf16[3,512,128]{2,1,0:T(8,128)(2,1)S(1)}, u32[]{:S(2)}, u32[]{:S(2)}) collective-permute-start(bf16[3,512,128]{2,1,0:T(8,128)(2,1)S(1)} %copy-done.5), channel_id=1, source_target_pairs={{0,24},{8,0},{16,8},{24,16},{1,25},{9,1},{17,9},{25,17},{2,26},{10... | collective-permute-start | bytes 1179656 | tf_op jit(solution)/shard_map/ppermute | solution.py:413
  50.6 8.9 %collective-permute-start.3 = (f32[64,640]{1,0:T(8,128)S(1)}, f32[64,640]{1,0:T(8,128)S(1)}, u32[]{:S(2)}, u32[]{:S(2)}) collective-permute-start(f32[64,640]{1,0:T(8,128)S(1)} %get-tuple-element.16), channel_id=1, source_target_pairs={{0,1},{1,0},{2,3},{3,2},{4,5},{5,4},{6,7},{7,6},{8,9},{9,8},{10,11... | collective-permute-start | bytes 491528 | tf_op jit(solution)/shard_map/ppermute | solution.py:422
  59.7 42.1 %copy-start.3 = (bf16[3,512,128]{2,1,0:T(8,128)(2,1)S(1)}, bf16[3,512,128]{2,1,0:T(8,128)(2,1)}, u32[]{:S(2)}) copy-start(bf16[3,512,128]{2,1,0:T(8,128)(2,1)} %get-tuple-element.10.own) | copy-start | bytes 1179652
  59.7 42.1 %copy-start.4 = (s32[2]{0:T(128)S(1)}, s32[2]{0:T(128)}, u32[]{:S(2)}) copy-start(s32[2]{0:T(128)} %pad_add_fusion.place) | copy-start | bytes 28
  59.7 16.9 %collective-permute-start.6 = (bf16[64,640]{1,0:T(8,128)(2,1)S(1)}, bf16[64,640]{1,0:T(8,128)(2,1)S(1)}, u32[]{:S(2)}, u32[]{:S(2)}) collective-permute-start(bf16[64,640]{1,0:T(8,128)(2,1)S(1)} %pair.1.own), channel_id=1, source_target_pairs={{0,6},{2,0},{4,2},{6,4},{1,7},{3,1},{5,3},{7,5},{8,14},{10,8},{12,... | collective-permute-start | bytes 245768 | tf_op jit(solution)/shard_map/ppermute | solution.py:425
  69.9 11.0 %collective-permute-start.5 = (bf16[64,640]{1,0:T(8,128)(2,1)S(1)}, bf16[64,640]{1,0:T(8,128)(2,1)S(1)}, u32[]{:S(2)}, u32[]{:S(2)}) collective-permute-start(bf16[64,640]{1,0:T(8,128)(2,1)S(1)} %pair.1.own), channel_id=1, source_target_pairs={{0,4},{2,6},{4,0},{6,2},{1,5},{3,7},{5,1},{7,3},{8,12},{10,14},{12... | collective-permute-start | bytes 245768 | tf_op jit(solution)/shard_map/ppermute | solution.py:425
  71.8 9.6 %collective-permute-start.4 = (bf16[64,640]{1,0:T(8,128)(2,1)S(1)}, bf16[64,640]{1,0:T(8,128)(2,1)S(1)}, u32[]{:S(2)}, u32[]{:S(2)}) collective-permute-start(bf16[64,640]{1,0:T(8,128)(2,1)S(1)} %pair.1.own), channel_id=1, source_target_pairs={{0,2},{2,4},{4,6},{6,0},{1,3},{3,5},{5,7},{7,1},{8,10},{10,12},{12... | collective-permute-start | bytes 245768 | tf_op jit(solution)/shard_map/ppermute | solution.py:425
  82.4 19.3 %all-to-all-start.2 = ((bf16[8,64,384]{2,1,0:T(8,128)(2,1)}), bf16[8,64,384]{2,1,0:T(8,128)(2,1)S(1)}, u32[]{:S(2)}, u32[]{:S(2)}) async-start(bf16[8,64,384]{2,1,0:T(8,128)(2,1)} %merge.1), calls=%async_computation.2 | async-start | bytes 786432 | tf_op jit(solution)/shard_map/all_to_all | solution.py:436

commit v5 on v4

--- a/solution.py
+++ b/solution.py
@@ -137,26 +137,20 @@
         rank = jnp.sum(dot(earlier, named.astype(BF)) * named, axis=1, keepdims=True)
         notes = squares[...]
         lane = iota((count, RANK), 1)
-        for i, note in ((6, target.astype(F32)), (7, rank), (8, place[1].astype(F32))):
+        for i, note in ((6, target.astype(F32)), (7, rank)):
             notes = jnp.where(lane == i, note, notes)
         partial[:, 3 * RANK :] = notes
         for copy in copies:
             copy.wait()
 
 
-def products_kernel(grads, merge_up, out, rows):
-    products = dot_nt(grads[...], merge_up[...])
-    rows[...] = jnp.zeros_like(rows)
-    for d in range(out.shape[0]):
-        rows[d, :MOST, :] = products[d * MOST : (d + 1) * MOST, :]
-    out[...] = rows[...].astype(BF)
-
-
-def pack_kernel(grads, after, out, rows):
-    peers = out.shape[0]
+def pack_kernel(grads, merge_up, out, rows):
+    peers, height = out.shape[0], out.shape[1]
     slots = grads.shape[0] // (peers // NX)
     blocks = grads.shape[1] // NX // RANK
     wide = grads[...].astype(F32)
+    products = dot_nt(grads[...], merge_up[...])
+    rows[:, blocks * slots :, :] = jnp.zeros((peers, height - blocks * slots, RANK), F32)
     for x in range(NX):
         for b in range(blocks):
             column = (x * blocks + b) * RANK
@@ -164,6 +158,8 @@
                 rows[g * NX + x, b * slots : (b + 1) * slots, :] = wide[
                     g * slots : (g + 1) * slots, column : column + RANK
                 ]
+    for d in range(peers):
+        rows[d, blocks * slots : blocks * slots + MOST, :] = products[d * MOST : (d + 1) * MOST, :]
     out[...] = rows[...].astype(BF)
 
 
@@ -179,40 +175,28 @@
     out[...] = rows[...].astype(BF)
 
 
-def pick_kernel(received, partial, keep, give, info):
+def pick_kernel(received, partial, out):
     count = partial.shape[0]
-    half = keep.shape[0]
     peers = received.shape[0]
-    tail = received[...].astype(F32).reshape(peers * 8, RANK).astype(BF)
+    tail = received[:, received.shape[1] - 8 :, :].astype(F32).reshape(peers * 8, RANK).astype(BF)
     notes = partial[:, 3 * RANK :]
     place = (notes[:, 6:7] * 8.0 + notes[:, 7:8]).astype(jnp.int32)
     chosen = place == iota((count, peers * 8), 1)
-    back = dot(chosen.astype(BF), tail)
-    upper = notes[:half, 8:9] > 0.5
-    for source, start in ((partial[:, : 3 * RANK], 0), (back, 3 * RANK), (notes, 4 * RANK)):
-        columns = slice(start, start + source.shape[1])
-        keep[:, columns] = jnp.where(upper, source[half:], source[:half])
-        give[:, columns] = jnp.where(upper, source[:half], source[half:])
-    info[...] = jnp.where(upper, notes[half:], notes[:half])
-
-
-def pair_kernel(keep, got, first, out):
-    total = keep[...] + got[...]
-    squares = total[:, 4 * RANK :]
-    rough = squares.astype(BF).astype(F32)
-    lane = iota(squares.shape, 1)
+    out[:, : 3 * RANK] = partial[:, : 3 * RANK].astype(BF)
+    out[:, 3 * RANK : 4 * RANK] = dot(chosen.astype(BF), tail).astype(BF)
+    rough = notes.astype(BF).astype(F32)
+    lane = iota(notes.shape, 1)
     for i in range(3):
-        rest = squares[:, i : i + 1] - rough[:, i : i + 1]
+        rest = notes[:, i : i + 1] - rough[:, i : i + 1]
         rough = jnp.where(lane == 3 + i, rest, rough)
-    rough = jnp.where(lane < 6, rough, 0.0)
-    out[:, : 4 * RANK] = total[:, : 4 * RANK].astype(BF)
     out[:, 4 * RANK :] = rough.astype(BF)
 
 
-def merge_kernel(own, near, far, last, info, second, third, out):
-    total = own[...].astype(F32)
-    for part in (near, far, last):
-        total = total + part[...].astype(F32)
+def merge_kernel(parts, *refs):
+    out = refs[-1]
+    total = parts[0].astype(F32)
+    for peer in range(1, parts.shape[0]):
+        total = total + parts[peer].astype(F32)
     squares = total[:, 4 * RANK :]
     inverse = [
         lax.rsqrt((squares[:, i : i + 1] + squares[:, 3 + i : 4 + i]) / MODEL_WIDTH + EPSILON)
@@ -225,7 +209,7 @@
     gate = 1.0 / (1.0 + jnp.exp(-mixed))
     grad = (back * gate * (1.0 + mixed * (1.0 - gate))).astype(BF)
     active = (mixed * gate).astype(BF)
-    notes = info[...]
+    notes = squares / parts.shape[0]
     lane = iota(notes.shape, 1)
     for i in range(3):
         rough = inverse[i].astype(BF).astype(F32)
@@ -245,7 +229,7 @@
     placed = None
     for k, turned in enumerate((own, first, second, third)):
         source = (place[0] + NX - k) % NX
-        rows = jnp.concatenate([merged[2 * source], merged[2 * source + 1]], axis=0)
+        rows = merged[source]
         notes = rows[:, 2 * RANK :].astype(F32)
         grad = rows[:, :RANK].astype(F32)
         for i in range(3):
@@ -330,25 +314,24 @@
     nzh, nc = lax.axis_size("zh"), lax.axis_size("c")
     peers = nyh * nyl * nzl * NX
     block = width // NX
-    place = jnp.stack([lax.axis_index("x"), lax.axis_index("c")]).astype(jnp.int32)
+    place = lax.axis_index("x").astype(jnp.int32).reshape(1)
     smem = pl.BlockSpec(memory_space=pltpu.SMEM)
     together = 2
     row_block = pl.BlockSpec((together * TREE, width), lambda b: (b, 0))
     cache_block = pl.BlockSpec((together, CACHE, HEAD_DIM), lambda b: (b, 0, 0))
 
-    height = block // RANK * NX * MOST
-    everyone = ("yh", "yl", "zl", "x")
-    products = call(
-        products_kernel,
-        "products",
-        shape((peers, 8, RANK)),
+    height = block // RANK * NX * MOST + 8
+    packed = call(
+        pack_kernel,
+        "pack",
+        shape((peers, height, RANK)),
         out_grad,
         merge_up,
-        scratch=[((peers, 8, RANK), F32)],
+        scratch=[((peers, height, RANK), F32)],
         grid=(1,),
         limit=60,
     )
-    products = lax.all_to_all(products, everyone, 0, 0, tiled=True)
+    received = lax.all_to_all(packed, ("yh", "yl", "zl", "x"), 0, 0, tiled=True)
     *turned, partial = pl.pallas_call(
         feature_kernel,
         grid=(branches // together,),
@@ -398,42 +381,20 @@
         norm_gains,
         merge_down,
     )
-    packed = call(
-        pack_kernel,
-        "pack",
-        shape((peers, height, RANK)),
-        out_grad,
-        unread=[partial],
-        scratch=[((peers, height, RANK), F32)],
-        grid=(1,),
-        limit=24,
-    )
-    received = lax.all_to_all(packed, everyone, 0, 0, tiled=True)
     for k in range(1, NX):
         turned[k] = lax.ppermute(turned[k], "x", [(i, (i + k) % NX) for i in range(NX)])
-    half = count // nc
-    keep, give, info = call(
-        pick_kernel,
-        "pick",
-        [shape((half, 5 * RANK), F32), shape((half, 5 * RANK), F32), shape((half, RANK), F32)],
-        products,
-        partial,
-    )
-    got = lax.ppermute(give, "c", [(i, 1 - i) for i in range(nc)])
-    own = call(pair_kernel, "pair", shape((half, 5 * RANK)), keep, got, unread=turned[1:2])
-    parts = [
-        lax.ppermute(own, "zh", [(i, (i + k) % nzh) for i in range(nzh)]) for k in range(1, nzh)
-    ]
+    sent = call(pick_kernel, "pick", shape((count, 5 * RANK)), received, partial)
+    share = count // (nzh * nc)
+    parts = lax.all_to_all(sent.reshape(nzh * nc, share, 5 * RANK), ("zh", "c"), 0, 0, tiled=True)
     merged = call(
         merge_kernel,
         "merge",
-        shape((NX * nc, half, 3 * RANK)),
-        own,
-        *parts,
-        info,
-        unread=turned[2:],
-    )
-    merged = lax.all_to_all(merged, ("x", "c"), 0, 0, tiled=True)
+        shape((NX * nzh * nc, share, 3 * RANK)),
+        parts,
+        unread=turned[1:],
+    )
+    merged = lax.all_to_all(merged, ("x", "zh", "c"), 0, 0, tiled=True)
+    merged = merged.reshape(NX, count, 3 * RANK)
     slots = call(
         unpack_kernel,
         "unpack",

time: 171 us -> 153 us (0.89)
  starting transfers between devices: 64.9 us -> 37.5 us
  waiting for transfers between devices: 19 us -> 29.3 us
    all_to_all x3, waiting for transfers between devices: 7.28 us -> 27.9 us  [the longest x1 13.6 us: body(): merged = lax.all_to_all(merged, ('x', 'zh', 'c'), 0, 0, tiled=True)]
    ppermute x4 -> x0, starting transfers between devices: 18.8 us -> none  [the longest x3 16.9 us: body(): lax.ppermute(own, 'zh', [(i, (i + k) % nzh) for i in range(nzh)])]
    all_to_all x3, starting transfers between devices: 35.7 us -> 27 us  [the longest x1 12.5 us: body(): received = lax.all_to_all(packed, ('yh', 'yl', 'zl', 'x'), 0, 0, tiled=True)]
    ppermute x3, waiting for transfers between devices: 7 us -> 1.37 us  [body(): lax.ppermute(turned[k], 'x', [(i, (i + k) % NX) for i in range(NX)])]
    ppermute x4 -> x0, waiting for transfers between devices: 4.75 us -> none  [the longest x3 4.75 us: body(): lax.ppermute(own, 'zh', [(i, (i + k) % nzh) for i in range(nzh)])]
    all_to_all x1, blocking collectives: 11.8 us -> 13.9 us  [body(): lax.all_to_all(grads, 'yh', 0, 0, tiled=True).reshape(rows, 4 * RANK)]
    all_to_all x1, blocking collectives: 21.2 us -> 19.3 us  [body(): lax.all_to_all(grads.reshape(nzl * nyl * nyh, piece, 4 * RANK), ('zl', 'y...]
    pallas_call x8 -> x6, Pallas kernels: 7.11 us -> 6.31 us  [call(): pl.pallas_call(kernel, grid=grid, in_specs=specs, out_specs=outs if isins...]
  transfers between devices with their start and end apart: 10 -> 6, of which waited for: 4 -> 4; matrix products, arithmetic and copies ran while one was open for 1% -> 0% of each run, Pallas kernels for 7% -> 7%
where the time goes in v5:
time: 153 us; the launch traced here: 152 us
  blocking collectives  63.2 us (41%)
  starting transfers between devices  37.5 us (25%)
  waiting for transfers between devices  29.3 us (19%)
  Pallas kernels  18.8 us (12%)
  local copies, waits for them, and re-layouts  2.88 us (2%)
    all_to_all x1, blocking collectives, body(): grads = lax.all_to_all(grads, ('zl', 'yl', 'x'), 0, 0, tiled=True)  29.9 us
    all_to_all x1, blocking collectives, body(): lax.all_to_all(grads.reshape(nzl * nyl * nyh, piece, 4 * RANK), ('zl', 'y...  19.3 us
    all_to_all x1, blocking collectives, body(): lax.all_to_all(grads, 'yh', 0, 0, tiled=True).reshape(rows, 4 * RANK)  13.9 us
    all_to_all x1, waiting for transfers between devices, body(): merged = lax.all_to_all(merged, ('x', 'zh', 'c'), 0, 0, tiled=True)  13.6 us
    all_to_all x1, starting transfers between devices, body(): received = lax.all_to_all(packed, ('yh', 'yl', 'zl', 'x'), 0, 0, tiled=True)  12.5 us
    ppermute x3, starting transfers between devices, body(): lax.ppermute(turned[k], 'x', [(i, (i + k) % NX) for i in range(NX)])  10.4 us
    all_to_all x1, starting transfers between devices, body(): lax.all_to_all(sent.reshape(nzh * nc, share, 5 * RANK), ('zh', 'c'), 0, 0...  9.41 us
    all_to_all x1, waiting for transfers between devices, body(): lax.all_to_all(sent.reshape(nzh * nc, share, 5 * RANK), ('zh', 'c'), 0, 0...  9.27 us
  transfers between devices with their start and end apart: 6, of which 4 were waited for; matrix products, arithmetic and copies ran while one was open for 0% of the time, Pallas kernels for 7%

profile of v5, /device:TPU:2, one launch (start us, length us, event | category | flops | bytes accessed | tf_op | source)
XLA Modules:
  0.0 152.3 jit_solution(18420598318871926813)
XLA Ops:
  0.6 2.7 %pack.1 = bf16[64,56,128]{2,1,0:T(8,128)(2,1)} custom-call(bf16[192,2048]{1,0:T(8,128)(2,1)} %grads.2, bf16[128,2048]{1,0:T(8,128)(2,1)} %merge_up.1), custom_call_target="tpu_custom_call" | custom-call | flops 1000000 | bytes 2000000 | tf_op jit(solution)/shard_map/pack/pallas_call | solution.py:279
  3.3 12.5 %all-to-all-start = ((bf16[64,56,128]{2,1,0:T(8,128)(2,1)}), bf16[64,56,128]{2,1,0:T(8,128)(2,1)S(1)}, u32[]{:S(2)}, u32[]{:S(2)}) async-start(bf16[64,56,128]{2,1,0:T(8,128)(2,1)} %pack.1), calls=%async_computation | async-start | bytes 1835008 | tf_op jit(solution)/shard_map/all_to_all | solution.py:334
  15.8 0.7 copy.17.targets
  16.5 8.9 %features.1 = (bf16[3,512,128]{2,1,0:T(8,128)(2,1)}, bf16[3,512,128]{2,1,0:T(8,128)(2,1)}, bf16[3,512,128]{2,1,0:T(8,128)(2,1)}, bf16[3,512,128]{2,1,0:T(8,128)(2,1)}, f32[128,512]{1,0:T(8,128)}) custom-call(s32[1]{0:T(128)} %bitcast.place, s32[8]{0:T(128)} %lengths.1, s32[8]{0:T(128)} %counts.1, s32[128,1]{1,0:T(8,128)} %copy.17.targets, s32[8,16]{1,0:T(8,128)} %parents.1, ...), custom_call_target="tpu_custom_call" | custom-call | flops 400000000 | bytes 8000000 | tf_op jit(solution)/shard_map/features/pallas_call | solution.py:335
  25.5 3.4 %collective-permute-start = (bf16[3,512,128]{2,1,0:T(8,128)(2,1)}, bf16[3,512,128]{2,1,0:T(8,128)(2,1)S(1)}, u32[]{:S(2)}, u32[]{:S(2)}) collective-permute-start(bf16[3,512,128]{2,1,0:T(8,128)(2,1)} %get-tuple-element.8), channel_id=1, source_target_pairs={{0,8},{8,16},{16,24},{24,0},{1,9},{9,17},{17,25},{25,1},{2,10},{10... | collective-permute-start | bytes 1179656 | tf_op jit(solution)/shard_map/ppermute | solution.py:385
  28.8 3.0 %collective-permute-start.1 = (bf16[3,512,128]{2,1,0:T(8,128)(2,1)}, bf16[3,512,128]{2,1,0:T(8,128)(2,1)S(1)}, u32[]{:S(2)}, u32[]{:S(2)}) collective-permute-start(bf16[3,512,128]{2,1,0:T(8,128)(2,1)} %get-tuple-element.9), channel_id=1, source_target_pairs={{0,16},{8,24},{16,0},{24,8},{1,17},{9,25},{17,1},{25,9},{2,18},{10... | collective-permute-start | bytes 1179656 | tf_op jit(solution)/shard_map/ppermute | solution.py:385
  31.8 4.1 %collective-permute-start.2 = (bf16[3,512,128]{2,1,0:T(8,128)(2,1)}, bf16[3,512,128]{2,1,0:T(8,128)(2,1)S(1)}, u32[]{:S(2)}, u32[]{:S(2)}) collective-permute-start(bf16[3,512,128]{2,1,0:T(8,128)(2,1)} %get-tuple-element.10), channel_id=1, source_target_pairs={{0,24},{8,0},{16,8},{24,16},{1,25},{9,1},{17,9},{25,17},{2,26},{10... | collective-permute-start | bytes 1179656 | tf_op jit(solution)/shard_map/ppermute | solution.py:385
  35.9 5.0 %all-to-all-done.received = bf16[64,56,128]{2,1,0:T(8,128)(2,1)S(1)} async-done(((bf16[64,56,128]{2,1,0:T(8,128)(2,1)}), bf16[64,56,128]{2,1,0:T(8,128)(2,1)S(1)}, u32[]{:S(2)}, u32[]{:S(2)}) %all-to-all-start) | async-done | bytes 917536 | tf_op jit(solution)/shard_map/all_to_all | solution.py:334
  40.9 0.9 copy-done.1
  41.9 1.0 pick.1
  42.9 9.4 %all-to-all-start.1 = ((bf16[8,16,640]{2,1,0:T(8,128)(2,1)}), bf16[8,16,640]{2,1,0:T(8,128)(2,1)S(1)}, u32[]{:S(2)}, u32[]{:S(2)}) async-start(bf16[8,16,640]{2,1,0:T(8,128)(2,1)} %bitcast.1), calls=%async_computation.1 | async-start | bytes 327680 | tf_op jit(solution)/shard_map/all_to_all | solution.py:388
  52.3 1.4 collective-permute-done.2.refs_2_.third
  53.6 9.3 %all-to-all-done.1.parts = bf16[8,16,640]{2,1,0:T(8,128)(2,1)S(1)} async-done(((bf16[8,16,640]{2,1,0:T(8,128)(2,1)}), bf16[8,16,640]{2,1,0:T(8,128)(2,1)S(1)}, u32[]{:S(2)}, u32[]{:S(2)}) %all-to-all-start.1) | async-done | bytes 163872 | tf_op jit(solution)/shard_map/all_to_all | solution.py:388
  62.9 0.9 merge.1
  63.9 5.2 %all-to-all-start.2 = ((bf16[32,16,384]{2,1,0:T(8,128)(2,1)}), bf16[32,16,384]{2,1,0:T(8,128)(2,1)S(1)}, u32[]{:S(2)}, u32[]{:S(2)}) async-start(bf16[32,16,384]{2,1,0:T(8,128)(2,1)} %merge.1), calls=%async_computation.2 | async-start | bytes 786432 | tf_op jit(solution)/shard_map/all_to_all | solution.py:396
  69.0 0.2 unpack.1.slots
  69.2 13.6 %all-to-all-done.2 = bf16[32,16,384]{2,1,0:T(8,128)(2,1)S(1)} async-done(((bf16[32,16,384]{2,1,0:T(8,128)(2,1)}), bf16[32,16,384]{2,1,0:T(8,128)(2,1)S(1)}, u32[]{:S(2)}, u32[]{:S(2)}) %all-to-all-start.2) | async-done | bytes 393248 | tf_op jit(solution)/shard_map/all_to_all | solution.py:396
  82.9 1.0 copy-done
  83.9 1.4 grads.3
  85.3 19.3 %all_to_all.30.parts = bf16[16,32,512]{2,1,0:T(8,128)(2,1)S(1)} all-to-all(bf16[16,32,512]{2,1,0:T(8,128)(2,1)S(1)} %bitcast.7), channel_id=1, replica_groups=mesh['yh'=4,'yl'=2,'zl'=2,'x'=4,'zh'=4,'c'=2] {'zl','yl','yh'}, dimensions={0} | all-to-all | bytes 1048576 | tf_op jit(solution)/shard_map/all_to_all | solution.py:409
  104.6 13.9 %all_to_all.31 = bf16[4,32,512]{2,1,0:T(8,128)(2,1)S(1)} all-to-all(bf16[4,32,512]{2,1,0:T(8,128)(2,1)S(1)} %total.1), channel_id=1, replica_groups=mesh['yh'=4,'yl'=2,'zl'=2,'x'=4,'zh'=4,'c'=2] {'yh'}, dimensions={0} | all-to-all | bytes 262144 | tf_op jit(solution)/shard_map/all_to_all | solution.py:414
  118.6 0.2 broadcast_in_dim.8
  118.8 29.9 %all_to_all.32 = bf16[16,128,512]{2,1,0:T(8,128)(2,1)S(1)} all-to-all(bf16[16,128,512]{2,1,0:T(8,128)(2,1)S(1)} %broadcast_in_dim.8), channel_id=1, replica_groups=mesh['yh'=4,'yl'=2,'zl'=2,'x'=4,'zh'=4,'c'=2] {'zl','yl','x'}, dimensions={0} | all-to-all | bytes 4194304 | tf_op jit(solution)/shard_map/all_to_all | solution.py:417
  148.7 3.6 %final.1 = (f32[2048,384]{1,0:T(8,128)}, f32[128,2048]{1,0:T(8,128)}) custom-call(bf16[2,2,4,128,512]{4,3,2,1,0:T(8,128)(2,1)S(1)} %bitcast.6), custom_call_target="tpu_custom_call" | custom-call | tf_op jit(solution)/shard_map/final/pallas_call | solution.py:420
  (7 shorter events, 0.1 us)
Async XLA Ops:
  0.6 15.2 %copy-start.2 = (s32[128,1]{0,1:T(1,128)S(1)}, s32[128,1]{0,1:T(1,128)}, u32[]{:S(2)}) copy-start(s32[128,1]{0,1:T(1,128)} %param.23) | copy-start | bytes 1540
  3.3 37.6 %all-to-all-start = ((bf16[64,56,128]{2,1,0:T(8,128)(2,1)}), bf16[64,56,128]{2,1,0:T(8,128)(2,1)S(1)}, u32[]{:S(2)}, u32[]{:S(2)}) async-start(bf16[64,56,128]{2,1,0:T(8,128)(2,1)} %pack.1), calls=%async_computation | async-start | bytes 1835008 | tf_op jit(solution)/shard_map/all_to_all | solution.py:334
  25.5 26.8 %collective-permute-start = (bf16[3,512,128]{2,1,0:T(8,128)(2,1)}, bf16[3,512,128]{2,1,0:T(8,128)(2,1)S(1)}, u32[]{:S(2)}, u32[]{:S(2)}) collective-permute-start(bf16[3,512,128]{2,1,0:T(8,128)(2,1)} %get-tuple-element.8), channel_id=1, source_target_pairs={{0,8},{8,16},{16,24},{24,0},{1,9},{9,17},{17,25},{25,1},{2,10},{10... | collective-permute-start | bytes 1179656 | tf_op jit(solution)/shard_map/ppermute | solution.py:385
  28.8 23.4 %collective-permute-start.1 = (bf16[3,512,128]{2,1,0:T(8,128)(2,1)}, bf16[3,512,128]{2,1,0:T(8,128)(2,1)S(1)}, u32[]{:S(2)}, u32[]{:S(2)}) collective-permute-start(bf16[3,512,128]{2,1,0:T(8,128)(2,1)} %get-tuple-element.9), channel_id=1, source_target_pairs={{0,16},{8,24},{16,0},{24,8},{1,17},{9,25},{17,1},{25,9},{2,18},{10... | collective-permute-start | bytes 1179656 | tf_op jit(solution)/shard_map/ppermute | solution.py:385
  31.8 21.8 %collective-permute-start.2 = (bf16[3,512,128]{2,1,0:T(8,128)(2,1)}, bf16[3,512,128]{2,1,0:T(8,128)(2,1)S(1)}, u32[]{:S(2)}, u32[]{:S(2)}) collective-permute-start(bf16[3,512,128]{2,1,0:T(8,128)(2,1)} %get-tuple-element.10), channel_id=1, source_target_pairs={{0,24},{8,0},{16,8},{24,16},{1,25},{9,1},{17,9},{25,17},{2,26},{10... | collective-permute-start | bytes 1179656 | tf_op jit(solution)/shard_map/ppermute | solution.py:385
  40.9 1.0 copy-start.1
  42.9 20.1 %all-to-all-start.1 = ((bf16[8,16,640]{2,1,0:T(8,128)(2,1)}), bf16[8,16,640]{2,1,0:T(8,128)(2,1)S(1)}, u32[]{:S(2)}, u32[]{:S(2)}) async-start(bf16[8,16,640]{2,1,0:T(8,128)(2,1)} %bitcast.1), calls=%async_computation.1 | async-start | bytes 327680 | tf_op jit(solution)/shard_map/all_to_all | solution.py:388
  63.9 19.0 %all-to-all-start.2 = ((bf16[32,16,384]{2,1,0:T(8,128)(2,1)}), bf16[32,16,384]{2,1,0:T(8,128)(2,1)S(1)}, u32[]{:S(2)}, u32[]{:S(2)}) async-start(bf16[32,16,384]{2,1,0:T(8,128)(2,1)} %merge.1), calls=%async_computation.2 | async-start | bytes 786432 | tf_op jit(solution)/shard_map/all_to_all | solution.py:396
  82.9 1.0 copy-start

commit v6 on v5

--- a/solution.py
+++ b/solution.py
@@ -175,21 +175,25 @@
     out[...] = rows[...].astype(BF)
 
 
-def pick_kernel(received, partial, out):
-    count = partial.shape[0]
-    peers = received.shape[0]
-    tail = received[:, received.shape[1] - 8 :, :].astype(F32).reshape(peers * 8, RANK).astype(BF)
+def ready_kernel(partial, base, chosen):
     notes = partial[:, 3 * RANK :]
     place = (notes[:, 6:7] * 8.0 + notes[:, 7:8]).astype(jnp.int32)
-    chosen = place == iota((count, peers * 8), 1)
-    out[:, : 3 * RANK] = partial[:, : 3 * RANK].astype(BF)
-    out[:, 3 * RANK : 4 * RANK] = dot(chosen.astype(BF), tail).astype(BF)
+    chosen[...] = (place == iota(chosen.shape, 1)).astype(BF)
+    base[:, : 3 * RANK] = partial[:, : 3 * RANK].astype(BF)
     rough = notes.astype(BF).astype(F32)
     lane = iota(notes.shape, 1)
     for i in range(3):
         rest = notes[:, i : i + 1] - rough[:, i : i + 1]
         rough = jnp.where(lane == 3 + i, rest, rough)
-    out[:, 4 * RANK :] = rough.astype(BF)
+    base[:, 3 * RANK :] = rough.astype(BF)
+
+
+def pick_kernel(received, base, chosen, out):
+    peers = received.shape[0]
+    tail = received[:, received.shape[1] - 8 :, :].astype(F32).reshape(peers * 8, RANK).astype(BF)
+    out[:, : 3 * RANK] = base[:, : 3 * RANK]
+    out[:, 3 * RANK : 4 * RANK] = dot(chosen[...], tail).astype(BF)
+    out[:, 4 * RANK :] = base[:, 3 * RANK :]
 
 
 def merge_kernel(parts, *refs):
@@ -256,10 +260,15 @@
 
 
 def final_kernel(parts, down, up):
-    for b in range(up.shape[1] // RANK):
-        rows = slice(b * RANK, (b + 1) * RANK)
-        down[rows, :] = parts[0, b, 0, :, : 3 * RANK].astype(F32)
-        up[:, rows] = parts[0, b, 0, :, 3 * RANK :].astype(F32)
+    piece = parts.shape[3]
+    for y in range(parts.shape[2]):
+        for z in range(parts.shape[0]):
+            start = (y * parts.shape[0] + z) * piece
+            block, rank = start // RANK, start % RANK
+            down[start : start + piece, :] = parts[z, 0, y, :, : 3 * RANK].astype(F32)
+            up[rank : rank + piece, block * RANK : (block + 1) * RANK] = parts[
+                z, 0, y, :, 3 * RANK :
+            ].astype(F32)
 
 
 def whole(shape):
@@ -310,9 +319,8 @@
 ):
     count, width = low_hidden.shape
     branches = parents.shape[0]
-    nyh, nyl, nzl = lax.axis_size("yh"), lax.axis_size("yl"), lax.axis_size("zl")
-    nzh, nc = lax.axis_size("zh"), lax.axis_size("c")
-    peers = nyh * nyl * nzl * NX
+    ny, nzl, nh = lax.axis_size("y"), lax.axis_size("zl"), lax.axis_size("head")
+    peers = ny * nzl * NX
     block = width // NX
     place = lax.axis_index("x").astype(jnp.int32).reshape(1)
     smem = pl.BlockSpec(memory_space=pltpu.SMEM)
@@ -321,17 +329,22 @@
     cache_block = pl.BlockSpec((together, CACHE, HEAD_DIM), lambda b: (b, 0, 0))
 
     height = block // RANK * NX * MOST + 8
-    packed = call(
+    steps = 4
+    some = peers // steps
+    packed = pl.pallas_call(
         pack_kernel,
-        "pack",
-        shape((peers, height, RANK)),
-        out_grad,
-        merge_up,
-        scratch=[((peers, height, RANK), F32)],
-        grid=(1,),
-        limit=60,
-    )
-    received = lax.all_to_all(packed, ("yh", "yl", "zl", "x"), 0, 0, tiled=True)
+        grid=(steps,),
+        in_specs=[
+            pl.BlockSpec((out_grad.shape[0] // steps, width), lambda i: (i, 0)),
+            whole(merge_up.shape),
+        ],
+        out_specs=pl.BlockSpec((some, height, RANK), lambda i: (i, 0, 0)),
+        out_shape=shape((peers, height, RANK)),
+        scratch_shapes=[pltpu.VMEM((some, height, RANK), F32)],
+        compiler_params=params(60),
+        name="pack",
+    )(out_grad, merge_up)
+    received = lax.all_to_all(packed, ("y", "zl", "x"), 0, 0, tiled=True)
     *turned, partial = pl.pallas_call(
         feature_kernel,
         grid=(branches // together,),
@@ -383,17 +396,20 @@
     )
     for k in range(1, NX):
         turned[k] = lax.ppermute(turned[k], "x", [(i, (i + k) % NX) for i in range(NX)])
-    sent = call(pick_kernel, "pick", shape((count, 5 * RANK)), received, partial)
-    share = count // (nzh * nc)
-    parts = lax.all_to_all(sent.reshape(nzh * nc, share, 5 * RANK), ("zh", "c"), 0, 0, tiled=True)
+    base, chosen = call(
+        ready_kernel, "ready", [shape((count, 4 * RANK)), shape((count, peers * 8))], partial
+    )
+    sent = call(pick_kernel, "pick", shape((count, 5 * RANK)), received, base, chosen)
+    share = count // nh
+    parts = lax.all_to_all(sent.reshape(nh, share, 5 * RANK), "head", 0, 0, tiled=True)
     merged = call(
         merge_kernel,
         "merge",
-        shape((NX * nzh * nc, share, 3 * RANK)),
+        shape((NX * nh, share, 3 * RANK)),
         parts,
         unread=turned[1:],
     )
-    merged = lax.all_to_all(merged, ("x", "zh", "c"), 0, 0, tiled=True)
+    merged = lax.all_to_all(merged, ("x", "head"), 0, 0, tiled=True)
     merged = merged.reshape(NX, count, 3 * RANK)
     slots = call(
         unpack_kernel,
@@ -402,32 +418,36 @@
         received,
         scratch=[((peers * NX * MOST, block), F32)],
     )
-    grads = call(
-        grads_kernel, "grads", shape((block, 4 * RANK)), place, *turned, slots, merged
-    )
-    piece = block // (nzl * nyl * nyh)
+    grads = call(grads_kernel, "grads", shape((block, 4 * RANK)), place, *turned, slots, merged)
+    piece = block // (ny * nzl)
     grads = lax.all_to_all(
-        grads.reshape(nzl * nyl * nyh, piece, 4 * RANK), ("zl", "yl", "yh"), 0, 0, tiled=True
-    )
-    grads = call(sum_kernel, "total", shape((nyh, piece, 4 * RANK)), grads)
-    rows = nyh * piece
-    grads = lax.all_to_all(grads, "yh", 0, 0, tiled=True).reshape(rows, 4 * RANK)
-    near = nzl * nyl
-    grads = jnp.broadcast_to(grads[None], (near * NX, rows, 4 * RANK))
-    grads = lax.all_to_all(grads, ("zl", "yl", "x"), 0, 0, tiled=True)
-    grads = grads.reshape(nzl, nyl, NX, rows, 4 * RANK)
-    step = nyl * rows
+        grads.reshape(ny * nzl, piece, 4 * RANK), ("y", "zl"), 0, 0, tiled=True
+    )
+    return call(sum_kernel, "total", shape((ny, piece, 4 * RANK)), grads)
+
+
+def gather(grads, width):
+    ny, piece, lanes = grads.shape
+    nzx = lax.axis_size("zx")
+    nzl = nzx // NX
+    grads = lax.all_to_all(grads, "y", 0, 0, tiled=True).reshape(ny * piece, lanes)
+    grads = jnp.broadcast_to(grads[None], (nzx, ny * piece, lanes))
+    grads = lax.all_to_all(grads, "zx", 0, 0, tiled=True)
+    grads = grads.reshape(nzl, NX, ny, piece, lanes)
+    part = 2
+    few = ny // part
+    rows = few * nzl * piece
     return pl.pallas_call(
         final_kernel,
-        grid=(nzl * NX,),
+        grid=(NX * part,),
         in_specs=[
             pl.BlockSpec(
-                (1, nyl, 1, rows, 4 * RANK), lambda i: (i % nzl, 0, i // nzl, 0, 0)
+                (nzl, 1, few, piece, lanes), lambda i: (0, i // part, i % part, 0, 0)
             )
         ],
         out_specs=[
-            pl.BlockSpec((step, 3 * RANK), lambda i: (i, 0)),
-            pl.BlockSpec((RANK, step), lambda i: (0, i)),
+            pl.BlockSpec((rows, 3 * RANK), lambda i: (i, 0)),
+            pl.BlockSpec((RANK, rows), lambda i: (0, i)),
         ],
         out_shape=[shape((width, 3 * RANK), F32), shape((RANK, width), F32)],
         compiler_params=params(),
@@ -436,8 +456,9 @@
 
 
 def solution(mesh):
-    fine = Mesh(mesh.devices.reshape(4, 2, 2, NX, 4, 2), ("yh", "yl", "zl", "x", "zh", "c"))
-    dp, head = ("yh", "yl", "zl", "x"), ("zh", "c")
+    fine = Mesh(mesh.devices.reshape(8, 2, NX, 8), ("y", "zl", "x", "head"))
+    coarse = Mesh(mesh.devices.reshape(8, 2 * NX, 8), ("y", "zx", "head"))
+    dp, head = ("y", "zl", "x"), "head"
     placed = (
         P(dp, head),
         P(dp, head),
@@ -455,10 +476,18 @@
         P(None, head),
         P(dp, head),
     )
-    return jax.shard_map(
-        body,
-        mesh=fine,
-        in_specs=placed,
-        out_specs=(P(head, None), P(None, head)),
-        check_vma=False,
-    )
+    own_sums = jax.shard_map(
+        body, mesh=fine, in_specs=placed, out_specs=P((*dp, head)), check_vma=False
+    )
+
+    def whole_program(*args):
+        width = args[9].shape[1] // mesh.shape["head"]
+        return jax.shard_map(
+            lambda sums: tuple(gather(sums, width)),
+            mesh=coarse,
+            in_specs=P(("y", "zx", "head")),
+            out_specs=(P("head", None), P(None, "head")),
+            check_vma=False,
+        )(own_sums(*args))
+
+    return whole_program

time: 153 us -> 157 us (1.026)
  blocking collectives: 63.2 us -> 66.8 us
    pallas_call x1 -> x2, Pallas kernels: 3.55 us -> 7.7 us  [the longest x1 4.13 us: body(): pl.pallas_call(pack_kernel, grid=(steps,), in_specs=[pl.BlockSpec((out_gr...]
    all_to_all x3, blocking collectives: 63.2 us -> 66.8 us  [the longest x1 28.4 us: gather(): grads = lax.all_to_all(grads, 'zx', 0, 0, tiled=True)]
    pallas_call x6, Pallas kernels: 6.31 us -> 3.7 us  [call(): pl.pallas_call(kernel, grid=grid, in_specs=specs, out_specs=outs if isins...]
    all_to_all x3, waiting for transfers between devices: 27.9 us -> 25.6 us  [the longest x1 13.6 us: body(): merged = lax.all_to_all(merged, ('x', 'head'), 0, 0, tiled=True)]
where the time goes in v6:
time: 157 us; the launch traced here: 156 us
  blocking collectives  66.8 us (43%)
  starting transfers between devices  37.5 us (24%)
  waiting for transfers between devices  28.1 us (18%)
  Pallas kernels  20.3 us (13%)
  local copies, waits for them, and re-layouts  2.85 us (2%)
    all_to_all x1, blocking collectives, gather(): grads = lax.all_to_all(grads, 'zx', 0, 0, tiled=True)  28.4 us
    all_to_all x1, blocking collectives, body(): lax.all_to_all(grads.reshape(ny * nzl, piece, 4 * RANK), ('y', 'zl'), 0,...  22.3 us
    all_to_all x1, blocking collectives, gather(): lax.all_to_all(grads, 'y', 0, 0, tiled=True).reshape(ny * piece, lanes)  16.1 us
    all_to_all x1, waiting for transfers between devices, body(): merged = lax.all_to_all(merged, ('x', 'head'), 0, 0, tiled=True)  13.6 us
    all_to_all x1, starting transfers between devices, body(): received = lax.all_to_all(packed, ('y', 'zl', 'x'), 0, 0, tiled=True)  12.5 us
    ppermute x3, starting transfers between devices, body(): lax.ppermute(turned[k], 'x', [(i, (i + k) % NX) for i in range(NX)])  10.4 us
    all_to_all x1, starting transfers between devices, body(): lax.all_to_all(sent.reshape(nh, share, 5 * RANK), 'head', 0, 0, tiled=True)  9.41 us
    pallas_call x1, Pallas kernels, body(): pl.pallas_call(feature_kernel, grid=(branches // together,), in_specs=[sm...  8.88 us
  transfers between devices with their start and end apart: 6, of which 4 were waited for; matrix products, arithmetic and copies ran while one was open for 0% of the time, Pallas kernels for 7%

profile of v6, /device:TPU:2, one launch (start us, length us, event | category | flops | bytes accessed | tf_op | source)
XLA Modules:
  0.0 156.2 jit_solution(1036346817933467949)
XLA Ops:
  0.6 4.1 %pack.1 = bf16[64,56,128]{2,1,0:T(8,128)(2,1)} custom-call(bf16[192,2048]{1,0:T(8,128)(2,1)} %grads.2, bf16[128,2048]{1,0:T(8,128)(2,1)} %merge_up.1), custom_call_target="tpu_custom_call" | custom-call | tf_op jit(solution)/shard_map/pack/pallas_call | solution.py:334
  4.8 12.5 %all-to-all-start = ((bf16[64,56,128]{2,1,0:T(8,128)(2,1)}), bf16[64,56,128]{2,1,0:T(8,128)(2,1)S(1)}, u32[]{:S(2)}, u32[]{:S(2)}) async-start(bf16[64,56,128]{2,1,0:T(8,128)(2,1)} %pack.1), calls=%async_computation | async-start | bytes 1835008 | tf_op jit(solution)/shard_map/all_to_all | solution.py:347
  17.3 0.7 copy.19.targets
  18.0 8.9 %features.1 = (bf16[3,512,128]{2,1,0:T(8,128)(2,1)}, bf16[3,512,128]{2,1,0:T(8,128)(2,1)}, bf16[3,512,128]{2,1,0:T(8,128)(2,1)}, bf16[3,512,128]{2,1,0:T(8,128)(2,1)}, f32[128,512]{1,0:T(8,128)}) custom-call(s32[1]{0:T(128)} %bitcast.place, s32[8]{0:T(128)} %lengths.1, s32[8]{0:T(128)} %counts.1, s32[128,1]{1,0:T(8,128)} %copy.19.targets, s32[8,16]{1,0:T(8,128)} %parents.1, ...), custom_call_target="tpu_custom_call" | custom-call | flops 400000000 | bytes 8000000 | tf_op jit(solution)/shard_map/features/pallas_call | solution.py:348
  26.9 3.4 %collective-permute-start = (bf16[3,512,128]{2,1,0:T(8,128)(2,1)}, bf16[3,512,128]{2,1,0:T(8,128)(2,1)S(1)}, u32[]{:S(2)}, u32[]{:S(2)}) collective-permute-start(bf16[3,512,128]{2,1,0:T(8,128)(2,1)} %get-tuple-element.11), channel_id=1, source_target_pairs={{0,8},{8,16},{16,24},{24,0},{1,9},{9,17},{17,25},{25,1},{2,10},{10... | collective-permute-start | bytes 1179656 | tf_op jit(solution)/shard_map/ppermute | solution.py:398
  30.3 3.0 %collective-permute-start.1 = (bf16[3,512,128]{2,1,0:T(8,128)(2,1)}, bf16[3,512,128]{2,1,0:T(8,128)(2,1)S(1)}, u32[]{:S(2)}, u32[]{:S(2)}) collective-permute-start(bf16[3,512,128]{2,1,0:T(8,128)(2,1)} %get-tuple-element.12), channel_id=1, source_target_pairs={{0,16},{8,24},{16,0},{24,8},{1,17},{9,25},{17,1},{25,9},{2,18},{10... | collective-permute-start | bytes 1179656 | tf_op jit(solution)/shard_map/ppermute | solution.py:398
  33.2 4.1 %collective-permute-start.2 = (bf16[3,512,128]{2,1,0:T(8,128)(2,1)}, bf16[3,512,128]{2,1,0:T(8,128)(2,1)S(1)}, u32[]{:S(2)}, u32[]{:S(2)}) collective-permute-start(bf16[3,512,128]{2,1,0:T(8,128)(2,1)} %get-tuple-element.13), channel_id=1, source_target_pairs={{0,24},{8,0},{16,8},{24,16},{1,25},{9,1},{17,9},{25,17},{2,26},{10... | collective-permute-start | bytes 1179656 | tf_op jit(solution)/shard_map/ppermute | solution.py:398
  37.3 0.9 copy-done.1
  38.3 0.2 ready.1
  38.5 3.8 %all-to-all-done.received = bf16[64,56,128]{2,1,0:T(8,128)(2,1)S(1)} async-done(((bf16[64,56,128]{2,1,0:T(8,128)(2,1)}), bf16[64,56,128]{2,1,0:T(8,128)(2,1)S(1)}, u32[]{:S(2)}, u32[]{:S(2)}) %all-to-all-start) | async-done | bytes 917536 | tf_op jit(solution)/shard_map/all_to_all | solution.py:347
  42.3 0.8 pick.1
  43.2 9.4 %all-to-all-start.1 = ((bf16[8,16,640]{2,1,0:T(8,128)(2,1)}), bf16[8,16,640]{2,1,0:T(8,128)(2,1)S(1)}, u32[]{:S(2)}, u32[]{:S(2)}) async-start(bf16[8,16,640]{2,1,0:T(8,128)(2,1)} %bitcast.1), calls=%async_computation.1 | async-start | bytes 327680 | tf_op jit(solution)/shard_map/all_to_all | solution.py:404
  52.6 2.5 %collective-permute-done.2.refs_2_.third = bf16[3,512,128]{2,1,0:T(8,128)(2,1)S(1)} collective-permute-done((bf16[3,512,128]{2,1,0:T(8,128)(2,1)}, bf16[3,512,128]{2,1,0:T(8,128)(2,1)S(1)}, u32[]{:S(2)}, u32[]{:S(2)}) %collective-permute-start.2) | collective-permute-done | bytes 393248 | tf_op jit(solution)/shard_map/ppermute | solution.py:398
  55.1 8.2 %all-to-all-done.1.parts = bf16[8,16,640]{2,1,0:T(8,128)(2,1)S(1)} async-done(((bf16[8,16,640]{2,1,0:T(8,128)(2,1)}), bf16[8,16,640]{2,1,0:T(8,128)(2,1)S(1)}, u32[]{:S(2)}, u32[]{:S(2)}) %all-to-all-start.1) | async-done | bytes 163872 | tf_op jit(solution)/shard_map/all_to_all | solution.py:404
  63.2 0.9 merge.1
  64.2 5.2 %all-to-all-start.2 = ((bf16[32,16,384]{2,1,0:T(8,128)(2,1)}), bf16[32,16,384]{2,1,0:T(8,128)(2,1)S(1)}, u32[]{:S(2)}, u32[]{:S(2)}) async-start(bf16[32,16,384]{2,1,0:T(8,128)(2,1)} %merge.1), calls=%async_computation.2 | async-start | bytes 786432 | tf_op jit(solution)/shard_map/all_to_all | solution.py:412
  69.4 0.2 unpack.1.slots
  69.6 13.6 %all-to-all-done.2 = bf16[32,16,384]{2,1,0:T(8,128)(2,1)S(1)} async-done(((bf16[32,16,384]{2,1,0:T(8,128)(2,1)}), bf16[32,16,384]{2,1,0:T(8,128)(2,1)S(1)}, u32[]{:S(2)}, u32[]{:S(2)}) %all-to-all-start.2) | async-done | bytes 393248 | tf_op jit(solution)/shard_map/all_to_all | solution.py:412
  83.2 1.0 copy-done
  84.2 1.4 grads.3
  85.6 22.3 %all_to_all.30.parts = bf16[16,32,512]{2,1,0:T(8,128)(2,1)S(1)} all-to-all(bf16[16,32,512]{2,1,0:T(8,128)(2,1)S(1)} %bitcast.7), channel_id=1, replica_groups=mesh['y'=8,'zl'=2,'x'=4,'head'=8] {'y','zl'}, dimensions={0} | all-to-all | bytes 1048576 | tf_op jit(solution)/shard_map/all_to_all | solution.py:423
  108.0 16.1 %all_to_all.31 = bf16[8,32,512]{2,1,0:T(8,128)(2,1)S(1)} all-to-all(bf16[8,32,512]{2,1,0:T(8,128)(2,1)S(1)} %total.1), channel_id=1, replica_groups=mesh['y'=8,'zl'=2,'x'=4,'head'=8] {'y'}, dimensions={0} | all-to-all | bytes 524288 | tf_op jit(solution)/shard_map/all_to_all | solution.py:433
  124.3 28.4 %all_to_all.32 = bf16[8,256,512]{2,1,0:T(8,128)(2,1)S(1)} all-to-all(bf16[8,256,512]{2,1,0:T(8,128)(2,1)S(1)} %broadcast_in_dim.8), channel_id=1, replica_groups=mesh['y'=8,'zl'=2,'x'=4,'head'=8] {'zl','x'}, dimensions={0} | all-to-all | bytes 4194304 | tf_op jit(solution)/shard_map/all_to_all | solution.py:435
  152.6 3.6 %final.1 = (f32[2048,384]{1,0:T(8,128)}, f32[128,2048]{1,0:T(8,128)}) custom-call(bf16[2,4,8,32,512]{4,3,2,1,0:T(8,128)(2,1)S(1)} %bitcast.6), custom_call_target="tpu_custom_call" | custom-call | tf_op jit(solution)/shard_map/final/pallas_call | solution.py:440
  (8 shorter events, 0.3 us)
Async XLA Ops:
  0.6 16.6 %copy-start.2 = (s32[128,1]{0,1:T(1,128)S(1)}, s32[128,1]{0,1:T(1,128)}, u32[]{:S(2)}) copy-start(s32[128,1]{0,1:T(1,128)} %param.24) | copy-start | bytes 1540
  4.8 37.6 %all-to-all-start = ((bf16[64,56,128]{2,1,0:T(8,128)(2,1)}), bf16[64,56,128]{2,1,0:T(8,128)(2,1)S(1)}, u32[]{:S(2)}, u32[]{:S(2)}) async-start(bf16[64,56,128]{2,1,0:T(8,128)(2,1)} %pack.1), calls=%async_computation | async-start | bytes 1835008 | tf_op jit(solution)/shard_map/all_to_all | solution.py:347
  26.9 25.7 %collective-permute-start = (bf16[3,512,128]{2,1,0:T(8,128)(2,1)}, bf16[3,512,128]{2,1,0:T(8,128)(2,1)S(1)}, u32[]{:S(2)}, u32[]{:S(2)}) collective-permute-start(bf16[3,512,128]{2,1,0:T(8,128)(2,1)} %get-tuple-element.11), channel_id=1, source_target_pairs={{0,8},{8,16},{16,24},{24,0},{1,9},{9,17},{17,25},{25,1},{2,10},{10... | collective-permute-start | bytes 1179656 | tf_op jit(solution)/shard_map/ppermute | solution.py:398
  30.3 22.4 %collective-permute-start.1 = (bf16[3,512,128]{2,1,0:T(8,128)(2,1)}, bf16[3,512,128]{2,1,0:T(8,128)(2,1)S(1)}, u32[]{:S(2)}, u32[]{:S(2)}) collective-permute-start(bf16[3,512,128]{2,1,0:T(8,128)(2,1)} %get-tuple-element.12), channel_id=1, source_target_pairs={{0,16},{8,24},{16,0},{24,8},{1,17},{9,25},{17,1},{25,9},{2,18},{10... | collective-permute-start | bytes 1179656 | tf_op jit(solution)/shard_map/ppermute | solution.py:398
  33.2 21.8 %collective-permute-start.2 = (bf16[3,512,128]{2,1,0:T(8,128)(2,1)}, bf16[3,512,128]{2,1,0:T(8,128)(2,1)S(1)}, u32[]{:S(2)}, u32[]{:S(2)}) collective-permute-start(bf16[3,512,128]{2,1,0:T(8,128)(2,1)} %get-tuple-element.13), channel_id=1, source_target_pairs={{0,24},{8,0},{16,8},{24,16},{1,25},{9,1},{17,9},{25,17},{2,26},{10... | collective-permute-start | bytes 1179656 | tf_op jit(solution)/shard_map/ppermute | solution.py:398
  37.3 1.0 copy-start.1
  43.2 20.1 %all-to-all-start.1 = ((bf16[8,16,640]{2,1,0:T(8,128)(2,1)}), bf16[8,16,640]{2,1,0:T(8,128)(2,1)S(1)}, u32[]{:S(2)}, u32[]{:S(2)}) async-start(bf16[8,16,640]{2,1,0:T(8,128)(2,1)} %bitcast.1), calls=%async_computation.1 | async-start | bytes 327680 | tf_op jit(solution)/shard_map/all_to_all | solution.py:404
  64.2 19.0 %all-to-all-start.2 = ((bf16[32,16,384]{2,1,0:T(8,128)(2,1)}), bf16[32,16,384]{2,1,0:T(8,128)(2,1)S(1)}, u32[]{:S(2)}, u32[]{:S(2)}) async-start(bf16[32,16,384]{2,1,0:T(8,128)(2,1)} %merge.1), calls=%async_computation.2 | async-start | bytes 786432 | tf_op jit(solution)/shard_map/all_to_all | solution.py:412
  83.2 1.0 copy-start

commit v7 on v5

--- a/solution.py
+++ b/solution.py
@@ -163,33 +163,44 @@
     out[...] = rows[...].astype(BF)
 
 
-def unpack_kernel(received, out, rows):
+def unpack_kernel(received, own, first, second, third, out, rows):
     peers = received.shape[0]
-    slots = out.shape[0] // peers
+    count, block = rows.shape
+    slots = count // peers
     for j in range(peers):
         wide = received[j].astype(F32)
-        for b in range(out.shape[1] // RANK):
+        for b in range(block // RANK):
             rows[j * slots : (j + 1) * slots, b * RANK : (b + 1) * RANK] = wide[
                 b * slots : (b + 1) * slots, :
             ]
-    out[...] = rows[...].astype(BF)
-
-
-def pick_kernel(received, partial, out):
-    count = partial.shape[0]
-    peers = received.shape[0]
-    tail = received[:, received.shape[1] - 8 :, :].astype(F32).reshape(peers * 8, RANK).astype(BF)
+    out[:count, :] = rows[...].astype(BF)
+    for k, turned in enumerate((own, first, second, third)):
+        for layer in range(3):
+            start = count + (k * 3 + layer) * RANK
+            for b in range(block // RANK):
+                columns = slice(b * RANK, (b + 1) * RANK)
+                out[start : start + RANK, columns] = turned[layer, columns, :]
+
+
+def ready_kernel(partial, base, chosen):
     notes = partial[:, 3 * RANK :]
     place = (notes[:, 6:7] * 8.0 + notes[:, 7:8]).astype(jnp.int32)
-    chosen = place == iota((count, peers * 8), 1)
-    out[:, : 3 * RANK] = partial[:, : 3 * RANK].astype(BF)
-    out[:, 3 * RANK : 4 * RANK] = dot(chosen.astype(BF), tail).astype(BF)
+    chosen[...] = (place == iota(chosen.shape, 1)).astype(BF)
+    base[:, : 3 * RANK] = partial[:, : 3 * RANK].astype(BF)
     rough = notes.astype(BF).astype(F32)
     lane = iota(notes.shape, 1)
     for i in range(3):
         rest = notes[:, i : i + 1] - rough[:, i : i + 1]
         rough = jnp.where(lane == 3 + i, rest, rough)
-    out[:, 4 * RANK :] = rough.astype(BF)
+    base[:, 3 * RANK :] = rough.astype(BF)
+
+
+def pick_kernel(received, base, chosen, out):
+    peers = received.shape[0]
+    tail = received[:, received.shape[1] - 8 :, :].astype(F32).reshape(peers * 8, RANK).astype(BF)
+    out[:, : 3 * RANK] = base[:, : 3 * RANK]
+    out[:, 3 * RANK : 4 * RANK] = dot(chosen[...], tail).astype(BF)
+    out[:, 4 * RANK :] = base[:, 3 * RANK :]
 
 
 def merge_kernel(parts, *refs):
@@ -222,28 +233,37 @@
         out[peer, :, 2 * RANK :] = notes
 
 
-def grads_kernel(place, own, first, second, third, slots, merged, out):
+def grads_kernel(place, slots, merged, out):
     blocks = slots.shape[1] // RANK
+    count = slots.shape[0] - NX * 3 * RANK
     peer_slots = NX * MOST
     down = [None] * 3
     placed = None
-    for k, turned in enumerate((own, first, second, third)):
+    for k in range(NX):
         source = (place[0] + NX - k) % NX
         rows = merged[source]
         notes = rows[:, 2 * RANK :].astype(F32)
         grad = rows[:, :RANK].astype(F32)
         for i in range(3):
             inverse = notes[:, i : i + 1] + notes[:, 3 + i : 4 + i]
-            term = dot(turned[i], (inverse * grad).astype(BF))
+            start = count + (k * 3 + i) * RANK
+            turned = jnp.concatenate(
+                [
+                    slots[start : start + RANK, b * RANK : (b + 1) * RANK]
+                    for b in range(blocks)
+                ],
+                axis=0,
+            )
+            term = dot(turned, (inverse * grad).astype(BF))
             down[i] = term if down[i] is None else down[i] + term
         slot = notes[:, 6:7].astype(jnp.int32) * peer_slots + notes[:, 7:8].astype(jnp.int32)
         slot = slot + source * MOST
-        chosen = (slot == iota((rows.shape[0], slots.shape[0]), 1)).astype(BF)
+        chosen = (slot == iota((rows.shape[0], count), 1)).astype(BF)
         term = dot_tn(rows[:, RANK : 2 * RANK], chosen)
         placed = term if placed is None else placed + term
     for i in range(3):
         out[:, i * RANK : (i + 1) * RANK] = down[i].astype(BF)
-    up = dot(placed.astype(BF), slots[...]).astype(BF)
+    up = dot(placed.astype(BF), slots[:count, :]).astype(BF)
     for b in range(blocks):
         out[b * RANK : (b + 1) * RANK, 3 * RANK :] = up[:, b * RANK : (b + 1) * RANK]
 
@@ -256,10 +276,12 @@
 
 
 def final_kernel(parts, down, up):
+    step = pl.program_id(0)
+    z, x = step % parts.shape[0], step // parts.shape[0]
     for b in range(up.shape[1] // RANK):
         rows = slice(b * RANK, (b + 1) * RANK)
-        down[rows, :] = parts[0, b, 0, :, : 3 * RANK].astype(F32)
-        up[:, rows] = parts[0, b, 0, :, 3 * RANK :].astype(F32)
+        down[rows, :] = parts[z, b, x, :, : 3 * RANK].astype(F32)
+        up[:, rows] = parts[z, b, x, :, 3 * RANK :].astype(F32)
 
 
 def whole(shape):
@@ -383,7 +405,10 @@
     )
     for k in range(1, NX):
         turned[k] = lax.ppermute(turned[k], "x", [(i, (i + k) % NX) for i in range(NX)])
-    sent = call(pick_kernel, "pick", shape((count, 5 * RANK)), received, partial)
+    base, chosen = call(
+        ready_kernel, "ready", [shape((count, 4 * RANK)), shape((count, peers * 8))], partial
+    )
+    sent = call(pick_kernel, "pick", shape((count, 5 * RANK)), received, base, chosen)
     share = count // (nzh * nc)
     parts = lax.all_to_all(sent.reshape(nzh * nc, share, 5 * RANK), ("zh", "c"), 0, 0, tiled=True)
     merged = call(
@@ -398,13 +423,12 @@
     slots = call(
         unpack_kernel,
         "unpack",
-        shape((peers * NX * MOST, block)),
+        shape((peers * NX * MOST + NX * 3 * RANK, block)),
         received,
+        *turned,
         scratch=[((peers * NX * MOST, block), F32)],
     )
-    grads = call(
-        grads_kernel, "grads", shape((block, 4 * RANK)), place, *turned, slots, merged
-    )
+    grads = call(grads_kernel, "grads", shape((block, 4 * RANK)), place, slots, merged)
     piece = block // (nzl * nyl * nyh)
     grads = lax.all_to_all(
         grads.reshape(nzl * nyl * nyh, piece, 4 * RANK), ("zl", "yl", "yh"), 0, 0, tiled=True
@@ -420,11 +444,7 @@
     return pl.pallas_call(
         final_kernel,
         grid=(nzl * NX,),
-        in_specs=[
-            pl.BlockSpec(
-                (1, nyl, 1, rows, 4 * RANK), lambda i: (i % nzl, 0, i // nzl, 0, 0)
-            )
-        ],
+        in_specs=[pl.BlockSpec(memory_space=pltpu.VMEM)],
         out_specs=[
             pl.BlockSpec((step, 3 * RANK), lambda i: (i, 0)),
             pl.BlockSpec((RANK, step), lambda i: (0, i)),

time: 153 us -> 153 us (level)
  waiting for transfers between devices: 29.3 us -> 23.8 us
  local copies, waits for them, and re-layouts: 2.88 us -> 5.87 us
    all_to_all x1, waiting for transfers between devices: 13.6 us -> 9.41 us  [body(): merged = lax.all_to_all(merged, ('x', 'zh', 'c'), 0, 0, tiled=True)]
    unnamed x7 -> x19, local copies, waits for them, and re-layouts: 2.68 us -> 5.67 us
    pallas_call x6 -> x7, Pallas kernels: 6.31 us -> 7.63 us  [call(): pl.pallas_call(kernel, grid=grid, in_specs=specs, out_specs=outs if isins...]
where the time goes in v7:
time: 153 us; the launch traced here: 152 us
  blocking collectives  64.2 us (42%)
  starting transfers between devices  37.5 us (25%)
  waiting for transfers between devices  23.8 us (16%)
  Pallas kernels  19.9 us (13%)
  local copies, waits for them, and re-layouts  5.87 us (4%)
    all_to_all x1, blocking collectives, body(): grads = lax.all_to_all(grads, ('zl', 'yl', 'x'), 0, 0, tiled=True)  29.8 us
    all_to_all x1, blocking collectives, body(): lax.all_to_all(grads.reshape(nzl * nyl * nyh, piece, 4 * RANK), ('zl', 'y...  20.4 us
    all_to_all x1, blocking collectives, body(): lax.all_to_all(grads, 'yh', 0, 0, tiled=True).reshape(rows, 4 * RANK)  13.9 us
    all_to_all x1, starting transfers between devices, body(): received = lax.all_to_all(packed, ('yh', 'yl', 'zl', 'x'), 0, 0, tiled=True)  12.5 us
    ppermute x3, starting transfers between devices, body(): lax.ppermute(turned[k], 'x', [(i, (i + k) % NX) for i in range(NX)])  10.4 us
    all_to_all x1, waiting for transfers between devices, body(): merged = lax.all_to_all(merged, ('x', 'zh', 'c'), 0, 0, tiled=True)  9.41 us
    all_to_all x1, starting transfers between devices, body(): lax.all_to_all(sent.reshape(nzh * nc, share, 5 * RANK), ('zh', 'c'), 0, 0...  9.41 us
    pallas_call x1, Pallas kernels, body(): pl.pallas_call(feature_kernel, grid=(branches // together,), in_specs=[sm...  8.87 us
  transfers between devices with their start and end apart: 6, of which 4 were waited for; matrix products, arithmetic and copies ran while one was open for 0% of the time, Pallas kernels for 7%

profile of v7, /device:TPU:2, one launch (start us, length us, event | category | flops | bytes accessed | tf_op | source)
XLA Modules:
  0.0 152.2 jit_solution(5189019100192380090)
XLA Ops:
  0.6 2.7 %pack.1 = bf16[64,56,128]{2,1,0:T(8,128)(2,1)} custom-call(bf16[192,2048]{1,0:T(8,128)(2,1)} %grads.2, bf16[128,2048]{1,0:T(8,128)(2,1)} %merge_up.1), custom_call_target="tpu_custom_call" | custom-call | flops 1000000 | bytes 2000000 | tf_op jit(solution)/shard_map/pack/pallas_call | solution.py:301
  3.3 12.5 %all-to-all-start = ((bf16[64,56,128]{2,1,0:T(8,128)(2,1)}), bf16[64,56,128]{2,1,0:T(8,128)(2,1)S(1)}, u32[]{:S(2)}, u32[]{:S(2)}) async-start(bf16[64,56,128]{2,1,0:T(8,128)(2,1)} %pack.1), calls=%async_computation | async-start | bytes 1835008 | tf_op jit(solution)/shard_map/all_to_all | solution.py:356
  16.5 8.9 %features.1 = (bf16[3,512,128]{2,1,0:T(8,128)(2,1)}, bf16[3,512,128]{2,1,0:T(8,128)(2,1)}, bf16[3,512,128]{2,1,0:T(8,128)(2,1)}, bf16[3,512,128]{2,1,0:T(8,128)(2,1)}, f32[128,512]{1,0:T(8,128)}) custom-call(s32[1]{0:T(128)} %bitcast.place, s32[8]{0:T(128)} %lengths.1, s32[8]{0:T(128)} %counts.1, s32[128,1]{1,0:T(8,128)} %copy.17.targets, s32[8,16]{1,0:T(8,128)} %parents.1, ...), custom_call_target="tpu_custom_call" | custom-call | flops 400000000 | bytes 8000000 | tf_op jit(solution)/shard_map/features/pallas_call | solution.py:357
  25.4 3.4 %collective-permute-start = (bf16[3,512,128]{2,1,0:T(8,128)(2,1)}, bf16[3,512,128]{2,1,0:T(8,128)(2,1)S(1)}, u32[]{:S(2)}, u32[]{:S(2)}) collective-permute-start(bf16[3,512,128]{2,1,0:T(8,128)(2,1)} %get-tuple-element.10), channel_id=1, source_target_pairs={{0,8},{8,16},{16,24},{24,0},{1,9},{9,17},{17,25},{25,1},{2,10},{10... | collective-permute-start | bytes 1179656 | tf_op jit(solution)/shard_map/ppermute | solution.py:407
  28.8 3.0 %collective-permute-start.1 = (bf16[3,512,128]{2,1,0:T(8,128)(2,1)}, bf16[3,512,128]{2,1,0:T(8,128)(2,1)S(1)}, u32[]{:S(2)}, u32[]{:S(2)}) collective-permute-start(bf16[3,512,128]{2,1,0:T(8,128)(2,1)} %get-tuple-element.11), channel_id=1, source_target_pairs={{0,16},{8,24},{16,0},{24,8},{1,17},{9,25},{17,1},{25,9},{2,18},{10... | collective-permute-start | bytes 1179656 | tf_op jit(solution)/shard_map/ppermute | solution.py:407
  31.8 4.1 %collective-permute-start.2 = (bf16[3,512,128]{2,1,0:T(8,128)(2,1)}, bf16[3,512,128]{2,1,0:T(8,128)(2,1)S(1)}, u32[]{:S(2)}, u32[]{:S(2)}) collective-permute-start(bf16[3,512,128]{2,1,0:T(8,128)(2,1)} %get-tuple-element.12), channel_id=1, source_target_pairs={{0,24},{8,0},{16,8},{24,16},{1,25},{9,1},{17,9},{25,17},{2,26},{10... | collective-permute-start | bytes 1179656 | tf_op jit(solution)/shard_map/ppermute | solution.py:407
  35.9 0.9 copy-done.7
  37.1 3.8 %all-to-all-done.received = bf16[64,56,128]{2,1,0:T(8,128)(2,1)S(1)} async-done(((bf16[64,56,128]{2,1,0:T(8,128)(2,1)}), bf16[64,56,128]{2,1,0:T(8,128)(2,1)S(1)}, u32[]{:S(2)}, u32[]{:S(2)}) %all-to-all-start) | async-done | bytes 917536 | tf_op jit(solution)/shard_map/all_to_all | solution.py:356
  40.9 0.8 pick.1
  41.7 9.4 %all-to-all-start.1 = ((bf16[8,16,640]{2,1,0:T(8,128)(2,1)}), bf16[8,16,640]{2,1,0:T(8,128)(2,1)S(1)}, u32[]{:S(2)}, u32[]{:S(2)}) async-start(bf16[8,16,640]{2,1,0:T(8,128)(2,1)} %bitcast.1), calls=%async_computation.1 | async-start | bytes 327680 | tf_op jit(solution)/shard_map/all_to_all | solution.py:413
  51.2 2.4 %collective-permute-done.2.third.refs_2_ = bf16[3,512,128]{2,1,0:T(8,128)(2,1)S(1)} collective-permute-done((bf16[3,512,128]{2,1,0:T(8,128)(2,1)}, bf16[3,512,128]{2,1,0:T(8,128)(2,1)S(1)}, u32[]{:S(2)}, u32[]{:S(2)}) %collective-permute-start.2) | collective-permute-done | bytes 393248 | tf_op jit(solution)/shard_map/ppermute | solution.py:407
  53.6 8.2 %all-to-all-done.1.parts = bf16[8,16,640]{2,1,0:T(8,128)(2,1)S(1)} async-done(((bf16[8,16,640]{2,1,0:T(8,128)(2,1)}), bf16[8,16,640]{2,1,0:T(8,128)(2,1)S(1)}, u32[]{:S(2)}, u32[]{:S(2)}) %all-to-all-start.1) | async-done | bytes 163872 | tf_op jit(solution)/shard_map/all_to_all | solution.py:413
  61.8 0.9 merge.1
  62.7 5.2 %all-to-all-start.2 = ((bf16[32,16,384]{2,1,0:T(8,128)(2,1)}), bf16[32,16,384]{2,1,0:T(8,128)(2,1)}, u32[]{:S(2)}, u32[]{:S(2)}) async-start(bf16[32,16,384]{2,1,0:T(8,128)(2,1)} %merge.1), calls=%async_computation.2 | async-start | bytes 786432 | tf_op jit(solution)/shard_map/all_to_all | solution.py:421
  68.0 1.0 copy-done.1
  69.0 1.0 copy-done.3
  70.0 1.0 copy-done.5
  71.0 1.0 copy-done.6
  72.4 9.4 %all-to-all-done.2 = bf16[32,16,384]{2,1,0:T(8,128)(2,1)} async-done(((bf16[32,16,384]{2,1,0:T(8,128)(2,1)}), bf16[32,16,384]{2,1,0:T(8,128)(2,1)}, u32[]{:S(2)}, u32[]{:S(2)}) %all-to-all-start.2) | async-done | bytes 393248 | tf_op jit(solution)/shard_map/all_to_all | solution.py:421
  81.9 2.4 %grads.3 = bf16[512,512]{1,0:T(8,128)(2,1)S(1)} custom-call(s32[1]{0:T(128)} %bitcast.place, bf16[2304,512]{1,0:T(8,128)(2,1)S(1)} %unpack.1.slots, bf16[4,128,384]{2,1,0:T(8,128)(2,1)} %bitcast.2.merged), custom_call_target="tpu_custom_call" | custom-call | flops 1000000 | bytes 2000000 | tf_op jit(solution)/shard_map/grads/pallas_call | solution.py:301
  84.2 20.4 %all_to_all.30.parts = bf16[16,32,512]{2,1,0:T(8,128)(2,1)S(1)} all-to-all(bf16[16,32,512]{2,1,0:T(8,128)(2,1)S(1)} %bitcast.7), channel_id=1, replica_groups=mesh['yh'=4,'yl'=2,'zl'=2,'x'=4,'zh'=4,'c'=2] {'zl','yl','yh'}, dimensions={0} | all-to-all | bytes 1048576 | tf_op jit(solution)/shard_map/all_to_all | solution.py:433
  104.7 13.9 %all_to_all.31 = bf16[4,32,512]{2,1,0:T(8,128)(2,1)S(1)} all-to-all(bf16[4,32,512]{2,1,0:T(8,128)(2,1)S(1)} %total.1), channel_id=1, replica_groups=mesh['yh'=4,'yl'=2,'zl'=2,'x'=4,'zh'=4,'c'=2] {'yh'}, dimensions={0} | all-to-all | bytes 262144 | tf_op jit(solution)/shard_map/all_to_all | solution.py:438
  118.9 29.8 %all_to_all.32 = bf16[16,128,512]{2,1,0:T(8,128)(2,1)S(1)} all-to-all(bf16[16,128,512]{2,1,0:T(8,128)(2,1)S(1)} %broadcast_in_dim.8), channel_id=1, replica_groups=mesh['yh'=4,'yl'=2,'zl'=2,'x'=4,'zh'=4,'c'=2] {'zl','yl','x'}, dimensions={0} | all-to-all | bytes 4194304 | tf_op jit(solution)/shard_map/all_to_all | solution.py:441
  148.7 3.4 %final.1 = (f32[2048,384]{1,0:T(8,128)}, f32[128,2048]{1,0:T(8,128)}) custom-call(bf16[2,2,4,128,512]{4,3,2,1,0:T(8,128)(2,1)S(1)} %bitcast.6), custom_call_target="tpu_custom_call" | custom-call | tf_op jit(solution)/shard_map/final/pallas_call | solution.py:444
  (20 shorter events, 1.7 us)
Async XLA Ops:
  0.6 15.2 %copy-start.8 = (s32[128,1]{0,1:T(1,128)S(1)}, s32[128,1]{0,1:T(1,128)}, u32[]{:S(2)}) copy-start(s32[128,1]{0,1:T(1,128)} %param.23) | copy-start | bytes 1540
  3.3 37.6 %all-to-all-start = ((bf16[64,56,128]{2,1,0:T(8,128)(2,1)}), bf16[64,56,128]{2,1,0:T(8,128)(2,1)S(1)}, u32[]{:S(2)}, u32[]{:S(2)}) async-start(bf16[64,56,128]{2,1,0:T(8,128)(2,1)} %pack.1), calls=%async_computation | async-start | bytes 1835008 | tf_op jit(solution)/shard_map/all_to_all | solution.py:356
  25.4 25.7 %collective-permute-start = (bf16[3,512,128]{2,1,0:T(8,128)(2,1)}, bf16[3,512,128]{2,1,0:T(8,128)(2,1)S(1)}, u32[]{:S(2)}, u32[]{:S(2)}) collective-permute-start(bf16[3,512,128]{2,1,0:T(8,128)(2,1)} %get-tuple-element.10), channel_id=1, source_target_pairs={{0,8},{8,16},{16,24},{24,0},{1,9},{9,17},{17,25},{25,1},{2,10},{10... | collective-permute-start | bytes 1179656 | tf_op jit(solution)/shard_map/ppermute | solution.py:407
  28.8 22.4 %collective-permute-start.1 = (bf16[3,512,128]{2,1,0:T(8,128)(2,1)}, bf16[3,512,128]{2,1,0:T(8,128)(2,1)S(1)}, u32[]{:S(2)}, u32[]{:S(2)}) collective-permute-start(bf16[3,512,128]{2,1,0:T(8,128)(2,1)} %get-tuple-element.11), channel_id=1, source_target_pairs={{0,16},{8,24},{16,0},{24,8},{1,17},{9,25},{17,1},{25,9},{2,18},{10... | collective-permute-start | bytes 1179656 | tf_op jit(solution)/shard_map/ppermute | solution.py:407
  31.8 21.8 %collective-permute-start.2 = (bf16[3,512,128]{2,1,0:T(8,128)(2,1)}, bf16[3,512,128]{2,1,0:T(8,128)(2,1)S(1)}, u32[]{:S(2)}, u32[]{:S(2)}) collective-permute-start(bf16[3,512,128]{2,1,0:T(8,128)(2,1)} %get-tuple-element.12), channel_id=1, source_target_pairs={{0,24},{8,0},{16,8},{24,16},{1,25},{9,1},{17,9},{25,17},{2,26},{10... | collective-permute-start | bytes 1179656 | tf_op jit(solution)/shard_map/ppermute | solution.py:407
  35.9 1.0 copy-start.7
  41.7 20.1 %all-to-all-start.1 = ((bf16[8,16,640]{2,1,0:T(8,128)(2,1)}), bf16[8,16,640]{2,1,0:T(8,128)(2,1)S(1)}, u32[]{:S(2)}, u32[]{:S(2)}) async-start(bf16[8,16,640]{2,1,0:T(8,128)(2,1)} %bitcast.1), calls=%async_computation.1 | async-start | bytes 327680 | tf_op jit(solution)/shard_map/all_to_all | solution.py:413
  51.1 16.8 %copy-start = (bf16[3,512,128]{2,1,0:T(8,128)(2,1)}, bf16[3,512,128]{2,1,0:T(8,128)(2,1)S(1)}, u32[]{:S(2)}) copy-start(bf16[3,512,128]{2,1,0:T(8,128)(2,1)S(1)} %collective-permute-done.first.refs_0_) | copy-start | bytes 1179652
  51.2 16.8 %copy-start.2 = (bf16[3,512,128]{2,1,0:T(8,128)(2,1)}, bf16[3,512,128]{2,1,0:T(8,128)(2,1)S(1)}, u32[]{:S(2)}) copy-start(bf16[3,512,128]{2,1,0:T(8,128)(2,1)S(1)} %collective-permute-done.1.second.refs_1_) | copy-start | bytes 1179652
  53.6 14.4 %copy-start.4 = (bf16[3,512,128]{2,1,0:T(8,128)(2,1)}, bf16[3,512,128]{2,1,0:T(8,128)(2,1)S(1)}, u32[]{:S(2)}) copy-start(bf16[3,512,128]{2,1,0:T(8,128)(2,1)S(1)} %collective-permute-done.2.third.refs_2_) | copy-start | bytes 1179652
  62.7 19.1 %all-to-all-start.2 = ((bf16[32,16,384]{2,1,0:T(8,128)(2,1)}), bf16[32,16,384]{2,1,0:T(8,128)(2,1)}, u32[]{:S(2)}, u32[]{:S(2)}) async-start(bf16[32,16,384]{2,1,0:T(8,128)(2,1)} %merge.1), calls=%async_computation.2 | async-start | bytes 786432 | tf_op jit(solution)/shard_map/all_to_all | solution.py:421
  68.0 1.0 copy-start.1
  69.0 1.0 copy-start.3
  70.0 1.0 copy-start.5
  71.0 1.0 copy-start.6

commit v8 on v7

--- a/solution.py
+++ b/solution.py
@@ -165,21 +165,19 @@
 
 def unpack_kernel(received, own, first, second, third, out, rows):
     peers = received.shape[0]
-    count, block = rows.shape
+    count, block = rows.shape[0], own.shape[1]
     slots = count // peers
-    for j in range(peers):
-        wide = received[j].astype(F32)
-        for b in range(block // RANK):
-            rows[j * slots : (j + 1) * slots, b * RANK : (b + 1) * RANK] = wide[
+    for b in range(block // RANK):
+        for j in range(peers):
+            rows[j * slots : (j + 1) * slots, :] = received[j].astype(F32)[
                 b * slots : (b + 1) * slots, :
             ]
-    out[:count, :] = rows[...].astype(BF)
-    for k, turned in enumerate((own, first, second, third)):
+        out[b * count : (b + 1) * count, :] = rows[...].astype(BF)
+    start = count * (block // RANK)
+    for turned in (own, first, second, third):
         for layer in range(3):
-            start = count + (k * 3 + layer) * RANK
-            for b in range(block // RANK):
-                columns = slice(b * RANK, (b + 1) * RANK)
-                out[start : start + RANK, columns] = turned[layer, columns, :]
+            out[start : start + block, :] = turned[layer]
+            start = start + block
 
 
 def ready_kernel(partial, base, chosen):
@@ -234,8 +232,9 @@
 
 
 def grads_kernel(place, slots, merged, out):
-    blocks = slots.shape[1] // RANK
-    count = slots.shape[0] - NX * 3 * RANK
+    block = out.shape[0]
+    blocks = block // RANK
+    count = slots.shape[0] // blocks - NX * 3 * RANK
     peer_slots = NX * MOST
     down = [None] * 3
     placed = None
@@ -246,14 +245,8 @@
         grad = rows[:, :RANK].astype(F32)
         for i in range(3):
             inverse = notes[:, i : i + 1] + notes[:, 3 + i : 4 + i]
-            start = count + (k * 3 + i) * RANK
-            turned = jnp.concatenate(
-                [
-                    slots[start : start + RANK, b * RANK : (b + 1) * RANK]
-                    for b in range(blocks)
-                ],
-                axis=0,
-            )
+            start = count * blocks + (k * 3 + i) * block
+            turned = slots[start : start + block, :]
             term = dot(turned, (inverse * grad).astype(BF))
             down[i] = term if down[i] is None else down[i] + term
         slot = notes[:, 6:7].astype(jnp.int32) * peer_slots + notes[:, 7:8].astype(jnp.int32)
@@ -263,9 +256,10 @@
         placed = term if placed is None else placed + term
     for i in range(3):
         out[:, i * RANK : (i + 1) * RANK] = down[i].astype(BF)
-    up = dot(placed.astype(BF), slots[:count, :]).astype(BF)
+    placed = placed.astype(BF)
     for b in range(blocks):
-        out[b * RANK : (b + 1) * RANK, 3 * RANK :] = up[:, b * RANK : (b + 1) * RANK]
+        up = dot(placed, slots[b * count : (b + 1) * count, :])
+        out[b * RANK : (b + 1) * RANK, 3 * RANK :] = up.astype(BF)
 
 
 def sum_kernel(parts, out):
@@ -275,13 +269,22 @@
     out[...] = jnp.broadcast_to(total.astype(BF)[None], out.shape)
 
 
-def final_kernel(parts, down, up):
-    step = pl.program_id(0)
-    z, x = step % parts.shape[0], step // parts.shape[0]
-    for b in range(up.shape[1] // RANK):
-        rows = slice(b * RANK, (b + 1) * RANK)
-        down[rows, :] = parts[z, b, x, :, : 3 * RANK].astype(F32)
-        up[:, rows] = parts[z, b, x, :, 3 * RANK :].astype(F32)
+def final_kernel(parts, down_out, up_out, down, up, sems):
+    near, rows = parts.shape[0] * parts.shape[1], parts.shape[3]
+    copies = []
+    for x in range(parts.shape[2]):
+        for n in range(near):
+            z, y = n // parts.shape[1], n % parts.shape[1]
+            piece = pl.ds((x * near + n) * rows, rows)
+            down[piece, :] = parts[z, y, x, :, : 3 * RANK].astype(F32)
+            up[:, piece] = parts[z, y, x, :, 3 * RANK :].astype(F32)
+        mine = pl.ds(x * near * rows, near * rows)
+        copies.append(pltpu.make_async_copy(down.at[mine], down_out.at[mine], sems.at[0, x]))
+        copies.append(pltpu.make_async_copy(up.at[:, mine], up_out.at[:, mine], sems.at[1, x]))
+        for copy in copies[-2:]:
+            copy.start()
+    for copy in copies:
+        copy.wait()
 
 
 def whole(shape):
@@ -423,10 +426,10 @@
     slots = call(
         unpack_kernel,
         "unpack",
-        shape((peers * NX * MOST + NX * 3 * RANK, block)),
+        shape((block // RANK * peers * NX * MOST + NX * 3 * block, RANK)),
         received,
         *turned,
-        scratch=[((peers * NX * MOST, block), F32)],
+        scratch=[((peers * NX * MOST, RANK), F32)],
     )
     grads = call(grads_kernel, "grads", shape((block, 4 * RANK)), place, slots, merged)
     piece = block // (nzl * nyl * nyh)
@@ -440,16 +443,16 @@
     grads = jnp.broadcast_to(grads[None], (near * NX, rows, 4 * RANK))
     grads = lax.all_to_all(grads, ("zl", "yl", "x"), 0, 0, tiled=True)
     grads = grads.reshape(nzl, nyl, NX, rows, 4 * RANK)
-    step = nyl * rows
     return pl.pallas_call(
         final_kernel,
-        grid=(nzl * NX,),
         in_specs=[pl.BlockSpec(memory_space=pltpu.VMEM)],
-        out_specs=[
-            pl.BlockSpec((step, 3 * RANK), lambda i: (i, 0)),
-            pl.BlockSpec((RANK, step), lambda i: (0, i)),
+        out_specs=[pl.BlockSpec(memory_space=pl.ANY)] * 2,
+        out_shape=[shape((width, 3 * RANK), F32), shape((RANK, width), F32)],
+        scratch_shapes=[
+            pltpu.VMEM((width, 3 * RANK), F32),
+            pltpu.VMEM((RANK, width), F32),
+            pltpu.SemaphoreType.DMA((2, NX)),
         ],
-        out_shape=[shape((width, 3 * RANK), F32), shape((RANK, width), F32)],
         compiler_params=params(),
         name="final",
     )(grads)

time: 153 us -> 152 us (level)
  the two profiles are of different devices: /device:TPU:2 before, /device:TPU:16 now
where the time goes in v8:
time: 152 us; the launch traced here: 151 us
  blocking collectives  63.8 us (42%)
  starting transfers between devices  37.8 us (25%)
  waiting for transfers between devices  24.2 us (16%)
  Pallas kernels  18.5 us (12%)
  local copies, waits for them, and re-layouts  5.87 us (4%)
    all_to_all x1, blocking collectives, body(): grads = lax.all_to_all(grads, ('zl', 'yl', 'x'), 0, 0, tiled=True)  31.4 us
    all_to_all x1, blocking collectives, body(): lax.all_to_all(grads.reshape(nzl * nyl * nyh, piece, 4 * RANK), ('zl', 'y...  22 us
    all_to_all x1, starting transfers between devices, body(): received = lax.all_to_all(packed, ('yh', 'yl', 'zl', 'x'), 0, 0, tiled=True)  12.3 us
    all_to_all x1, waiting for transfers between devices, body(): merged = lax.all_to_all(merged, ('x', 'zh', 'c'), 0, 0, tiled=True)  12 us
    ppermute x3, starting transfers between devices, body(): lax.ppermute(turned[k], 'x', [(i, (i + k) % NX) for i in range(NX)])  11.3 us
    all_to_all x1, blocking collectives, body(): lax.all_to_all(grads, 'yh', 0, 0, tiled=True).reshape(rows, 4 * RANK)  10.4 us
    all_to_all x1, starting transfers between devices, body(): lax.all_to_all(sent.reshape(nzh * nc, share, 5 * RANK), ('zh', 'c'), 0, 0...  9.41 us
    pallas_call x1, Pallas kernels, body(): pl.pallas_call(feature_kernel, grid=(branches // together,), in_specs=[sm...  8.87 us
  transfers between devices with their start and end apart: 6, of which 5 were waited for; matrix products, arithmetic and copies ran while one was open for 0% of the time, Pallas kernels for 7%

profile of v8, /device:TPU:16, one launch (start us, length us, event | category | flops | bytes accessed | tf_op | source)
XLA Modules:
  0.0 150.9 jit_solution(1562611261792124544)
XLA Ops:
  0.6 2.7 %pack.1 = bf16[64,56,128]{2,1,0:T(8,128)(2,1)} custom-call(bf16[192,2048]{1,0:T(8,128)(2,1)} %grads.2, bf16[128,2048]{1,0:T(8,128)(2,1)} %merge_up.1), custom_call_target="tpu_custom_call" | custom-call | flops 1000000 | bytes 2000000 | tf_op jit(solution)/shard_map/pack/pallas_call | solution.py:304
  3.3 12.3 %all-to-all-start = ((bf16[64,56,128]{2,1,0:T(8,128)(2,1)}), bf16[64,56,128]{2,1,0:T(8,128)(2,1)S(1)}, u32[]{:S(2)}, u32[]{:S(2)}) async-start(bf16[64,56,128]{2,1,0:T(8,128)(2,1)} %pack.1), calls=%async_computation | async-start | bytes 1835008 | tf_op jit(solution)/shard_map/all_to_all | solution.py:359
  16.4 8.9 %features.1 = (bf16[3,512,128]{2,1,0:T(8,128)(2,1)}, bf16[3,512,128]{2,1,0:T(8,128)(2,1)}, bf16[3,512,128]{2,1,0:T(8,128)(2,1)}, bf16[3,512,128]{2,1,0:T(8,128)(2,1)}, f32[128,512]{1,0:T(8,128)}) custom-call(s32[1]{0:T(128)} %bitcast.place, s32[8]{0:T(128)} %lengths.1, s32[8]{0:T(128)} %counts.1, s32[128,1]{1,0:T(8,128)} %copy.17.targets, s32[8,16]{1,0:T(8,128)} %parents.1, ...), custom_call_target="tpu_custom_call" | custom-call | flops 400000000 | bytes 8000000 | tf_op jit(solution)/shard_map/features/pallas_call | solution.py:360
  25.2 3.4 %collective-permute-start = (bf16[3,512,128]{2,1,0:T(8,128)(2,1)}, bf16[3,512,128]{2,1,0:T(8,128)(2,1)S(1)}, u32[]{:S(2)}, u32[]{:S(2)}) collective-permute-start(bf16[3,512,128]{2,1,0:T(8,128)(2,1)} %get-tuple-element.10), channel_id=1, source_target_pairs={{0,8},{8,16},{16,24},{24,0},{1,9},{9,17},{17,25},{25,1},{2,10},{10... | collective-permute-start | bytes 1179656 | tf_op jit(solution)/shard_map/ppermute | solution.py:410
  28.6 4.6 %collective-permute-start.1 = (bf16[3,512,128]{2,1,0:T(8,128)(2,1)}, bf16[3,512,128]{2,1,0:T(8,128)(2,1)S(1)}, u32[]{:S(2)}, u32[]{:S(2)}) collective-permute-start(bf16[3,512,128]{2,1,0:T(8,128)(2,1)} %get-tuple-element.11), channel_id=1, source_target_pairs={{0,16},{8,24},{16,0},{24,8},{1,17},{9,25},{17,1},{25,9},{2,18},{10... | collective-permute-start | bytes 1179656 | tf_op jit(solution)/shard_map/ppermute | solution.py:410
  33.2 3.4 %collective-permute-start.2 = (bf16[3,512,128]{2,1,0:T(8,128)(2,1)}, bf16[3,512,128]{2,1,0:T(8,128)(2,1)S(1)}, u32[]{:S(2)}, u32[]{:S(2)}) collective-permute-start(bf16[3,512,128]{2,1,0:T(8,128)(2,1)} %get-tuple-element.12), channel_id=1, source_target_pairs={{0,24},{8,0},{16,8},{24,16},{1,25},{9,1},{17,9},{25,17},{2,26},{10... | collective-permute-start | bytes 1179656 | tf_op jit(solution)/shard_map/ppermute | solution.py:410
  36.6 0.9 copy-done.7
  37.8 2.1 %all-to-all-done.received = bf16[64,56,128]{2,1,0:T(8,128)(2,1)S(1)} async-done(((bf16[64,56,128]{2,1,0:T(8,128)(2,1)}), bf16[64,56,128]{2,1,0:T(8,128)(2,1)S(1)}, u32[]{:S(2)}, u32[]{:S(2)}) %all-to-all-start) | async-done | bytes 917536 | tf_op jit(solution)/shard_map/all_to_all | solution.py:359
  39.9 0.8 pick.1
  40.7 9.4 %all-to-all-start.1 = ((bf16[8,16,640]{2,1,0:T(8,128)(2,1)}), bf16[8,16,640]{2,1,0:T(8,128)(2,1)S(1)}, u32[]{:S(2)}, u32[]{:S(2)}) async-start(bf16[8,16,640]{2,1,0:T(8,128)(2,1)} %bitcast.1), calls=%async_computation.1 | async-start | bytes 327680 | tf_op jit(solution)/shard_map/all_to_all | solution.py:416
  50.1 1.6 %collective-permute-done.1.second.refs_1_ = bf16[3,512,128]{2,1,0:T(8,128)(2,1)S(1)} collective-permute-done((bf16[3,512,128]{2,1,0:T(8,128)(2,1)}, bf16[3,512,128]{2,1,0:T(8,128)(2,1)S(1)}, u32[]{:S(2)}, u32[]{:S(2)}) %collective-permute-start.1) | collective-permute-done | bytes 393248 | tf_op jit(solution)/shard_map/ppermute | solution.py:410
  52.3 8.0 %all-to-all-done.1.parts = bf16[8,16,640]{2,1,0:T(8,128)(2,1)S(1)} async-done(((bf16[8,16,640]{2,1,0:T(8,128)(2,1)}), bf16[8,16,640]{2,1,0:T(8,128)(2,1)S(1)}, u32[]{:S(2)}, u32[]{:S(2)}) %all-to-all-start.1) | async-done | bytes 163872 | tf_op jit(solution)/shard_map/all_to_all | solution.py:416
  60.3 0.9 merge.1
  61.2 4.8 %all-to-all-start.2 = ((bf16[32,16,384]{2,1,0:T(8,128)(2,1)}), bf16[32,16,384]{2,1,0:T(8,128)(2,1)}, u32[]{:S(2)}, u32[]{:S(2)}) async-start(bf16[32,16,384]{2,1,0:T(8,128)(2,1)} %merge.1), calls=%async_computation.2 | async-start | bytes 786432 | tf_op jit(solution)/shard_map/all_to_all | solution.py:424
  66.1 1.0 copy-done.1
  67.0 1.0 copy-done.3
  68.0 1.0 copy-done.5
  69.0 1.0 copy-done.6
  70.3 12.0 %all-to-all-done.2 = bf16[32,16,384]{2,1,0:T(8,128)(2,1)} async-done(((bf16[32,16,384]{2,1,0:T(8,128)(2,1)}), bf16[32,16,384]{2,1,0:T(8,128)(2,1)}, u32[]{:S(2)}, u32[]{:S(2)}) %all-to-all-start.2) | async-done | bytes 393248 | tf_op jit(solution)/shard_map/all_to_all | solution.py:424
  82.3 2.5 %grads.3 = bf16[512,512]{1,0:T(8,128)(2,1)S(1)} custom-call(s32[1]{0:T(128)} %bitcast.place, bf16[9216,128]{1,0:T(8,128)(2,1)S(1)} %unpack.1.slots, bf16[4,128,384]{2,1,0:T(8,128)(2,1)} %bitcast.2.merged), custom_call_target="tpu_custom_call" | custom-call | flops 1000000 | bytes 2000000 | tf_op jit(solution)/shard_map/grads/pallas_call | solution.py:304
  84.8 22.0 %all_to_all.30.parts = bf16[16,32,512]{2,1,0:T(8,128)(2,1)S(1)} all-to-all(bf16[16,32,512]{2,1,0:T(8,128)(2,1)S(1)} %bitcast.7), channel_id=1, replica_groups=mesh['yh'=4,'yl'=2,'zl'=2,'x'=4,'zh'=4,'c'=2] {'zl','yl','yh'}, dimensions={0} | all-to-all | bytes 1048576 | tf_op jit(solution)/shard_map/all_to_all | solution.py:436
  106.8 10.4 %all_to_all.31 = bf16[4,32,512]{2,1,0:T(8,128)(2,1)S(1)} all-to-all(bf16[4,32,512]{2,1,0:T(8,128)(2,1)S(1)} %total.1), channel_id=1, replica_groups=mesh['yh'=4,'yl'=2,'zl'=2,'x'=4,'zh'=4,'c'=2] {'yh'}, dimensions={0} | all-to-all | bytes 262144 | tf_op jit(solution)/shard_map/all_to_all | solution.py:441
  117.4 31.4 %all_to_all.32 = bf16[16,128,512]{2,1,0:T(8,128)(2,1)S(1)} all-to-all(bf16[16,128,512]{2,1,0:T(8,128)(2,1)S(1)} %broadcast_in_dim.8), channel_id=1, replica_groups=mesh['yh'=4,'yl'=2,'zl'=2,'x'=4,'zh'=4,'c'=2] {'zl','yl','x'}, dimensions={0} | all-to-all | bytes 4194304 | tf_op jit(solution)/shard_map/all_to_all | solution.py:444
  148.8 2.1 %final.1 = (f32[2048,384]{1,0:T(8,128)}, f32[128,2048]{1,0:T(8,128)}) custom-call(bf16[2,2,4,128,512]{4,3,2,1,0:T(8,128)(2,1)S(1)} %bitcast.6), custom_call_target="tpu_custom_call" | custom-call | tf_op jit(solution)/shard_map/final/pallas_call | solution.py:446
  (20 shorter events, 2.2 us)
Async XLA Ops:
  0.6 15.0 %copy-start.8 = (s32[128,1]{0,1:T(1,128)S(1)}, s32[128,1]{0,1:T(1,128)}, u32[]{:S(2)}) copy-start(s32[128,1]{0,1:T(1,128)} %param.23) | copy-start | bytes 1540
  3.3 36.5 %all-to-all-start = ((bf16[64,56,128]{2,1,0:T(8,128)(2,1)}), bf16[64,56,128]{2,1,0:T(8,128)(2,1)S(1)}, u32[]{:S(2)}, u32[]{:S(2)}) async-start(bf16[64,56,128]{2,1,0:T(8,128)(2,1)} %pack.1), calls=%async_computation | async-start | bytes 1835008 | tf_op jit(solution)/shard_map/all_to_all | solution.py:359
  25.2 24.9 %collective-permute-start = (bf16[3,512,128]{2,1,0:T(8,128)(2,1)}, bf16[3,512,128]{2,1,0:T(8,128)(2,1)S(1)}, u32[]{:S(2)}, u32[]{:S(2)}) collective-permute-start(bf16[3,512,128]{2,1,0:T(8,128)(2,1)} %get-tuple-element.10), channel_id=1, source_target_pairs={{0,8},{8,16},{16,24},{24,0},{1,9},{9,17},{17,25},{25,1},{2,10},{10... | collective-permute-start | bytes 1179656 | tf_op jit(solution)/shard_map/ppermute | solution.py:410
  28.6 23.1 %collective-permute-start.1 = (bf16[3,512,128]{2,1,0:T(8,128)(2,1)}, bf16[3,512,128]{2,1,0:T(8,128)(2,1)S(1)}, u32[]{:S(2)}, u32[]{:S(2)}) collective-permute-start(bf16[3,512,128]{2,1,0:T(8,128)(2,1)} %get-tuple-element.11), channel_id=1, source_target_pairs={{0,16},{8,24},{16,0},{24,8},{1,17},{9,25},{17,1},{25,9},{2,18},{10... | collective-permute-start | bytes 1179656 | tf_op jit(solution)/shard_map/ppermute | solution.py:410
  33.2 19.1 %collective-permute-start.2 = (bf16[3,512,128]{2,1,0:T(8,128)(2,1)}, bf16[3,512,128]{2,1,0:T(8,128)(2,1)S(1)}, u32[]{:S(2)}, u32[]{:S(2)}) collective-permute-start(bf16[3,512,128]{2,1,0:T(8,128)(2,1)} %get-tuple-element.12), channel_id=1, source_target_pairs={{0,24},{8,0},{16,8},{24,16},{1,25},{9,1},{17,9},{25,17},{2,26},{10... | collective-permute-start | bytes 1179656 | tf_op jit(solution)/shard_map/ppermute | solution.py:410
  36.6 1.0 copy-start.7
  40.7 19.6 %all-to-all-start.1 = ((bf16[8,16,640]{2,1,0:T(8,128)(2,1)}), bf16[8,16,640]{2,1,0:T(8,128)(2,1)S(1)}, u32[]{:S(2)}, u32[]{:S(2)}) async-start(bf16[8,16,640]{2,1,0:T(8,128)(2,1)} %bitcast.1), calls=%async_computation.1 | async-start | bytes 327680 | tf_op jit(solution)/shard_map/all_to_all | solution.py:416
  50.1 15.9 %copy-start = (bf16[3,512,128]{2,1,0:T(8,128)(2,1)}, bf16[3,512,128]{2,1,0:T(8,128)(2,1)S(1)}, u32[]{:S(2)}) copy-start(bf16[3,512,128]{2,1,0:T(8,128)(2,1)S(1)} %collective-permute-done.first.refs_0_) | copy-start | bytes 1179652
  51.7 14.3 %copy-start.2 = (bf16[3,512,128]{2,1,0:T(8,128)(2,1)}, bf16[3,512,128]{2,1,0:T(8,128)(2,1)S(1)}, u32[]{:S(2)}) copy-start(bf16[3,512,128]{2,1,0:T(8,128)(2,1)S(1)} %collective-permute-done.1.second.refs_1_) | copy-start | bytes 1179652
  52.3 13.7 %copy-start.4 = (bf16[3,512,128]{2,1,0:T(8,128)(2,1)}, bf16[3,512,128]{2,1,0:T(8,128)(2,1)S(1)}, u32[]{:S(2)}) copy-start(bf16[3,512,128]{2,1,0:T(8,128)(2,1)S(1)} %collective-permute-done.2.third.refs_2_) | copy-start | bytes 1179652
  61.2 21.1 %all-to-all-start.2 = ((bf16[32,16,384]{2,1,0:T(8,128)(2,1)}), bf16[32,16,384]{2,1,0:T(8,128)(2,1)}, u32[]{:S(2)}, u32[]{:S(2)}) async-start(bf16[32,16,384]{2,1,0:T(8,128)(2,1)} %merge.1), calls=%async_computation.2 | async-start | bytes 786432 | tf_op jit(solution)/shard_map/all_to_all | solution.py:424
  66.0 1.0 copy-start.1
  67.0 1.0 copy-start.3
  68.0 1.0 copy-start.5
  69.0 1.0 copy-start.6

commit v9 on v8

--- a/solution.py
+++ b/solution.py
@@ -13,6 +13,7 @@
 MOST = 3
 NX = 4
 PEERS = 64
+SHIFTS = (0, 2, 1, 3)
 EPSILON = 1e-05
 MASKED = -1e30
 BF = jnp.bfloat16
@@ -122,7 +123,7 @@
         block = own.shape[1]
         copies = []
         for k, out in enumerate((own, first, second, third)):
-            chunk = (place[0] + k) % (width // block)
+            chunk = (place[0] + SHIFTS[k]) % (width // block)
             chunk = pl.ds(pl.multiple_of(chunk * block, block), block)
             for layer in range(3):
                 turned[k, layer] = rows[layer, :, chunk].T
@@ -239,7 +240,7 @@
     down = [None] * 3
     placed = None
     for k in range(NX):
-        source = (place[0] + NX - k) % NX
+        source = (place[0] + NX - SHIFTS[k]) % NX
         rows = merged[source]
         notes = rows[:, 2 * RANK :].astype(F32)
         grad = rows[:, :RANK].astype(F32)
@@ -407,7 +408,7 @@
         merge_down,
     )
     for k in range(1, NX):
-        turned[k] = lax.ppermute(turned[k], "x", [(i, (i + k) % NX) for i in range(NX)])
+        turned[k] = lax.ppermute(turned[k], "x", [(i, (i + SHIFTS[k]) % NX) for i in range(NX)])
     base, chosen = call(
         ready_kernel, "ready", [shape((count, 4 * RANK)), shape((count, peers * 8))], partial
     )

time: 152 us -> 151 us (level)
  transfers between devices with their start and end apart: 6 -> 6, of which waited for: 5 -> 4; matrix products, arithmetic and copies ran while one was open for 0% -> 0% of each run, Pallas kernels for 7% -> 7%
where the time goes in v9:
time: 151 us; the launch traced here: 150 us
  blocking collectives  63.2 us (42%)
  starting transfers between devices  38.4 us (25%)
  waiting for transfers between devices  23.7 us (16%)
  Pallas kernels  18.5 us (12%)
  local copies, waits for them, and re-layouts  5.87 us (4%)
    all_to_all x1, blocking collectives, body(): grads = lax.all_to_all(grads, ('zl', 'yl', 'x'), 0, 0, tiled=True)  31.4 us
    all_to_all x1, blocking collectives, body(): lax.all_to_all(grads.reshape(nzl * nyl * nyh, piece, 4 * RANK), ('zl', 'y...  21.4 us
    all_to_all x1, starting transfers between devices, body(): received = lax.all_to_all(packed, ('yh', 'yl', 'zl', 'x'), 0, 0, tiled=True)  12.3 us
    all_to_all x1, waiting for transfers between devices, body(): merged = lax.all_to_all(merged, ('x', 'zh', 'c'), 0, 0, tiled=True)  12.1 us
    ppermute x3, starting transfers between devices, body(): lax.ppermute(turned[k], 'x', [(i, (i + SHIFTS[k]) % NX) for i in range(NX)])  11.9 us
    all_to_all x1, blocking collectives, body(): lax.all_to_all(grads, 'yh', 0, 0, tiled=True).reshape(rows, 4 * RANK)  10.4 us
    all_to_all x1, starting transfers between devices, body(): lax.all_to_all(sent.reshape(nzh * nc, share, 5 * RANK), ('zh', 'c'), 0, 0...  9.41 us
    all_to_all x1, waiting for transfers between devices, body(): lax.all_to_all(sent.reshape(nzh * nc, share, 5 * RANK), ('zh', 'c'), 0, 0...  9.04 us
  transfers between devices with their start and end apart: 6, of which 4 were waited for; matrix products, arithmetic and copies ran while one was open for 0% of the time, Pallas kernels for 7%

profile of v9, /device:TPU:16, one launch (start us, length us, event | category | flops | bytes accessed | tf_op | source)
XLA Modules:
  0.0 150.5 jit_solution(15000623073170660685)
XLA Ops:
  0.6 2.7 %pack.1 = bf16[64,56,128]{2,1,0:T(8,128)(2,1)} custom-call(bf16[192,2048]{1,0:T(8,128)(2,1)} %grads.2, bf16[128,2048]{1,0:T(8,128)(2,1)} %merge_up.1), custom_call_target="tpu_custom_call" | custom-call | flops 1000000 | bytes 2000000 | tf_op jit(solution)/shard_map/pack/pallas_call | solution.py:305
  3.3 12.3 %all-to-all-start = ((bf16[64,56,128]{2,1,0:T(8,128)(2,1)}), bf16[64,56,128]{2,1,0:T(8,128)(2,1)S(1)}, u32[]{:S(2)}, u32[]{:S(2)}) async-start(bf16[64,56,128]{2,1,0:T(8,128)(2,1)} %pack.1), calls=%async_computation | async-start | bytes 1835008 | tf_op jit(solution)/shard_map/all_to_all | solution.py:360
  16.4 8.9 %features.1 = (bf16[3,512,128]{2,1,0:T(8,128)(2,1)}, bf16[3,512,128]{2,1,0:T(8,128)(2,1)}, bf16[3,512,128]{2,1,0:T(8,128)(2,1)}, bf16[3,512,128]{2,1,0:T(8,128)(2,1)}, f32[128,512]{1,0:T(8,128)}) custom-call(s32[1]{0:T(128)} %bitcast.place, s32[8]{0:T(128)} %lengths.1, s32[8]{0:T(128)} %counts.1, s32[128,1]{1,0:T(8,128)} %copy.17.targets, s32[8,16]{1,0:T(8,128)} %parents.1, ...), custom_call_target="tpu_custom_call" | custom-call | flops 400000000 | bytes 8000000 | tf_op jit(solution)/shard_map/features/pallas_call | solution.py:361
  25.2 4.9 %collective-permute-start = (bf16[3,512,128]{2,1,0:T(8,128)(2,1)}, bf16[3,512,128]{2,1,0:T(8,128)(2,1)S(1)}, u32[]{:S(2)}, u32[]{:S(2)}) collective-permute-start(bf16[3,512,128]{2,1,0:T(8,128)(2,1)} %get-tuple-element.10), channel_id=1, source_target_pairs={{0,16},{8,24},{16,0},{24,8},{1,17},{9,25},{17,1},{25,9},{2,18},{10... | collective-permute-start | bytes 1179656 | tf_op jit(solution)/shard_map/ppermute | solution.py:411
  30.1 2.5 %collective-permute-start.1 = (bf16[3,512,128]{2,1,0:T(8,128)(2,1)}, bf16[3,512,128]{2,1,0:T(8,128)(2,1)S(1)}, u32[]{:S(2)}, u32[]{:S(2)}) collective-permute-start(bf16[3,512,128]{2,1,0:T(8,128)(2,1)} %get-tuple-element.11), channel_id=1, source_target_pairs={{0,8},{8,16},{16,24},{24,0},{1,9},{9,17},{17,25},{25,1},{2,10},{10... | collective-permute-start | bytes 1179656 | tf_op jit(solution)/shard_map/ppermute | solution.py:411
  32.6 4.6 %collective-permute-start.2 = (bf16[3,512,128]{2,1,0:T(8,128)(2,1)}, bf16[3,512,128]{2,1,0:T(8,128)(2,1)S(1)}, u32[]{:S(2)}, u32[]{:S(2)}) collective-permute-start(bf16[3,512,128]{2,1,0:T(8,128)(2,1)} %get-tuple-element.12), channel_id=1, source_target_pairs={{0,24},{8,0},{16,8},{24,16},{1,25},{9,1},{17,9},{25,17},{2,26},{10... | collective-permute-start | bytes 1179656 | tf_op jit(solution)/shard_map/ppermute | solution.py:411
  37.2 0.9 copy-done.7
  38.4 1.6 %all-to-all-done.received = bf16[64,56,128]{2,1,0:T(8,128)(2,1)S(1)} async-done(((bf16[64,56,128]{2,1,0:T(8,128)(2,1)}), bf16[64,56,128]{2,1,0:T(8,128)(2,1)S(1)}, u32[]{:S(2)}, u32[]{:S(2)}) %all-to-all-start) | async-done | bytes 917536 | tf_op jit(solution)/shard_map/all_to_all | solution.py:360
  40.0 0.8 pick.1
  40.8 9.4 %all-to-all-start.1 = ((bf16[8,16,640]{2,1,0:T(8,128)(2,1)}), bf16[8,16,640]{2,1,0:T(8,128)(2,1)S(1)}, u32[]{:S(2)}, u32[]{:S(2)}) async-start(bf16[8,16,640]{2,1,0:T(8,128)(2,1)} %bitcast.1), calls=%async_computation.1 | async-start | bytes 327680 | tf_op jit(solution)/shard_map/all_to_all | solution.py:417
  50.2 1.0 collective-permute-done.1.second.refs_1_
  51.3 9.0 %all-to-all-done.1.parts = bf16[8,16,640]{2,1,0:T(8,128)(2,1)S(1)} async-done(((bf16[8,16,640]{2,1,0:T(8,128)(2,1)}), bf16[8,16,640]{2,1,0:T(8,128)(2,1)S(1)}, u32[]{:S(2)}, u32[]{:S(2)}) %all-to-all-start.1) | async-done | bytes 163872 | tf_op jit(solution)/shard_map/all_to_all | solution.py:417
  60.3 0.9 merge.1
  61.3 4.7 %all-to-all-start.2 = ((bf16[32,16,384]{2,1,0:T(8,128)(2,1)}), bf16[32,16,384]{2,1,0:T(8,128)(2,1)}, u32[]{:S(2)}, u32[]{:S(2)}) async-start(bf16[32,16,384]{2,1,0:T(8,128)(2,1)} %merge.1), calls=%async_computation.2 | async-start | bytes 786432 | tf_op jit(solution)/shard_map/all_to_all | solution.py:425
  66.1 1.0 copy-done.1
  67.0 1.0 copy-done.3
  68.0 1.0 copy-done.5
  69.0 1.0 copy-done.6
  70.3 12.1 %all-to-all-done.2 = bf16[32,16,384]{2,1,0:T(8,128)(2,1)} async-done(((bf16[32,16,384]{2,1,0:T(8,128)(2,1)}), bf16[32,16,384]{2,1,0:T(8,128)(2,1)}, u32[]{:S(2)}, u32[]{:S(2)}) %all-to-all-start.2) | async-done | bytes 393248 | tf_op jit(solution)/shard_map/all_to_all | solution.py:425
  82.4 2.5 %grads.3 = bf16[512,512]{1,0:T(8,128)(2,1)S(1)} custom-call(s32[1]{0:T(128)} %bitcast.place, bf16[9216,128]{1,0:T(8,128)(2,1)S(1)} %unpack.1.slots, bf16[4,128,384]{2,1,0:T(8,128)(2,1)} %bitcast.2.merged), custom_call_target="tpu_custom_call" | custom-call | flops 1000000 | bytes 2000000 | tf_op jit(solution)/shard_map/grads/pallas_call | solution.py:305
  84.9 21.4 %all_to_all.30.parts = bf16[16,32,512]{2,1,0:T(8,128)(2,1)S(1)} all-to-all(bf16[16,32,512]{2,1,0:T(8,128)(2,1)S(1)} %bitcast.7), channel_id=1, replica_groups=mesh['yh'=4,'yl'=2,'zl'=2,'x'=4,'zh'=4,'c'=2] {'zl','yl','yh'}, dimensions={0} | all-to-all | bytes 1048576 | tf_op jit(solution)/shard_map/all_to_all | solution.py:437
  106.4 10.4 %all_to_all.31 = bf16[4,32,512]{2,1,0:T(8,128)(2,1)S(1)} all-to-all(bf16[4,32,512]{2,1,0:T(8,128)(2,1)S(1)} %total.1), channel_id=1, replica_groups=mesh['yh'=4,'yl'=2,'zl'=2,'x'=4,'zh'=4,'c'=2] {'yh'}, dimensions={0} | all-to-all | bytes 262144 | tf_op jit(solution)/shard_map/all_to_all | solution.py:442
  117.0 31.4 %all_to_all.32 = bf16[16,128,512]{2,1,0:T(8,128)(2,1)S(1)} all-to-all(bf16[16,128,512]{2,1,0:T(8,128)(2,1)S(1)} %broadcast_in_dim.8), channel_id=1, replica_groups=mesh['yh'=4,'yl'=2,'zl'=2,'x'=4,'zh'=4,'c'=2] {'zl','yl','x'}, dimensions={0} | all-to-all | bytes 4194304 | tf_op jit(solution)/shard_map/all_to_all | solution.py:445
  148.4 2.1 %final.1 = (f32[2048,384]{1,0:T(8,128)}, f32[128,2048]{1,0:T(8,128)}) custom-call(bf16[2,2,4,128,512]{4,3,2,1,0:T(8,128)(2,1)S(1)} %bitcast.6), custom_call_target="tpu_custom_call" | custom-call | tf_op jit(solution)/shard_map/final/pallas_call | solution.py:447
  (20 shorter events, 1.6 us)
Async XLA Ops:
  0.6 15.0 %copy-start.8 = (s32[128,1]{0,1:T(1,128)S(1)}, s32[128,1]{0,1:T(1,128)}, u32[]{:S(2)}) copy-start(s32[128,1]{0,1:T(1,128)} %param.23) | copy-start | bytes 1540
  3.3 36.6 %all-to-all-start = ((bf16[64,56,128]{2,1,0:T(8,128)(2,1)}), bf16[64,56,128]{2,1,0:T(8,128)(2,1)S(1)}, u32[]{:S(2)}, u32[]{:S(2)}) async-start(bf16[64,56,128]{2,1,0:T(8,128)(2,1)} %pack.1), calls=%async_computation | async-start | bytes 1835008 | tf_op jit(solution)/shard_map/all_to_all | solution.py:360
  25.2 25.0 %collective-permute-start = (bf16[3,512,128]{2,1,0:T(8,128)(2,1)}, bf16[3,512,128]{2,1,0:T(8,128)(2,1)S(1)}, u32[]{:S(2)}, u32[]{:S(2)}) collective-permute-start(bf16[3,512,128]{2,1,0:T(8,128)(2,1)} %get-tuple-element.10), channel_id=1, source_target_pairs={{0,16},{8,24},{16,0},{24,8},{1,17},{9,25},{17,1},{25,9},{2,18},{10... | collective-permute-start | bytes 1179656 | tf_op jit(solution)/shard_map/ppermute | solution.py:411
  30.1 21.1 %collective-permute-start.1 = (bf16[3,512,128]{2,1,0:T(8,128)(2,1)}, bf16[3,512,128]{2,1,0:T(8,128)(2,1)S(1)}, u32[]{:S(2)}, u32[]{:S(2)}) collective-permute-start(bf16[3,512,128]{2,1,0:T(8,128)(2,1)} %get-tuple-element.11), channel_id=1, source_target_pairs={{0,8},{8,16},{16,24},{24,0},{1,9},{9,17},{17,25},{25,1},{2,10},{10... | collective-permute-start | bytes 1179656 | tf_op jit(solution)/shard_map/ppermute | solution.py:411
  32.6 18.7 %collective-permute-start.2 = (bf16[3,512,128]{2,1,0:T(8,128)(2,1)}, bf16[3,512,128]{2,1,0:T(8,128)(2,1)S(1)}, u32[]{:S(2)}, u32[]{:S(2)}) collective-permute-start(bf16[3,512,128]{2,1,0:T(8,128)(2,1)} %get-tuple-element.12), channel_id=1, source_target_pairs={{0,24},{8,0},{16,8},{24,16},{1,25},{9,1},{17,9},{25,17},{2,26},{10... | collective-permute-start | bytes 1179656 | tf_op jit(solution)/shard_map/ppermute | solution.py:411
  37.2 1.0 copy-start.7
  40.8 19.5 %all-to-all-start.1 = ((bf16[8,16,640]{2,1,0:T(8,128)(2,1)}), bf16[8,16,640]{2,1,0:T(8,128)(2,1)S(1)}, u32[]{:S(2)}, u32[]{:S(2)}) async-start(bf16[8,16,640]{2,1,0:T(8,128)(2,1)} %bitcast.1), calls=%async_computation.1 | async-start | bytes 327680 | tf_op jit(solution)/shard_map/all_to_all | solution.py:417
  50.2 15.8 %copy-start = (bf16[3,512,128]{2,1,0:T(8,128)(2,1)}, bf16[3,512,128]{2,1,0:T(8,128)(2,1)S(1)}, u32[]{:S(2)}) copy-start(bf16[3,512,128]{2,1,0:T(8,128)(2,1)S(1)} %collective-permute-done.first.refs_0_) | copy-start | bytes 1179652
  51.3 14.8 %copy-start.2 = (bf16[3,512,128]{2,1,0:T(8,128)(2,1)}, bf16[3,512,128]{2,1,0:T(8,128)(2,1)S(1)}, u32[]{:S(2)}) copy-start(bf16[3,512,128]{2,1,0:T(8,128)(2,1)S(1)} %collective-permute-done.1.second.refs_1_) | copy-start | bytes 1179652
  51.3 14.8 %copy-start.4 = (bf16[3,512,128]{2,1,0:T(8,128)(2,1)}, bf16[3,512,128]{2,1,0:T(8,128)(2,1)S(1)}, u32[]{:S(2)}) copy-start(bf16[3,512,128]{2,1,0:T(8,128)(2,1)S(1)} %collective-permute-done.2.third.refs_2_) | copy-start | bytes 1179652
  61.3 21.2 %all-to-all-start.2 = ((bf16[32,16,384]{2,1,0:T(8,128)(2,1)}), bf16[32,16,384]{2,1,0:T(8,128)(2,1)}, u32[]{:S(2)}, u32[]{:S(2)}) async-start(bf16[32,16,384]{2,1,0:T(8,128)(2,1)} %merge.1), calls=%async_computation.2 | async-start | bytes 786432 | tf_op jit(solution)/shard_map/all_to_all | solution.py:425
  66.0 1.0 copy-start.1
  67.0 1.0 copy-start.3
  68.0 1.0 copy-start.5
  69.0 1.0 copy-start.6
